TPU v7x, 32 devices: a whole 2x2x4 slice. The times are simulated.
32 devices in a mesh: chan: 8 (over z, y), rows: 4 (over x, core).
Axes of the slice: x: 2, y: 2, z: 4, core: 2. Of those that a mesh axis runs over, the one named last changes fastest.
Arguments:
- activations: bfloat16 [1024, 8, 256], P('chan', 'rows'), may hold values from -6 to 6
- weights: bfloat16 [3, 3, 1024, 1024], P(None, None, 'chan'), may hold values from -0.0625 to 0.0625
- cotangent: bfloat16 [1024, 8, 256], P('chan', 'rows'), may hold values from -6 to 6
Outputs:
- output_map: bfloat16 [1024, 8, 256], P('chan', 'rows')
- input_grad: bfloat16 [1024, 8, 256], P('chan', 'rows')
- filter_grad: float32 [3, 3, 1024, 1024], P(None, None, ('chan', 'rows'))
All inputs are finite; a program needn't handle non-finite values.
Results may differ from a plain program's by a relative error of at most 0.001.
Values may be sent and summed in bfloat16 or wider, within the bound.
No kernel may reach another device: no remote copies, remote signals or barrier semaphores. Data moves between devices by JAX's collectives and lax.ppermute only.
A program may use at most 64 MiB of HBM per device.

v0:
```python
import math

import jax
import jax.numpy as jnp
from jax import lax
from jax.sharding import PartitionSpec as P


def padded_2(x, sides, width):
    for axis, dim in sides:
        size, length = (lax.axis_size(axis), x.shape[dim])
        up = [(i, (i + 1) % size) for i in range(size - 1)]
        down = [(j, i) for i, j in up]
        last = lax.slice_in_dim(x, length - width, length, axis=dim)
        first = lax.slice_in_dim(x, 0, width, axis=dim)
        before = lax.ppermute(last, axis, up)
        after = lax.ppermute(first, axis, down)
        x = jnp.concatenate([before, x, after], axis=dim)
    return x


def shift_columns(values, offset):
    if offset == 0:
        return values
    extent = values.shape[-1]
    widths = [(0, 0)] * (values.ndim - 1)
    if offset > 0:
        return jnp.pad(values[..., offset:], widths + [(0, offset)])
    return jnp.pad(values[..., : extent + offset], widths + [(-offset, 0)])


def forward_terms(weights, slab):
    number, padded_rows, width = slab.shape
    height = padded_rows - 2
    filters = weights.shape[2]
    parts = jnp.zeros((3, filters, height * width), jnp.float32)
    for tap_row in range(3):
        window = slab[:, tap_row : tap_row + height].reshape(number, height * width)
        parts = parts + jnp.einsum(
            "kon,np->kop", weights[tap_row], window, preferred_element_type=jnp.float32
        )
    total = jnp.zeros((filters, height, width), jnp.float32)
    for tap_col in range(3):
        total = total + shift_columns(parts[tap_col].reshape(filters, height, width), tap_col - 1)
    return total


def data_terms(chosen, gslab):
    number, padded_rows, width = gslab.shape
    height = padded_rows - 2
    outputs = chosen.shape[3]
    parts = jnp.zeros((3, outputs, height * width), jnp.float32)
    for tap_row in range(3):
        window = gslab[:, 2 - tap_row : 2 - tap_row + height].reshape(number, height * width)
        parts = parts + jnp.einsum(
            "koc,op->kcp", chosen[tap_row], window, preferred_element_type=jnp.float32
        )
    total = jnp.zeros((outputs, height, width), jnp.float32)
    for tap_col in range(3):
        total = total + shift_columns(parts[tap_col].reshape(outputs, height, width), 1 - tap_col)
    return total


def filter_terms(cotangent, slab):
    filters, height, width = cotangent.shape
    number = slab.shape[0]
    grid = []
    for tap_row in range(3):
        window = slab[:, tap_row : tap_row + height].reshape(number, height * width)
        line = []
        for tap_col in range(3):
            shifted = shift_columns(cotangent, 1 - tap_col).reshape(filters, height * width)
            line.append(
                lax.dot_general(
                    shifted, window, (((1,), (1,)), ((), ())), preferred_element_type=jnp.float32
                )
            )
        grid.append(jnp.stack(line))
    return jnp.stack(grid)


def per_device(activations, weights, cotangent):
    local_channels, height, width = activations.shape
    stacked = jnp.stack([activations, cotangent])
    padded = padded_2(stacked, (("rows", 2),), 1)
    xpadded = padded[0]
    gpadded = padded[1]
    gathered = lax.all_gather(xpadded, "chan", axis=0, tiled=True)
    output = forward_terms(weights, gathered)
    filter_sums = filter_terms(cotangent, gathered)
    grad_in = lax.psum_scatter(
        data_terms(weights, gpadded), "chan", scatter_dimension=0, tiled=True
    )
    cells = height * lax.axis_size("rows") * width
    filter_grad = lax.psum_scatter(filter_sums, "rows", scatter_dimension=2, tiled=True) * (
        1.0 / math.sqrt(cells)
    )
    return (output.astype(jnp.bfloat16), grad_in.astype(jnp.bfloat16), filter_grad)


def solution(mesh):
    placed = (P("chan", "rows", None), P(None, None, "chan", None), P("chan", "rows", None))
    return jax.shard_map(
        per_device,
        mesh=mesh,
        in_specs=placed,
        out_specs=(
            P("chan", "rows", None),
            P("chan", "rows", None),
            P(None, None, ("chan", "rows"), None),
        ),
        check_vma=False,
    )
```

profile of v0, /device:TPU:0, one launch (start us, length us, event | category | flops | bytes accessed | tf_op | source)
XLA Modules:
  0.0 223.2 jit_solution(1619187482368888429)
XLA Ops:
  7.2 0.0 copy-start.3
  7.2 0.0 all-gather.3.cloned.1.call-start
  7.2 1.0 copy_bitcast_fusion
  8.3 2.4 %collective-permute-start = (bf16[2,128,1,256]{3,1,2,0:T(8,128)(2,1)S(1)}, bf16[2,128,1,256]{3,1,2,0:T(8,128)(2,1)S(1)}, u32[]{:S(2)}, u32[]{:S(2)}) collective-permute-start(bf16[2,128,1,256]{3,1,2,0:T(8,128)(2,1)S(1)} %get-tuple-element.17), channel_id=1, source_target_pairs={{0,1},{1,2},{2,3},{4,5},{5,6},{6,7},{8,9},{9,10},{10,11},{12,13},{... | collective-permute-start | bytes 393224 | tf_op jit(solution)/shard_map/ppermute | solution.py:16
  10.7 1.3 collective-permute-start.1
  12.0 0.0 collective-permute-done
  12.0 4.0 %collective-permute-done.1 = bf16[2,128,1,256]{3,1,2,0:T(8,128)(2,1)S(1)} collective-permute-done((bf16[2,128,1,256]{3,1,2,0:T(8,128)(2,1)S(1)}, bf16[2,128,1,256]{3,1,2,0:T(8,128)(2,1)S(1)}, u32[]{:S(2)}, u32[]{:S(2)}) %collective-permute-start.1) | collective-permute-done | bytes 131104 | tf_op jit(solution)/shard_map/ppermute | solution.py:17
  16.0 0.1 pad_maximum_fusion.1
  16.1 0.7 slice_bitcast_fusion
  16.8 0.0 all-gather.3.cloned.1.call-update
  16.8 0.0 reduce-scatter.2.cloned.1.call-start
  16.9 0.0 copy-done.3
  16.9 0.2 fusion.45
  17.2 52.6 %all-gather.3.cloned.1.call-done = bf16[1,1024,4,256]{3,1,2,0:T(8,128)(2,1)} async-done(((bf16[1,128,4,256]{3,1,2,0:T(8,128)(2,1)}), bf16[1,1024,4,256]{3,1,2,0:T(8,128)(2,1)}) %all-gather.3.cloned.1.call-update) | async-done | bytes 2097168 | tf_op jit(solution)/shard_map/all_gather | solution.py:88
  69.8 0.0 copy-start
  69.8 1.8 convolution_bitcast_fusion.7
  71.6 1.7 convolution_bitcast_fusion.5
  73.3 0.0 copy-done
  73.3 0.5 convolution_bitcast_fusion.8
  73.8 0.5 convolution_bitcast_fusion.6
  74.3 0.5 convolution_bitcast_fusion.3
  74.8 0.5 convolution_bitcast_fusion.4
  75.3 0.5 convolution_bitcast_fusion.2
  75.7 0.1 maximum_bitcast_fusion
  75.9 0.5 convolution_bitcast_fusion.1
  76.3 0.1 maximum_bitcast_fusion.1
  76.4 0.5 convolution_bitcast_fusion
  76.9 0.1 maximum_bitcast_fusion.2
  77.0 2.9 %pad_maximum_fusion = f32[3,3,128,1024]{3,2,1,0:T(8,128)} fusion(f32[1,3,128,1024]{3,2,1,0:T(8,128)S(1)} %maximum_bitcast_fusion.2, f32[1,3,128,1024]{3,2,1,0:T(8,128)S(1)} %maximum_bitcast_fusion.1, f32[1,3,128,1024]{3,2,1,0:T(8,128)S(1)} %maximum_bitcast_fusion), kind=kLoop, calls=%fused_computation.1 | loop fusion | flops 2359296 | bytes 9437184 | tf_op jit(solution)/shard_map/stack | solution.py:79
  79.9 0.0 reduce-scatter.2.cloned.1.call-update
  79.9 0.6 copy-done.5
  80.5 0.6 dynamic-slice
  81.8 0.1 copy.37
  81.9 0.1 copy.36
  82.1 0.1 copy.38
  82.2 0.0 copy-start.1
  82.2 2.2 %fusion.3 = f32[512,3,1024]{2,0,1:T(8,128)S(1)} fusion(bf16[128,512,1]{0,1,2:T(8,128)(2,1)S(1)} %bitcast.123, bf16[3,3,128,1024]{3,2,1,0:T(8,128)(2,1)} %param.4), kind=kOutput, calls=%fused_computation.20 | convolution fusion | flops 402653184 | bytes 7208960 | tf_op jit(solution)/shard_map/koc,op->kcp/dot_general | solution.py:55
  84.5 0.0 copy-done.1
  84.5 1.0 fusion.6
  85.4 1.0 add_bitcast_fusion
  86.5 2.6 %fusion.41 = (f32[1,1024,512]{1,2,0:T(8,128)S(1)}, f32[1,1024,512]{1,2,0:T(8,128)}, f32[1,1024,512]{1,2,0:T(8,128)}) fusion(f32[3,1024,512]{1,2,0:T(8,128)S(1)} %add_bitcast_fusion), kind=kLoop, calls=%fused_computation.68 | loop fusion | bytes 12582912 | tf_op jit(solution)/shard_map/slice | solution.py:60
  89.1 1.6 slice.126
  90.7 4.1 %copy.58 = f32[1024,2,255]{2,1,0:T(2,128)} copy(f32[1024,2,255]{0,2,1:T(8,128)} %slice.126) | data formatting | bytes 4177920
  94.9 4.3 %copy.40 = f32[1024,2,256]{2,1,0:T(2,128)} copy(f32[1024,2,256]{0,2,1:T(8,128)} %bitcast.115) | data formatting | bytes 4194304 | tf_op jit(solution)/shard_map/reshape;squeeze | solution.py:60
  99.2 4.1 %copy.59 = f32[1024,2,255]{2,1,0:T(2,128)} copy(f32[1024,2,255]{0,2,1:T(8,128)} %bitcast.114) | data formatting | bytes 4177920
  103.3 5.2 %pad_add_fusion = f32[1024,2,256]{2,1,0:T(2,128)} fusion(f32[1024,2,255]{2,1,0:T(2,128)} %copy.59, f32[1024,2,256]{2,1,0:T(2,128)} %copy.40, f32[1024,2,255]{2,1,0:T(2,128)} %copy.58), kind=kLoop, calls=%fused_computation.2 | loop fusion | flops 1048576 | bytes 8372224 | tf_op jit(solution)/shard_map/add | solution.py:60
  108.5 92.3 %all-reduce.8 = bf16[1024,2,256]{2,1,0:T(2,128)(2,1)S(1)} all-reduce(f32[1024,2,256]{2,1,0:T(2,128)} %pad_add_fusion), channel_id=3, replica_groups=mesh['chan'=8,'rows'=4] {'chan'}, use_global_device_ids=true, to_apply=%region_0.1.clone | all-reduce | flops 524288 | bytes 3145728
  200.9 0.8 dynamic-slice_convert_fusion
  201.6 1.5 fusion.42
  203.1 1.3 copy.30
  204.5 1.6 copy.31
  206.1 2.3 %copy.32 = bf16[1024,2,256]{0,2,1:T(8,128)(2,1)} copy(bf16[1024,2,256]{2,0,1:T(8,128)(2,1)} %get-tuple-element.6) | data formatting | bytes 2097152 | tf_op jit(solution)/shard_map/slice | solution.py:38
  208.4 0.0 copy-done.2
  208.4 1.9 fusion.8
  210.4 0.0 copy-start.4
  210.4 0.7 convolution_add_fusion.1
  211.1 0.5 copy-done.4
  211.6 0.7 fusion
  212.3 0.1 fusion.43
  212.4 0.1 copy.57
  212.6 0.1 copy.34
  212.7 0.1 copy.56
  212.9 1.0 add_convert_fusion
  213.9 2.5 %broadcast_multiply_fusion = f32[3,3,32,1024]{3,2,1,0:T(8,128)} fusion(f32[3,3,32,1024]{3,2,1,0:T(8,128)} %reduce-scatter.2.cloned.1.call-done), kind=kLoop, calls=%fused_computation.33 | loop fusion | flops 294912 | bytes 2359296 | tf_op jit(solution)/shard_map/mul | solution.py:95
  (8 shorter events, 0.1 us)
Async XLA Ops:
  7.2 9.7 %copy-start.3 = (bf16[128,2,256]{2,1,0:T(2,128)(2,1)S(1)}, bf16[128,2,256]{2,1,0:T(2,128)(2,1)}, u32[]{:S(2)}) copy-start(bf16[128,2,256]{2,1,0:T(2,128)(2,1)} %param.5) | copy-start | bytes 393220
  7.2 62.6 %all-gather.3.cloned.1.call-start = ((), (), s32[]{:S(2)}) async-start(), calls=%async_computation.2 | async-start | bytes 2359296 | tf_op jit(solution)/shard_map/all_gather | solution.py:88
  8.3 3.7 %collective-permute-start = (bf16[2,128,1,256]{3,1,2,0:T(8,128)(2,1)S(1)}, bf16[2,128,1,256]{3,1,2,0:T(8,128)(2,1)S(1)}, u32[]{:S(2)}, u32[]{:S(2)}) collective-permute-start(bf16[2,128,1,256]{3,1,2,0:T(8,128)(2,1)S(1)} %get-tuple-element.17), channel_id=1, source_target_pairs={{0,1},{1,2},{2,3},{4,5},{5,6},{6,7},{8,9},{9,10},{10,11},{12,13},{... | collective-permute-start | bytes 393224 | tf_op jit(solution)/shard_map/ppermute | solution.py:16
  10.7 5.3 %collective-permute-start.1 = (bf16[2,128,1,256]{3,1,2,0:T(8,128)(2,1)S(1)}, bf16[2,128,1,256]{3,1,2,0:T(8,128)(2,1)S(1)}, u32[]{:S(2)}, u32[]{:S(2)}) collective-permute-start(bf16[2,128,1,256]{3,1,2,0:T(8,128)(2,1)S(1)} %get-tuple-element.18), channel_id=1, source_target_pairs={{1,0},{2,1},{3,2},{5,4},{6,5},{7,6},{9,8},{10,9},{11,10},{13,12},{... | collective-permute-start | bytes 393224 | tf_op jit(solution)/shard_map/ppermute | solution.py:17
  16.8 197.1 %reduce-scatter.2.cloned.1.call-start = ((), (), s32[]{:S(2)}) async-start(), calls=%async_computation.1 | async-start | bytes 5898240 | tf_op jit(solution)/shard_map/reduce_scatter | solution.py:95
  69.8 3.6 %copy-start = (bf16[1,1024,4,256]{3,1,2,0:T(8,128)(2,1)S(1)}, bf16[1,1024,4,256]{3,1,2,0:T(8,128)(2,1)}, u32[]{:S(2)}) copy-start(bf16[1,1024,4,256]{3,1,2,0:T(8,128)(2,1)} %all-gather.3.cloned.1.call-done) | copy-start | bytes 6291460
  79.9 0.7 copy-start.5
  82.2 2.3 %copy-start.1 = (bf16[3,3,128,1024]{3,2,1,0:T(8,128)(2,1)S(1)}, bf16[3,3,128,1024]{3,2,1,0:T(8,128)(2,1)}, u32[]{:S(2)}) copy-start(bf16[3,3,128,1024]{3,2,1,0:T(8,128)(2,1)} %param.4) | copy-start | bytes 7077892
  204.5 3.9 %copy-start.2 = (bf16[3,3,128,1024]{3,2,1,0:T(8,128)(2,1)S(1)}, bf16[3,3,128,1024]{3,2,1,0:T(8,128)(2,1)}, u32[]{:S(2)}) copy-start(bf16[3,3,128,1024]{3,2,1,0:T(8,128)(2,1)} %param.4) | copy-start | bytes 7077892
  210.4 1.2 copy-start.4
Sparse Core Ops, SparseCore 0:
  17.0 52.7 all-gather.2
  80.0 46.2 reduce-scatter.1
where the time goes:
time: 224 us; the launch traced here: 223 us
  blocking collectives  92.3 us (41%)
  waiting for transfers between devices  56.6 us (25%)
  local copies, waits for them, and re-layouts  29.1 us (13%)
  between operations  15 us (7%)
  matrix products  14.5 us (6%)
  other arithmetic  11.9 us (5%)
  starting transfers between devices  3.74 us (2%)
    unnamed x1, blocking collectives  92.3 us
    all_gather x1, waiting for transfers between devices, per_device(): gathered = lax.all_gather(xpadded, 'chan', axis=0, tiled=True)  52.6 us
    unnamed x19, local copies, waits for them, and re-layouts  10.3 us
    dot_general x9, matrix products, filter_terms(): lax.dot_general(shifted, window, (((1,), (1,)), ((), ())), preferred_elem...  6.85 us
    slice x4, local copies, waits for them, and re-layouts, forward_terms(): window = slab[:, tap_row:tap_row + height].reshape(number, height * width)  6.78 us
    add x1, other arithmetic, data_terms(): total + shift_columns(parts[tap_col].reshape(outputs, height, width), 1 -...  5.2 us
  transfers between devices with their start and end apart: 4, of which 2 were waited for; matrix products, arithmetic and copies ran while one was open for 18% of the time, Pallas kernels for 0%

commit v1 on v0

v1 whole, which is shorter than its diff:
```python
import math

import jax
import jax.numpy as jnp
from jax import lax
from jax.sharding import PartitionSpec as P

BF16, F32 = jnp.bfloat16, jnp.float32
SPAN = 124.0
LEAST = 2.0**-100


def exchange(x, axis, distance):
    size = lax.axis_size(axis)
    return lax.ppermute(x, axis, [(i, i ^ distance) for i in range(size)])


def shift_columns(values, offset):
    if offset == 0:
        return values
    extent = values.shape[-1]
    widths = [(0, 0)] * (values.ndim - 1)
    if offset > 0:
        return jnp.pad(values[..., offset:], widths + [(0, offset)])
    return jnp.pad(values[..., : extent + offset], widths + [(-offset, 0)])


def encode(values):
    top = jnp.maximum(jnp.max(jnp.abs(values), axis=0, keepdims=True) * 1.01, LEAST)
    top = lax.reduce_precision(top, 8, 7)
    factor = (2 * SPAN) / top
    code = jnp.exp2(jnp.abs(values) * factor - SPAN)
    code = jnp.where(values < 0, -code, code).astype(BF16)
    return jnp.concatenate([code, jnp.broadcast_to(top.astype(BF16), (16, top.shape[1]))], axis=0)


def decode(coded):
    number = coded.shape[0] - 16
    step = coded[number : number + 1].astype(F32) * (0.5 / SPAN)
    code = coded[:number].astype(F32)
    size = (jnp.log2(jnp.abs(code)) + SPAN) * step
    return jnp.where(code < 0, -size, size)


def gathered(x):
    size, me = lax.axis_size("chan"), lax.axis_index("chan")
    blocks = jnp.stack([x] + [exchange(x, "chan", k) for k in range(1, size)])
    bit = 1
    while bit < size:
        pairs = blocks.reshape((-1, 2, bit) + x.shape)
        swapped = jnp.stack([pairs[:, 1], pairs[:, 0]], axis=1)
        blocks = jnp.where((me // bit) % 2 == 1, swapped, pairs).reshape(blocks.shape)
        bit *= 2
    return blocks.reshape((size * x.shape[0],) + x.shape[1:])


def per_device(activations, weights, cotangent):
    local, height, width = activations.shape
    chans, rows = lax.axis_size("chan"), lax.axis_size("rows")
    chips, zs = rows // 2, chans // 2
    me, row = lax.axis_index("chan"), lax.axis_index("rows")
    core, chip = row % 2, row // 2
    own_y, own_z = me % 2, me // 2
    first = core == 0
    share = local // rows
    channels = weights.shape[3]
    cells = height * rows * width
    taps = weights.reshape(9, local, channels)

    edges = [(i, i + 1) for i in range(1, rows - 1, 2)]
    edge = jnp.where(first, cotangent[:, 0], cotangent[:, height - 1])
    halo = lax.ppermute(edge, "rows", edges + [(j, i) for i, j in edges])
    mine = jnp.concatenate([cotangent, halo[:, None]], axis=1)
    other = exchange(mine, "rows", 1)
    low, high = jnp.where(first, mine, other), jnp.where(first, other, mine)
    slab = jnp.concatenate([low[:, height:], low[:, :height], high], axis=1)

    xs = gathered(activations.reshape(local, height * width))
    xo = exchange(xs, "rows", 1)
    xchip = jnp.concatenate([jnp.where(first, xs, xo), jnp.where(first, xo, xs)], axis=1)

    window = jnp.where(first, slab[:, : height + 2], slab[:, height:])
    shifted = [shift_columns(window, 1 - b) for b in range(3)]
    stack = jnp.concatenate(
        [shifted[b][:, 2 - a : 2 - a + height].reshape(local, -1) for a in range(3) for b in range(3)], axis=0
    )
    partial = lax.dot_general(
        stack, taps.reshape(9 * local, channels), (((0,), (0,)), ((), ())), preferred_element_type=F32
    )
    pairs = partial.reshape(height * width, zs, 2, local)
    keep = jnp.where(own_y == 0, pairs[:, :, 0], pairs[:, :, 1]).reshape(height * width, zs * local)
    give = jnp.where(own_y == 0, pairs[:, :, 1], pairs[:, :, 0]).reshape(height * width, zs * local)
    total = keep + decode(exchange(encode(give), "chan", 1))
    coded = encode(total)
    grad = lax.dynamic_slice_in_dim(total, own_z * local, local, axis=1)
    for k in range(1, zs):
        piece = lax.dynamic_slice_in_dim(coded, (own_z ^ k) * local, local, axis=1)
        grad = grad + decode(exchange(piece, "chan", 2 * k))
    input_grad = grad.T.reshape(local, height, width).astype(BF16)

    def half(x, axis):
        shape = x.shape[:axis] + (chips, 2, share) + x.shape[axis + 1 :]
        x = x.reshape(shape)
        return jnp.where(first, lax.index_in_dim(x, 0, axis + 1, False), lax.index_in_dim(x, 1, axis + 1, False))

    gs = half(slab, 0)
    moved = [shift_columns(gs, 1 - b) for b in range(3)]
    lines = jnp.stack(
        [moved[b][:, :, 2 - a : 2 - a + 2 * height].reshape(chips, share, -1) for a in range(3) for b in range(3)],
        axis=1,
    )
    sums = lax.dot_general(
        lines.reshape(chips * 9 * share, -1), xchip, (((1,), (1,)), ((), ())), preferred_element_type=F32
    ).reshape(chips, 9 * share, channels)
    filter_sum = lax.dynamic_index_in_dim(sums, chip, 0, False)
    for k in range(1, chips):
        piece = encode(lax.dynamic_index_in_dim(sums, chip ^ k, 0, False))
        filter_sum = filter_sum + decode(exchange(piece, "rows", 2 * k))
    filter_grad = (filter_sum * (1.0 / math.sqrt(cells))).reshape(3, 3, share, channels)

    wh = half(taps, 1).reshape(9 * chips * share, channels)
    parts = lax.dot_general(wh, xchip, (((1,), (0,)), ((), ())), preferred_element_type=F32)
    parts = parts.reshape(3, 3, chips * share, 2 * height, width)
    line = sum(shift_columns(
        sum(jnp.pad(parts[a, b], ((0, 0), (2 - a, a), (0, 0))) for a in range(3)), b - 1) for b in range(3))
    up = [(i, i + 2) for i in range(rows - 2)]
    above = lax.ppermute(line[:, -1], "rows", up)
    below = lax.ppermute(line[:, 0], "rows", [(j, i) for i, j in up])
    inner = line[:, 1:-1]
    inner = inner.at[:, 0].add(above).at[:, -1].add(below).astype(BF16)
    stay = jnp.where(first, inner[:, :height], inner[:, height:])
    go = jnp.where(first, inner[:, height:], inner[:, :height])
    come = exchange(go, "rows", 1)
    stay, come = (x.reshape(chips, share, height, width) for x in (stay, come))
    output = jnp.stack([jnp.where(first, stay, come), jnp.where(first, come, stay)], axis=1)
    return output.reshape(local, height, width), input_grad, filter_grad


def solution(mesh):
    placed = (P("chan", "rows", None), P(None, None, "chan", None), P("chan", "rows", None))
    return jax.shard_map(
        per_device,
        mesh=mesh,
        in_specs=placed,
        out_specs=(
            P("chan", "rows", None),
            P("chan", "rows", None),
            P(None, None, ("chan", "rows"), None),
        ),
        check_vma=False,
    )
```

time: 224 us -> 132 us (0.59)
  blocking collectives: 92.3 us -> 0 us
  starting transfers between devices: 3.74 us -> 26.9 us
  waiting for transfers between devices: 56.6 us -> 34.9 us
  between operations: 15 us -> 1.5 us
  other arithmetic: 11.9 us -> 23.5 us
  matrix products: 14.5 us -> 5.96 us
  local copies, waits for them, and re-layouts: 29.1 us -> 37.5 us
    unnamed x1 -> x0, blocking collectives: 92.3 us -> none
    all_gather x1 -> x0, waiting for transfers between devices: 52.6 us -> none  [per_device(): gathered = lax.all_gather(xpadded, 'chan', axis=0, tiled=True)]
    ppermute x2 -> x18, waiting for transfers between devices: 4.03 us -> 34.9 us  [the longest x15 28.3 us: exchange(): return lax.ppermute(x, axis, [(i, i ^ distance) for i in range(size)])]
    ppermute x2 -> x18, starting transfers between devices: 3.66 us -> 26.9 us  [the longest x15 19.8 us: exchange(): return lax.ppermute(x, axis, [(i, i ^ distance) for i in range(size)])]
    dot_general x15 -> x3, matrix products: 14.5 us -> 5.96 us  [the longest x1 3.02 us: per_device(): lax.dot_general(lines.reshape(chips * 9 * share, -1), xchip, (((1,), (1,)...]
    select_n x0 -> x11, other arithmetic: none -> 8.1 us  [the longest x2 2.96 us: half(): jnp.where(first, lax.index_in_dim(x, 0, axis + 1, False), lax.index_in_di...]
    slice x13, local copies, waits for them, and re-layouts: 11.8 us -> 4.56 us  [the longest x2 1.22 us: per_device(): shifted[b][:, 2 - a:2 - a + height].reshape(local, -1)]
    unnamed x19 -> x71, local copies, waits for them, and re-layouts: 10.3 us -> 15.4 us
  transfers between devices with their start and end apart: 4 -> 18, of which waited for: 2 -> 6; matrix products, arithmetic and copies ran while one was open for 18% -> 37% of each run, Pallas kernels for 0% -> 0%
where the time goes in v1:
time: 132 us; the launch traced here: 130 us
  local copies, waits for them, and re-layouts  37.5 us (28%)
  waiting for transfers between devices  34.9 us (26%)
  starting transfers between devices  26.9 us (20%)
  other arithmetic  23.5 us (18%)
  matrix products  5.96 us (5%)
  between operations  1.5 us (1%)
    ppermute x15, waiting for transfers between devices, exchange(): return lax.ppermute(x, axis, [(i, i ^ distance) for i in range(size)])  28.3 us
    ppermute x15, starting transfers between devices, exchange(): return lax.ppermute(x, axis, [(i, i ^ distance) for i in range(size)])  19.8 us
    unnamed x71, local copies, waits for them, and re-layouts  15.4 us
    another operation x10, local copies, waits for them, and re-layouts, per_device(): jnp.stack([moved[b][:, :, 2 - a:2 - a + 2 * height].reshape(chips, share,...  6.78 us
    ppermute x1, waiting for transfers between devices, per_device(): above = lax.ppermute(line[:, -1], 'rows', up)  5.03 us
    ppermute x1, starting transfers between devices, per_device(): above = lax.ppermute(line[:, -1], 'rows', up)  4.55 us
    reduce_max x3, other arithmetic, encode(): jnp.max(jnp.abs(values), axis=0, keepdims=True) * 1.01  4.02 us
    dot_general x1, matrix products, per_device(): lax.dot_general(lines.reshape(chips * 9 * share, -1), xchip, (((1,), (1,)...  3.02 us
  transfers between devices with their start and end apart: 18, of which 6 were waited for; matrix products, arithmetic and copies ran while one was open for 37% of the time, Pallas kernels for 0%

profile of v1, /device:TPU:0, one launch (start us, length us, event | category | flops | bytes accessed | tf_op | source)
XLA Modules:
  0.0 130.3 jit_solution(15089841343723297458)
XLA Ops:
  0.6 1.6 %copy.30 = bf16[16,8,2,256]{3,1,2,0:T(8,128)(2,1)} copy(bf16[16,8,2,256]{3,2,1,0:T(2,128)(2,1)} %bitcast.174) | data formatting | bytes 262144
  2.3 6.0 %collective-permute-start.6 = (bf16[128,512]{1,0:T(8,128)(2,1)}, bf16[128,512]{1,0:T(8,128)(2,1)}, u32[]{:S(2)}, u32[]{:S(2)}) collective-permute-start(bf16[128,512]{1,0:T(8,128)(2,1)} %bitcast.77), channel_id=1, source_target_pairs={{0,28},{4,24},{8,20},{12,16},{16,12},{20,8},{24,4},{28,0},{1,29},{... | collective-permute-start | bytes 393224 | tf_op jit(solution)/shard_map/ppermute | solution.py:15
  8.5 0.7 collective-permute-start.4
  9.2 1.5 %collective-permute-start = (bf16[128,512]{1,0:T(8,128)(2,1)}, bf16[128,512]{1,0:T(8,128)(2,1)}, u32[]{:S(2)}, u32[]{:S(2)}) collective-permute-start(bf16[128,512]{1,0:T(8,128)(2,1)} %bitcast.77), channel_id=1, source_target_pairs={{0,4},{4,0},{8,12},{12,8},{16,20},{20,16},{24,28},{28,24},{1,5},{5... | collective-permute-start | bytes 393224 | tf_op jit(solution)/shard_map/ppermute | solution.py:15
  10.8 1.2 fusion.74
  12.0 0.6 fusion.48
  12.6 1.3 collective-permute-start.11
  14.0 2.9 %slice_select_fusion = bf16[9,2,1,32,1024]{4,3,2,1,0:T(8,128)(2,1)} fusion(bf16[9,2,2,32,1024]{4,3,2,1,0:T(8,128)(2,1)} %bitcast.155, pred[]{:T(512)S(6)} %eq.22), kind=kLoop, calls=%fused_computation.20 | loop fusion | flops 589824 | bytes 3538945 | tf_op jit(solution)/shard_map/jit(_where)/select_n | solution.py:104
  17.1 2.5 %copy.19 = bf16[1024,1152]{1,0:T(8,128)(2,1)} copy(bf16[1024,1152]{0,1:T(8,128)(2,1)S(1)} %bitcast.156) | data formatting | bytes 4718592 | tf_op jit(solution)/shard_map/dot_general | solution.py:87
  19.6 2.1 %collective-permute-start.3 = (bf16[128,512]{1,0:T(8,128)(2,1)}, bf16[128,512]{1,0:T(8,128)(2,1)S(1)}, u32[]{:S(2)}, u32[]{:S(2)}) collective-permute-start(bf16[128,512]{1,0:T(8,128)(2,1)} %bitcast.77), channel_id=1, source_target_pairs={{0,16},{4,20},{8,24},{12,28},{16,0},{20,4},{24,8},{28,12},{1,17},{... | collective-permute-start | bytes 393224 | tf_op jit(solution)/shard_map/ppermute | solution.py:15
  21.7 0.9 copy.18
  23.0 1.3 %collective-permute-start.1 = (bf16[128,512]{1,0:T(8,128)(2,1)}, bf16[128,512]{1,0:T(8,128)(2,1)S(1)}, u32[]{:S(2)}, u32[]{:S(2)}) collective-permute-start(bf16[128,512]{1,0:T(8,128)(2,1)} %bitcast.77), channel_id=1, source_target_pairs={{0,8},{4,12},{8,0},{12,4},{16,24},{20,28},{24,16},{28,20},{1,9},{5... | collective-permute-start | bytes 393224 | tf_op jit(solution)/shard_map/ppermute | solution.py:15
  24.3 0.9 bitcast_dynamic-update-slice_fusion.6
  25.2 4.7 %collective-permute-done.1 = bf16[128,512]{1,0:T(8,128)(2,1)S(1)} collective-permute-done((bf16[128,512]{1,0:T(8,128)(2,1)}, bf16[128,512]{1,0:T(8,128)(2,1)S(1)}, u32[]{:S(2)}, u32[]{:S(2)}) %collective-permute-start.1) | collective-permute-done | bytes 131104 | tf_op jit(solution)/shard_map/ppermute | solution.py:15
  29.9 7.3 %collective-permute-done.2 = bf16[128,512]{1,0:T(8,128)(2,1)S(1)} collective-permute-done((bf16[128,512]{1,0:T(8,128)(2,1)}, bf16[128,512]{1,0:T(8,128)(2,1)S(1)}, u32[]{:S(2)}, u32[]{:S(2)}) %collective-permute-start.2) | collective-permute-done | bytes 131104 | tf_op jit(solution)/shard_map/ppermute | solution.py:15
  37.2 0.9 bitcast_dynamic-update-slice_fusion.2
  38.2 0.9 bitcast_dynamic-update-slice_fusion.1
  39.1 0.9 bitcast_dynamic-update-slice_fusion
  44.3 0.9 pad_slice_fusion.6
  45.6 1.5 %copy-done.3 = bf16[1024,1152]{1,0:T(8,128)(2,1)S(1)} copy-done((bf16[1024,1152]{1,0:T(8,128)(2,1)S(1)}, bf16[1024,1152]{1,0:T(8,128)(2,1)}, u32[]{:S(2)}) %copy-start.3) | copy-done | bytes 2359320
  47.1 1.5 %fusion.10 = f32[512,4,2,128]{0,3,2,1:T(8,128)S(1)} fusion(bf16[4,2,128,1152]{3,2,1,0:T(8,128)(2,1)S(1)} %bitcast.161, bf16[1152,512]{1,0:T(8,128)(2,1)S(1)} %constant_dynamic-update-slice_fusion.1), kind=kOutput, calls=%fused_computation.21 | convolution fusion | flops 1207959552 | bytes 5636096 | tf_op jit(solution)/shard_map/dot_general | solution.py:87
  48.9 1.1 fusion.65
  50.0 0.7 stack_reshape.38
  50.7 0.7 stack_reshape.35
  51.5 0.7 stack_reshape.32
  52.2 1.1 pad_slice_fusion
  53.3 1.6 %stack_reshape.36 = bf16[2,1,32,1024]{3,2,1,0:T(8,128)(2,1)} reshape(bf16[2,32,4,256]{3,2,1,0:T(4,128)(2,1)} %get-tuple-element.59) | data formatting | bytes 262144 | tf_op jit(solution)/shard_map/stack;reshape | solution.py:108
  54.9 0.7 stack_reshape.33
  55.7 0.7 stack_reshape.34
  56.4 0.7 stack_reshape.37
  57.1 0.7 constant_dynamic-update-slice_fusion.18
  58.9 0.9 pad_maximum_fusion.6
  60.7 0.7 constant_dynamic-update-slice_fusion.17
  61.4 1.6 %constant_dynamic-update-slice_fusion.16 = bf16[2,9,32,1024]{3,2,1,0:T(8,128)(2,1)} fusion(bf16[2,9,32,1024]{3,2,1,0:T(8,128)(2,1)} %constant_dynamic-update-slice_fusion.17, bf16[2,1,32,1024]{3,2,1,0:T(8,128)(2,1)} %stack_reshape.33), kind=kLoop, calls=%fused_computation.156 | loop fusion | bytes 262144
  63.0 1.6 %constant_dynamic-update-slice_fusion.15 = bf16[2,9,32,1024]{3,2,1,0:T(8,128)(2,1)} fusion(bf16[2,9,32,1024]{3,2,1,0:T(8,128)(2,1)} %constant_dynamic-update-slice_fusion.16, bf16[2,1,32,1024]{3,2,1,0:T(8,128)(2,1)} %stack_reshape.34), kind=kLoop, calls=%fused_computation.155 | loop fusion | bytes 262144
  64.5 0.7 constant_dynamic-update-slice_fusion.14
  65.2 1.6 %constant_dynamic-update-slice_fusion.13 = bf16[2,9,32,1024]{3,2,1,0:T(8,128)(2,1)} fusion(bf16[2,9,32,1024]{3,2,1,0:T(8,128)(2,1)} %constant_dynamic-update-slice_fusion.14, bf16[2,1,32,1024]{3,2,1,0:T(8,128)(2,1)} %stack_reshape.36), kind=kLoop, calls=%fused_computation.153 | loop fusion | bytes 262144
  66.8 0.7 constant_dynamic-update-slice_fusion.12
  67.4 6.8 %collective-permute-done.13 = bf16[528,512]{1,0:T(8,128)(2,1)} collective-permute-done((bf16[528,512]{1,0:T(8,128)(2,1)}, bf16[528,512]{1,0:T(8,128)(2,1)}, u32[]{:S(2)}, u32[]{:S(2)}) %collective-permute-start.13) | collective-permute-done | bytes 540704 | tf_op jit(solution)/shard_map/ppermute | solution.py:15
  74.3 0.7 fusion.52
  75.0 1.5 %abs_reduce_fusion.1 = (f32[512]{0:T(512)S(1)}, f32[512,512]{1,0:T(8,128)S(1)}) fusion(f32[512,512]{1,0:T(8,128)S(1)} %copy.22, f32[512]{0:T(512)S(1)} %bitcast.193, bf16[528,512]{1,0:T(8,128)(2,1)} %collective-permute-done.13), kind=kLoop, calls=%fused_computation.47 | loop fusion | flops 2883072 | bytes 2625536 | tf_op jit(solution)/shard_map/reduce_max | solution.py:29
  77.4 0.7 constant_dynamic-update-slice_fusion.11
  78.1 0.7 constant_dynamic-update-slice_fusion.10
  78.7 5.6 %collective-permute-start.15 = (bf16[528,128]{1,0:T(8,128)(2,1)S(1)}, bf16[528,128]{1,0:T(8,128)(2,1)S(1)}, u32[]{:S(2)}, u32[]{:S(2)}) collective-permute-start(bf16[528,128]{1,0:T(8,128)(2,1)S(1)} %get-tuple-element.54), channel_id=1, source_target_pairs={{0,16},{4,20},{8,24},{12,28},{16,0},{20,4},{24,8},{28,12},{1,17},{... | collective-permute-start | bytes 405512 | tf_op jit(solution)/shard_map/ppermute | solution.py:15
  84.4 9.4 %collective-permute-done.15 = bf16[528,128]{1,0:T(8,128)(2,1)S(1)} collective-permute-done((bf16[528,128]{1,0:T(8,128)(2,1)S(1)}, bf16[528,128]{1,0:T(8,128)(2,1)S(1)}, u32[]{:S(2)}, u32[]{:S(2)}) %collective-permute-start.15) | collective-permute-done | bytes 135200 | tf_op jit(solution)/shard_map/ppermute | solution.py:15
  93.9 1.4 %broadcast_select_fusion.2 = (bf16[1024,512]{1,0:T(8,128)(2,1)S(1)}, bf16[1024,512]{1,0:T(8,128)(2,1)S(1)}) fusion(bf16[1024,512]{1,0:T(8,128)(2,1)S(1)} %fusion.23, bf16[1024,512]{1,0:T(8,128)(2,1)} %collective-permute-done.7, pred[]{:T(512)S(6)} %eq.22), kind=kLoop, calls=%fused_computation.44 | loop fusion | flops 1048576 | bytes 4194305 | tf_op jit(solution)/shard_map/jit(_where)/select_n | solution.py:80
  95.6 1.0 copy-done.18
  96.6 3.0 %fusion = f32[2,288,1024]{2,1,0:T(8,128)} fusion(bf16[2,288,1024]{2,1,0:T(8,128)(2,1)S(1)} %bitcast.192, bf16[1024,512]{1,0:T(8,128)(2,1)S(1)} %get-tuple-element.42, bf16[1024,512]{1,0:T(8,128)(2,1)S(1)} %get-tuple-element.41), kind=kOutput, calls=%fused_computation.1 | convolution fusion | flops 1212153856 | bytes 5636096 | tf_op jit(solution)/shard_map/dot_general | solution.py:112
  99.6 2.6 %copy.14 = bf16[1024,1024]{1,0:T(8,128)(2,1)} copy(bf16[1024,1024]{0,1:T(8,128)(2,1)S(1)} %fusion.2) | data formatting | bytes 4194304 | tf_op jit(solution)/shard_map/dot_general | solution.py:122
  102.2 1.4 %abs_reduce_fusion = f32[1024]{0:T(1024)S(1)} fusion(f32[2,288,1024]{2,1,0:T(8,128)} %fusion, s32[]{:T(128)S(6)} %select_n.327), kind=kLoop, calls=%fused_computation.27 | loop fusion | flops 588800 | bytes 1183748 | tf_op jit(solution)/shard_map/reduce_max | solution.py:29
  103.6 1.8 %fusion.7 = bf16[288,1024]{1,0:T(8,128)(2,1)S(1)} fusion(f32[2,288,1024]{2,1,0:T(8,128)} %fusion, s32[]{:T(128)S(6)} %select_n.327, f32[1024]{0:T(1024)S(1)} %get-tuple-element.84), kind=kLoop, calls=%fused_computation.17 | loop fusion | flops 2359296 | bytes 1773572 | tf_op jit(solution)/shard_map/convert_element_type | solution.py:33
  105.5 0.9 pad_maximum_fusion.5
  106.3 0.8 collective-permute-start.17
  107.1 1.4 %fusion.75 = f32[3,3,64,4,256]{4,2,3,1,0:T(8,128)S(1)} fusion(bf16[3,3,64,1024,1]{3,2,4,1,0:T(8,128)(2,1)S(1)} %bitcast.166, bf16[4,256,1024,1,1]{2,1,0,4,3:T(8,128)(2,1)S(1)} %bitcast.162), kind=kOutput, calls=%fused_computation.192 | convolution fusion | flops 1207959552 | bytes 5636096 | tf_op jit(solution)/shard_map/dot_general | solution.py:122
  109.1 1.3 collective-permute-start.9
  110.4 4.5 %collective-permute-start.8 = (f32[64,256]{1,0:T(8,128)S(1)}, f32[64,256]{1,0:T(8,128)S(1)}, u32[]{:S(2)}, u32[]{:S(2)}) collective-permute-start(f32[64,256]{1,0:T(8,128)S(1)} %get-tuple-element.44), channel_id=1, source_target_pairs={{0,2},{1,3},{4,6},{5,7},{8,10},{9,11},{12,14},{13,15},{16,18},{17,... | collective-permute-start | bytes 196616 | tf_op jit(solution)/shard_map/ppermute | solution.py:127
  115.2 5.0 %collective-permute-done.8 = f32[64,256]{1,0:T(8,128)S(1)} collective-permute-done((f32[64,256]{1,0:T(8,128)S(1)}, f32[64,256]{1,0:T(8,128)S(1)}, u32[]{:S(2)}, u32[]{:S(2)}) %collective-permute-start.8) | collective-permute-done | bytes 65568 | tf_op jit(solution)/shard_map/ppermute | solution.py:127
  120.3 1.6 %collective-permute-done.9 = f32[64,256]{1,0:T(8,128)S(1)} collective-permute-done((f32[64,256]{1,0:T(8,128)S(1)}, f32[64,256]{1,0:T(8,128)S(1)}, u32[]{:S(2)}, u32[]{:S(2)}) %collective-permute-start.9) | collective-permute-done | bytes 65568 | tf_op jit(solution)/shard_map/ppermute | solution.py:128
  122.7 1.0 fusion.40
  123.6 1.7 %copy.27 = bf16[128,2,256]{2,1,0:T(2,128)(2,1)} copy(bf16[128,2,256]{0,2,1:T(8,128)(2,1)} %bitcast.186) | data formatting | bytes 262144 | tf_op jit(solution)/shard_map/convert_element_type | solution.py:99
  125.3 0.9 broadcast_select_fusion.6
  126.2 0.8 copy.15
  127.0 0.7 fusion.49
  127.7 2.5 %fusion.9 = f32[288,1024]{1,0:T(8,128)} fusion(f32[2,288,1024]{2,1,0:T(8,128)S(1)} %copy-done.1, s32[]{:T(128)S(6)} %select_n.326, bf16[304,1024]{1,0:T(8,128)(2,1)} %collective-permute-done.17, f32[1024]{0:T(1024)S(1)} %bitcast.191), kind=kLoop, calls=%fused_computation.19 | loop fusion | flops 2949120 | bytes 2953220 | tf_op jit(solution)/shard_map/mul | solution.py:119
  (127 shorter events, 10.2 us)
Async XLA Ops:
  0.6 13.3 %copy-start.7 = (bf16[128,2,256]{2,1,0:T(2,128)(2,1)S(1)}, bf16[128,2,256]{2,1,0:T(2,128)(2,1)}, u32[]{:S(2)}) copy-start(bf16[128,2,256]{2,1,0:T(2,128)(2,1)} %param.7) | copy-start | bytes 393220
  2.3 36.8 %collective-permute-start.6 = (bf16[128,512]{1,0:T(8,128)(2,1)}, bf16[128,512]{1,0:T(8,128)(2,1)}, u32[]{:S(2)}, u32[]{:S(2)}) collective-permute-start(bf16[128,512]{1,0:T(8,128)(2,1)} %bitcast.77), channel_id=1, source_target_pairs={{0,28},{4,24},{8,20},{12,16},{16,12},{20,8},{24,4},{28,0},{1,29},{... | collective-permute-start | bytes 393224 | tf_op jit(solution)/shard_map/ppermute | solution.py:15
  8.3 29.9 %collective-permute-start.5 = (bf16[128,512]{1,0:T(8,128)(2,1)}, bf16[128,512]{1,0:T(8,128)(2,1)}, u32[]{:S(2)}, u32[]{:S(2)}) collective-permute-start(bf16[128,512]{1,0:T(8,128)(2,1)} %bitcast.77), channel_id=1, source_target_pairs={{0,24},{4,28},{8,16},{12,20},{16,8},{20,12},{24,0},{28,4},{1,25},{... | collective-permute-start | bytes 393224 | tf_op jit(solution)/shard_map/ppermute | solution.py:15
  8.5 28.7 %collective-permute-start.4 = (bf16[128,512]{1,0:T(8,128)(2,1)}, bf16[128,512]{1,0:T(8,128)(2,1)}, u32[]{:S(2)}, u32[]{:S(2)}) collective-permute-start(bf16[128,512]{1,0:T(8,128)(2,1)} %bitcast.77), channel_id=1, source_target_pairs={{0,20},{4,16},{8,28},{12,24},{16,4},{20,0},{24,12},{28,8},{1,21},{... | collective-permute-start | bytes 393224 | tf_op jit(solution)/shard_map/ppermute | solution.py:15
  9.2 13.7 %collective-permute-start = (bf16[128,512]{1,0:T(8,128)(2,1)}, bf16[128,512]{1,0:T(8,128)(2,1)}, u32[]{:S(2)}, u32[]{:S(2)}) collective-permute-start(bf16[128,512]{1,0:T(8,128)(2,1)} %bitcast.77), channel_id=1, source_target_pairs={{0,4},{4,0},{8,12},{12,8},{16,20},{20,16},{24,28},{28,24},{1,5},{5... | collective-permute-start | bytes 393224 | tf_op jit(solution)/shard_map/ppermute | solution.py:15
  12.6 7.0 %collective-permute-start.11 = (bf16[128,256]{1,0:T(8,128)(2,1)}, bf16[128,256]{1,0:T(8,128)(2,1)}, u32[]{:S(2)}, u32[]{:S(2)}) collective-permute-start(bf16[128,256]{1,0:T(8,128)(2,1)} %fusion.48), channel_id=1, source_target_pairs={{1,2},{2,1},{5,6},{6,5},{9,10},{10,9},{13,14},{14,13},{17,18},{18,... | collective-permute-start | bytes 196616 | tf_op jit(solution)/shard_map/ppermute | solution.py:72
  14.0 3.1 %copy-start = (bf16[3,3,128,1024]{3,2,1,0:T(8,128)(2,1)S(1)}, bf16[3,3,128,1024]{3,2,1,0:T(8,128)(2,1)}, u32[]{:S(2)}) copy-start(bf16[3,3,128,1024]{3,2,1,0:T(8,128)(2,1)} %param.8) | copy-start | bytes 7077892
  17.0 5.6 %copy-start.5 = (bf16[128,2,256]{2,1,0:T(2,128)(2,1)S(1)}, bf16[128,2,256]{2,1,0:T(2,128)(2,1)}, u32[]{:S(2)}) copy-start(bf16[128,2,256]{2,1,0:T(2,128)(2,1)} %param.9) | copy-start | bytes 393220
  19.6 17.6 %collective-permute-start.3 = (bf16[128,512]{1,0:T(8,128)(2,1)}, bf16[128,512]{1,0:T(8,128)(2,1)S(1)}, u32[]{:S(2)}, u32[]{:S(2)}) collective-permute-start(bf16[128,512]{1,0:T(8,128)(2,1)} %bitcast.77), channel_id=1, source_target_pairs={{0,16},{4,20},{8,24},{12,28},{16,0},{20,4},{24,8},{28,12},{1,17},{... | collective-permute-start | bytes 393224 | tf_op jit(solution)/shard_map/ppermute | solution.py:15
  23.0 6.9 %collective-permute-start.1 = (bf16[128,512]{1,0:T(8,128)(2,1)}, bf16[128,512]{1,0:T(8,128)(2,1)S(1)}, u32[]{:S(2)}, u32[]{:S(2)}) collective-permute-start(bf16[128,512]{1,0:T(8,128)(2,1)} %bitcast.77), channel_id=1, source_target_pairs={{0,8},{4,12},{8,0},{12,4},{16,24},{20,28},{24,16},{28,20},{1,9},{5... | collective-permute-start | bytes 393224 | tf_op jit(solution)/shard_map/ppermute | solution.py:15
  29.9 7.3 %collective-permute-start.2 = (bf16[128,512]{1,0:T(8,128)(2,1)}, bf16[128,512]{1,0:T(8,128)(2,1)S(1)}, u32[]{:S(2)}, u32[]{:S(2)}) collective-permute-start(bf16[128,512]{1,0:T(8,128)(2,1)} %bitcast.77), channel_id=1, source_target_pairs={{0,12},{4,8},{8,4},{12,0},{16,28},{20,24},{24,20},{28,16},{1,13},{... | collective-permute-start | bytes 393224 | tf_op jit(solution)/shard_map/ppermute | solution.py:15
  37.2 4.7 %collective-permute-start.12 = (bf16[128,3,256]{2,1,0:T(4,128)(2,1)S(1)}, bf16[128,3,256]{2,1,0:T(4,128)(2,1)S(1)}, u32[]{:S(2)}, u32[]{:S(2)}) collective-permute-start(bf16[128,3,256]{2,1,0:T(4,128)(2,1)S(1)} %pad_maximum_fusion.9), channel_id=1, source_target_pairs={{0,1},{1,0},{2,3},{3,2},{4,5},{5,4},{6,7},{7,6},{8,9},{9,8},{10,11... | collective-permute-start | bytes 589832 | tf_op jit(solution)/shard_map/ppermute | solution.py:15
  41.3 52.6 %collective-permute-start.7 = (bf16[1024,512]{1,0:T(8,128)(2,1)S(1)}, bf16[1024,512]{1,0:T(8,128)(2,1)}, u32[]{:S(2)}, u32[]{:S(2)}) collective-permute-start(bf16[1024,512]{1,0:T(8,128)(2,1)S(1)} %fusion.23), channel_id=1, source_target_pairs={{0,1},{1,0},{2,3},{3,2},{4,5},{5,4},{6,7},{7,6},{8,9},{9,8},{10,11... | collective-permute-start | bytes 3145736 | tf_op jit(solution)/shard_map/ppermute | solution.py:15
  45.4 1.7 %copy-start.3 = (bf16[1024,1152]{1,0:T(8,128)(2,1)S(1)}, bf16[1024,1152]{1,0:T(8,128)(2,1)}, u32[]{:S(2)}) copy-start(bf16[1024,1152]{1,0:T(8,128)(2,1)} %copy.19) | copy-start | bytes 7077892
  58.9 1.4 %copy-start.2 = (f32[512,4,1,128]{0,3,2,1:T(8,128)S(1)}, f32[512,4,1,128]{0,3,2,1:T(8,128)}, u32[]{:S(2)}) copy-start(f32[512,4,1,128]{0,3,2,1:T(8,128)} %get-tuple-element.40) | copy-start | bytes 3145732
  59.8 1.0 copy-start.10
  59.8 14.5 %collective-permute-start.13 = (bf16[528,512]{1,0:T(8,128)(2,1)}, bf16[528,512]{1,0:T(8,128)(2,1)}, u32[]{:S(2)}, u32[]{:S(2)}) collective-permute-start(bf16[528,512]{1,0:T(8,128)(2,1)} %pad_maximum_fusion.6), channel_id=1, source_target_pairs={{0,4},{4,0},{8,12},{12,8},{16,20},{20,16},{24,28},{28,24},{1,5},{5... | collective-permute-start | bytes 1622024 | tf_op jit(solution)/shard_map/ppermute | solution.py:15
  60.3 4.2 %copy-start.9 = (bf16[2,1,32,1024]{3,2,1,0:T(8,128)(2,1)S(1)}, bf16[2,1,32,1024]{3,2,1,0:T(8,128)(2,1)}, u32[]{:S(2)}) copy-start(bf16[2,1,32,1024]{3,2,1,0:T(8,128)(2,1)} %stack_reshape.35) | copy-start | bytes 393220
  60.7 6.0 %copy-start.11 = (bf16[2,1,32,1024]{3,2,1,0:T(8,128)(2,1)S(1)}, bf16[2,1,32,1024]{3,2,1,0:T(8,128)(2,1)}, u32[]{:S(2)}) copy-start(bf16[2,1,32,1024]{3,2,1,0:T(8,128)(2,1)} %stack_reshape.37) | copy-start | bytes 393220
  76.4 0.9 copy-start.8
  76.9 7.5 %collective-permute-start.14 = (bf16[528,128]{1,0:T(8,128)(2,1)S(1)}, bf16[528,128]{1,0:T(8,128)(2,1)S(1)}, u32[]{:S(2)}, u32[]{:S(2)}) collective-permute-start(bf16[528,128]{1,0:T(8,128)(2,1)S(1)} %get-tuple-element.53), channel_id=1, source_target_pairs={{0,8},{4,12},{8,0},{12,4},{16,24},{20,28},{24,16},{28,20},{1,9},{5... | collective-permute-start | bytes 405512 | tf_op jit(solution)/shard_map/ppermute | solution.py:15
  78.7 15.1 %collective-permute-start.15 = (bf16[528,128]{1,0:T(8,128)(2,1)S(1)}, bf16[528,128]{1,0:T(8,128)(2,1)S(1)}, u32[]{:S(2)}, u32[]{:S(2)}) collective-permute-start(bf16[528,128]{1,0:T(8,128)(2,1)S(1)} %get-tuple-element.54), channel_id=1, source_target_pairs={{0,16},{4,20},{8,24},{12,28},{16,0},{20,4},{24,8},{28,12},{1,17},{... | collective-permute-start | bytes 405512 | tf_op jit(solution)/shard_map/ppermute | solution.py:15
  84.4 9.5 %collective-permute-start.16 = (bf16[528,128]{1,0:T(8,128)(2,1)S(1)}, bf16[528,128]{1,0:T(8,128)(2,1)S(1)}, u32[]{:S(2)}, u32[]{:S(2)}) collective-permute-start(bf16[528,128]{1,0:T(8,128)(2,1)S(1)} %get-tuple-element.55), channel_id=1, source_target_pairs={{0,24},{4,28},{8,16},{12,20},{16,8},{20,12},{24,0},{28,4},{1,25},{... | collective-permute-start | bytes 405512 | tf_op jit(solution)/shard_map/ppermute | solution.py:15
  84.4 10.9 %copy-start.12 = (bf16[528,128]{1,0:T(8,128)(2,1)}, bf16[528,128]{1,0:T(8,128)(2,1)S(1)}, u32[]{:S(2)}) copy-start(bf16[528,128]{1,0:T(8,128)(2,1)S(1)} %collective-permute-done.14) | copy-start | bytes 405508
  93.8 1.5 %copy-start.14 = (bf16[528,128]{1,0:T(8,128)(2,1)}, bf16[528,128]{1,0:T(8,128)(2,1)S(1)}, u32[]{:S(2)}) copy-start(bf16[528,128]{1,0:T(8,128)(2,1)S(1)} %collective-permute-done.15) | copy-start | bytes 405508
  93.8 1.5 %copy-start.16 = (bf16[528,128]{1,0:T(8,128)(2,1)}, bf16[528,128]{1,0:T(8,128)(2,1)S(1)}, u32[]{:S(2)}) copy-start(bf16[528,128]{1,0:T(8,128)(2,1)S(1)} %collective-permute-done.16) | copy-start | bytes 405508
  95.3 1.3 copy-start.18
  102.2 4.9 %copy-start.6 = (bf16[9,2,1,32,1024]{4,3,2,1,0:T(8,128)(2,1)S(1)}, bf16[9,2,1,32,1024]{4,3,2,1,0:T(8,128)(2,1)}, u32[]{:S(2)}) copy-start(bf16[9,2,1,32,1024]{4,3,2,1,0:T(8,128)(2,1)} %slice_select_fusion) | copy-start | bytes 3538948
  103.6 3.5 %copy-start.4 = (bf16[1024,1024]{1,0:T(8,128)(2,1)S(1)}, bf16[1024,1024]{1,0:T(8,128)(2,1)}, u32[]{:S(2)}) copy-start(bf16[1024,1024]{1,0:T(8,128)(2,1)} %copy.14) | copy-start | bytes 6291460
  106.3 20.7 %collective-permute-start.17 = (bf16[304,1024]{1,0:T(8,128)(2,1)}, bf16[304,1024]{1,0:T(8,128)(2,1)}, u32[]{:S(2)}, u32[]{:S(2)}) collective-permute-start(bf16[304,1024]{1,0:T(8,128)(2,1)} %pad_maximum_fusion.5), channel_id=1, source_target_pairs={{0,2},{1,3},{2,0},{3,1},{4,6},{5,7},{6,4},{7,5},{8,10},{9,11},{10,... | collective-permute-start | bytes 1867784 | tf_op jit(solution)/shard_map/ppermute | solution.py:15
  109.1 12.9 %collective-permute-start.9 = (f32[64,256]{1,0:T(8,128)S(1)}, f32[64,256]{1,0:T(8,128)S(1)}, u32[]{:S(2)}, u32[]{:S(2)}) collective-permute-start(f32[64,256]{1,0:T(8,128)S(1)} %get-tuple-element.43), channel_id=1, source_target_pairs={{2,0},{3,1},{6,4},{7,5},{10,8},{11,9},{14,12},{15,13},{18,16},{19,... | collective-permute-start | bytes 196616 | tf_op jit(solution)/shard_map/ppermute | solution.py:128
  110.4 9.8 %collective-permute-start.8 = (f32[64,256]{1,0:T(8,128)S(1)}, f32[64,256]{1,0:T(8,128)S(1)}, u32[]{:S(2)}, u32[]{:S(2)}) collective-permute-start(f32[64,256]{1,0:T(8,128)S(1)} %get-tuple-element.44), channel_id=1, source_target_pairs={{0,2},{1,3},{4,6},{5,7},{8,10},{9,11},{12,14},{13,15},{16,18},{17,... | collective-permute-start | bytes 196616 | tf_op jit(solution)/shard_map/ppermute | solution.py:127
  115.2 7.5 %copy-start.13 = (bf16[528,128]{1,0:T(8,128)(2,1)S(1)}, bf16[528,128]{1,0:T(8,128)(2,1)}, u32[]{:S(2)}) copy-start(bf16[528,128]{1,0:T(8,128)(2,1)} %copy-done.12) | copy-start | bytes 405508
  115.2 7.5 %copy-start.15 = (bf16[528,128]{1,0:T(8,128)(2,1)S(1)}, bf16[528,128]{1,0:T(8,128)(2,1)}, u32[]{:S(2)}) copy-start(bf16[528,128]{1,0:T(8,128)(2,1)} %copy-done.14) | copy-start | bytes 405508
  115.2 7.5 %copy-start.17 = (bf16[528,128]{1,0:T(8,128)(2,1)S(1)}, bf16[528,128]{1,0:T(8,128)(2,1)}, u32[]{:S(2)}) copy-start(bf16[528,128]{1,0:T(8,128)(2,1)} %copy-done.16) | copy-start | bytes 405508
  122.0 5.7 %copy-start.1 = (f32[2,288,1024]{2,1,0:T(8,128)S(1)}, f32[2,288,1024]{2,1,0:T(8,128)}, u32[]{:S(2)}) copy-start(f32[2,288,1024]{2,1,0:T(8,128)} %fusion) | copy-start | bytes 7077892
  122.7 2.7 %collective-permute-start.10 = (bf16[64,2,256]{2,0,1:T(8,128)(2,1)}, bf16[64,2,256]{2,0,1:T(8,128)(2,1)}, u32[]{:S(2)}, u32[]{:S(2)}) collective-permute-start(bf16[64,2,256]{2,0,1:T(8,128)(2,1)} %broadcast_select_fusion.7), channel_id=1, source_target_pairs={{0,1},{1,0},{2,3},{3,2},{4,5},{5,4},{6,7},{7,6},{8,9},{9,8},{10,11... | collective-permute-start | bytes 196616 | tf_op jit(solution)/shard_map/ppermute | solution.py:15

commit v2 on v1

--- a/solution.py
+++ b/solution.py
@@ -1,13 +1,277 @@
+import functools
 import math
 
 import jax
 import jax.numpy as jnp
 from jax import lax
+from jax.experimental import pallas as pl
+from jax.experimental.pallas import tpu as pltpu
 from jax.sharding import PartitionSpec as P
 
 BF16, F32 = jnp.bfloat16, jnp.float32
 SPAN = 124.0
 LEAST = 2.0**-100
+EXTRA = 16
+VMEM_BYTES = 40 * 2**20
+
+
+def call(body, outs, args, scratch=(), flops=0):
+    size = sum(math.prod(x.shape) * x.dtype.itemsize for x in (*outs, *args))
+    return pl.pallas_call(
+        body,
+        out_shape=tuple(outs),
+        in_specs=[pl.BlockSpec(memory_space=pltpu.VMEM)] * len(args),
+        out_specs=tuple(pl.BlockSpec(memory_space=pltpu.VMEM) for _ in outs),
+        scratch_shapes=list(scratch),
+        compiler_params=pltpu.CompilerParams(vmem_limit_bytes=VMEM_BYTES),
+        cost_estimate=pl.CostEstimate(flops=flops, bytes_accessed=size, transcendentals=0),
+    )(*args)
+
+
+def shape(dims, dtype):
+    return jax.ShapeDtypeStruct(dims, dtype)
+
+
+def rounded_up(top):
+    return jnp.maximum(top * 1.01, LEAST).astype(BF16)
+
+
+def put_coded(ref, columns, values):
+    number = values.shape[0]
+    size = jnp.abs(values)
+    top = rounded_up(jnp.max(size, axis=0, keepdims=True))
+    code = jnp.exp2(size * ((2 * SPAN) / top.astype(F32)) - SPAN)
+    ref[:number, columns] = jnp.where(values < 0, -code, code).astype(BF16)
+    ref[number:, columns] = jnp.broadcast_to(top, (EXTRA, values.shape[1]))
+
+
+def get_coded(ref, columns):
+    number = ref.shape[0] - EXTRA
+    step = ref[number:, columns].astype(F32)[:1] * (0.5 / SPAN)
+    code = ref[:number, columns].astype(F32)
+    size = (jnp.log2(jnp.abs(code)) + SPAN) * step
+    return jnp.where(code < 0, -size, size)
+
+
+def window_of(core, own, adj, halo, width):
+    before = jnp.where(core == 0, halo, adj[:, -width:])
+    after = jnp.where(core == 0, adj[:, :width], halo)
+    return jnp.concatenate([before, own, after], axis=1)
+
+
+def data_kernel(width, own_ref, adj_ref, halo_ref, w_ref, keep_ref, give_ref, left):
+    core = lax.axis_index("rows") % 2
+    y = lax.axis_index("chan") % 2
+    local, cells = own_ref.shape
+    slab = window_of(core, own_ref[...], adj_ref[...], halo_ref[...], width).astype(F32)
+    turned = slab.T
+    count = turned.shape[0]
+    column = lax.broadcasted_iota(jnp.int32, turned.shape, 0) % width
+    moved = [
+        jnp.where(column == width - 1, 0.0, pltpu.roll(turned, count - 1, 0)),
+        turned,
+        jnp.where(column == 0, 0.0, pltpu.roll(turned, 1, 0)),
+    ]
+    moved = [m.astype(BF16) for m in moved]
+    for a in range(3):
+        for b in range(3):
+            tap = 3 * a + b
+            left[:, tap * local : (tap + 1) * local] = moved[b][(2 - a) * width : (2 - a) * width + cells]
+    for z in range(w_ref.shape[1] // (2 * local)):
+        sums = jnp.dot(left[...], w_ref[:, 2 * z * local : 2 * (z + 1) * local], preferred_element_type=F32)
+        even, odd = sums[:, :local], sums[:, local:]
+        here = slice(z * local, (z + 1) * local)
+        keep_ref[:, here] = jnp.where(y == 0, even, odd)
+        put_coded(give_ref, here, jnp.where(y == 0, odd, even))
+
+
+def data_sums(own, adj, halo, taps, width):
+    local, cells = own.shape
+    channels = taps.shape[1]
+    outs = [shape((cells, channels // 2), F32), shape((cells + EXTRA, channels // 2), BF16)]
+    return call(
+        functools.partial(data_kernel, width), outs, (own, adj, halo, taps),
+        [pltpu.VMEM((cells, 9 * local), BF16)], 2 * cells * 9 * local * channels,
+    )
+
+
+def middle_kernel(come_ref, keep_ref, own_ref, *piece_refs):
+    z = (lax.axis_index("chan") // 2)
+    local = own_ref.shape[1]
+    for k in range(len(piece_refs) + 1):
+        here = pl.ds(pl.multiple_of((z ^ k) * local, local), local)
+        total = keep_ref[:, here] + get_coded(come_ref, here)
+        if k == 0:
+            own_ref[...] = total
+        else:
+            put_coded(piece_refs[k - 1], slice(None), total)
+
+
+def middle(come, keep, local):
+    cells, columns = keep.shape
+    outs = [shape((cells, local), F32)] + [shape((cells + EXTRA, local), BF16)] * (columns // local - 1)
+    return call(middle_kernel, outs, (come, keep))
+
+
+def last_data_kernel(own_ref, *refs):
+    total = own_ref[...]
+    for ref in refs[:-1]:
+        total = total + get_coded(ref, slice(None))
+    refs[-1][...] = total.T.astype(BF16)
+
+
+def last_data(own, pieces):
+    return call(last_data_kernel, [shape(own.shape[::-1], BF16)], (own, *pieces))[0]
+
+
+def pair_of(y, near, far):
+    return jnp.concatenate([jnp.where(y == 0, near, far), jnp.where(y == 0, far, near)], axis=0)
+
+
+def filter_kernel(pairs, width, own_ref, adj_ref, halo_ref, rim_ref, *refs):
+    row = lax.axis_index("rows")
+    core, chip = row % 2, row // 2
+    y = lax.axis_index("chan") % 2
+    near, far, near_o, far_o = (refs[i * pairs : (i + 1) * pairs] for i in range(4))
+    keep_ref, give_ref, left = refs[4 * pairs :]
+    local, cells = own_ref.shape
+    share = keep_ref.shape[0] // 9
+    own, adj = own_ref[...], adj_ref[...]
+    halo, rim = halo_ref[...], rim_ref[...]
+    mine = window_of(core, own, adj, halo, width)
+    theirs = window_of(1 - core, adj, own, rim, width)
+    both = jnp.concatenate([mine, theirs], axis=1)
+    place = lax.broadcasted_iota(jnp.int32, (2 * share, local), 0)
+    wanted = jnp.where(place < share, chip * 2 + core, (1 - chip) * 2 + core) * share + place % share
+    pick = (lax.broadcasted_iota(jnp.int32, (2 * share, local), 1) == wanted).astype(BF16)
+    chosen = jnp.dot(pick, both, preferred_element_type=F32)
+    count = chosen.shape[1]
+    column = lax.broadcasted_iota(jnp.int32, chosen.shape, 1) % width
+    moved = [
+        jnp.where(column == width - 1, 0.0, pltpu.roll(chosen, count - 1, 1)),
+        chosen,
+        jnp.where(column == 0, 0.0, pltpu.roll(chosen, 1, 1)),
+    ]
+    moved = [m.astype(BF16) for m in moved]
+    span = count // 2
+    for part in range(2):
+        for a in range(3):
+            for b in range(3):
+                tap = 3 * a + b
+                start = part * span + (2 - a) * width
+                for q in range(2):
+                    left[q * 9 * share + tap * share : q * 9 * share + (tap + 1) * share,
+                         part * cells : (part + 1) * cells] = moved[b][q * share : (q + 1) * share, start : start + cells]
+    for t in range(pairs):
+        right = jnp.concatenate(
+            [pair_of(y, near[t][...], far[t][...]), pair_of(y, near_o[t][...], far_o[t][...])], axis=1
+        )
+        here = slice(t * 2 * local, (t + 1) * 2 * local)
+        for q in (1, 0):
+            sums = lax.dot_general(
+                left[q * 9 * share : (q + 1) * 9 * share], right, (((1,), (1,)), ((), ())), preferred_element_type=F32
+            )
+            if q:
+                put_coded(give_ref, here, sums)
+            else:
+                keep_ref[:, here] = sums
+
+
+def filter_sums(own, adj, halo, rim, near, far, near_o, far_o, share, width):
+    local, cells = own.shape
+    pairs = len(near)
+    outs = [shape((9 * share, pairs * 2 * local), F32), shape((9 * share + EXTRA, pairs * 2 * local), BF16)]
+    return call(
+        functools.partial(filter_kernel, pairs, width), outs, (own, adj, halo, rim, *near, *far, *near_o, *far_o),
+        [pltpu.VMEM((18 * share, 2 * cells), BF16)], 2 * 18 * share * 2 * cells * pairs * 2 * local,
+    )
+
+
+def last_filter_kernel(groups, scale, *refs):
+    z = lax.axis_index("chan") // 2
+    out_ref = refs[-1]
+    step = out_ref.shape[1] // sum(groups)
+    t = 0
+    for i, pairs in enumerate(groups):
+        for j in range(pairs):
+            here = slice(j * step, (j + 1) * step)
+            there = pl.ds(pl.multiple_of((z ^ t) * step, step), step)
+            out_ref[:, there] = (refs[2 * i][:, here] + get_coded(refs[2 * i + 1], here)) * scale
+            t += 1
+
+
+def last_filter(groups, parts, channels, scale):
+    outs = [shape((parts[0].shape[0], channels), F32)]
+    return call(functools.partial(last_filter_kernel, groups, scale), outs, parts)[0]
+
+
+def output_kernel(pairs, width, w_ref, *refs):
+    core = lax.axis_index("rows") % 2
+    chan = lax.axis_index("chan")
+    y, z = chan % 2, chan // 2
+    near, far, near_o, far_o = (refs[i * pairs : (i + 1) * pairs] for i in range(4))
+    inner_ref, edge_ref, xs, xo = refs[4 * pairs :]
+    local, cells = near[0].shape
+    for t in range(pairs):
+        there = pl.ds(pl.multiple_of((z ^ t) * 2 * local, 2 * local), 2 * local)
+        xs[there, :] = pair_of(y, near[t][...], far[t][...])
+        other = pair_of(y, near_o[t][...], far_o[t][...])
+        xo[there, :] = jnp.where(core == 0, other[:, :width], other[:, -width:])
+    filters = w_ref.shape[1]
+    w = w_ref[...].reshape(9 * filters, w_ref.shape[2])
+    parts = jnp.dot(w, xs[...], preferred_element_type=F32)
+    beside = w_ref[pl.ds(jnp.where(core == 0, 6, 0), 3)].reshape(3 * filters, w_ref.shape[2])
+    more = jnp.dot(beside, xo[...], preferred_element_type=F32)
+    rows = cells // width
+    lines = [[None] * 3 for _ in range(rows + 2)]
+    for a in range(3):
+        for r in range(rows):
+            for b in range(3):
+                tap = 3 * a + b
+                value = parts[tap * filters : (tap + 1) * filters, r * width : (r + 1) * width]
+                line = lines[r - a + 2]
+                line[b] = value if line[b] is None else line[b] + value
+    for b in range(3):
+        value = more[b * filters : (b + 1) * filters]
+        lines[rows][b] = lines[rows][b] + jnp.where(core == 0, value, 0.0)
+        lines[1][b] = lines[1][b] + jnp.where(core == 0, 0.0, value)
+    column = lax.broadcasted_iota(jnp.int32, (filters, width), 1)
+    total = []
+    for line in lines:
+        left = jnp.where(column == 0, 0.0, pltpu.roll(line[0], 1, 1))
+        right = jnp.where(column == width - 1, 0.0, pltpu.roll(line[2], width - 1, 1))
+        total.append(left + line[1] + right)
+    for r in range(rows):
+        inner_ref[:, r * width : (r + 1) * width] = total[r + 1]
+    edge_ref[...] = jnp.where(core == 0, total[0], total[-1])
+
+
+def output_sums(taps, near, far, near_o, far_o, width):
+    filters, channels = taps.shape[1:]
+    cells = near[0].shape[1]
+    outs = [shape((filters, cells), F32), shape((filters, width), F32)]
+    return call(
+        functools.partial(output_kernel, len(near), width), outs, (taps, *near, *far, *near_o, *far_o),
+        [pltpu.VMEM((channels, cells), BF16), pltpu.VMEM((channels, width), BF16)],
+        2 * 9 * filters * channels * cells * 7 // 6,
+    )
+
+
+def last_output_kernel(width, inner_ref, edge_ref, out_ref):
+    core = lax.axis_index("rows") % 2
+    edge = edge_ref[...]
+    rows = inner_ref.shape[1] // width
+    for r in range(rows):
+        value = inner_ref[:, r * width : (r + 1) * width]
+        if r == 0:
+            value = value + jnp.where(core == 0, edge, 0.0)
+        if r == rows - 1:
+            value = value + jnp.where(core == 0, 0.0, edge)
+        out_ref[:, r * width : (r + 1) * width] = value.astype(BF16)
+
+
+def last_output(inner, edge, width):
+    return call(functools.partial(last_output_kernel, width), [shape(inner.shape, BF16)], (inner, edge))[0]
 
 
 def exchange(x, axis, distance):
@@ -54,7 +318,7 @@
     return blocks.reshape((size * x.shape[0],) + x.shape[1:])
 
 
-def per_device(activations, weights, cotangent):
+def plain(activations, weights, cotangent):
     local, height, width = activations.shape
     chans, rows = lax.axis_size("chan"), lax.axis_size("rows")
     chips, zs = rows // 2, chans // 2
@@ -136,6 +400,65 @@
     return output.reshape(local, height, width), input_grad, filter_grad
 
 
+def fast(activations, weights, cotangent):
+    local, height, width = activations.shape
+    chans, rows = lax.axis_size("chan"), lax.axis_size("rows")
+    zs, share, channels = chans // 2, local // rows, weights.shape[3]
+    first = lax.axis_index("rows") % 2 == 0
+    taps = weights.reshape(9, local, channels)
+
+    edges = [(i, i + 1) for i in range(1, rows - 1, 2)]
+    edges += [(j, i) for i, j in edges]
+    edge = jnp.where(first, cotangent[:, 0], cotangent[:, height - 1])
+    halo = lax.ppermute(edge, "rows", edges)
+    g = cotangent.reshape(local, height * width)
+    adj = exchange(g, "rows", 1)
+    x = activations.reshape(local, height * width)
+
+    keep, give = data_sums(g, adj, halo, taps.reshape(9 * local, channels), width)
+    come = exchange(give, "chan", 1)
+
+    blocks = {0: x}
+    for k in (6, 4, 2, 7, 5, 3, 1):
+        blocks[k] = exchange(x, "chan", k)
+    near, far = [blocks[2 * t] for t in range(zs)], [blocks[2 * t + 1] for t in range(zs)]
+    near_o, far_o = ([exchange(b, "rows", 1) for b in side] for side in (near, far))
+    rim = exchange(halo, "rows", 1)
+
+    groups, parts, start = (zs // 2, zs - zs // 2), [], 0
+    for pairs in groups:
+        chosen = slice(start, start + pairs)
+        mine, gift = filter_sums(
+            g, adj, halo, rim, near[chosen], far[chosen], near_o[chosen], far_o[chosen], share, width
+        )
+        parts += [mine, exchange(gift, "rows", 2)]
+        start += pairs
+
+    inner, rest = output_sums(taps, near, far, near_o, far_o, width)
+    output = last_output(inner, lax.ppermute(rest, "rows", edges), width)
+
+    own, *pieces = middle(come, keep, local)
+    pieces = [exchange(piece, "chan", 2 * k) for k, piece in enumerate(pieces, 1)]
+    input_grad = last_data(own, pieces)
+
+    scale = 1.0 / math.sqrt(height * rows * width)
+    filter_grad = last_filter(groups, parts, channels, scale)
+    return (
+        output.reshape(local, height, width),
+        input_grad.reshape(local, height, width),
+        filter_grad.reshape(3, 3, share, channels),
+    )
+
+
+def per_device(activations, weights, cotangent):
+    local, height, width = activations.shape
+    rows = lax.axis_size("rows")
+    whole_tiles = local % 128 == 0 and width % 128 == 0 and (local // rows) % 16 == 0
+    if whole_tiles and height == 2 and rows == 4:
+        return fast(activations, weights, cotangent)
+    return plain(activations, weights, cotangent)
+
+
 def solution(mesh):
     placed = (P("chan", "rows", None), P(None, None, "chan", None), P("chan", "rows", None))
     return jax.shard_map(

time: 132 us -> 63.6 us (0.48)
  local copies, waits for them, and re-layouts: 37.5 us -> 6.11 us
  other arithmetic: 23.5 us -> 0.02 us
  waiting for transfers between devices: 34.9 us -> 17.1 us
  Pallas kernels: 0 us -> 9.08 us
  matrix products: 5.96 us -> 0 us
  starting transfers between devices: 26.9 us -> 29.4 us
    unnamed x71 -> x6, local copies, waits for them, and re-layouts: 15.4 us -> 3.51 us
    ppermute x15 -> x23, waiting for transfers between devices: 28.3 us -> 17.1 us  [exchange(): return lax.ppermute(x, axis, [(i, i ^ distance) for i in range(size)])]
    pallas_call x0 -> x8, Pallas kernels: none -> 9.08 us  [call(): pl.pallas_call(body, out_shape=tuple(outs), in_specs=[pl.BlockSpec(memory...]
    another operation x13 -> x0, local copies, waits for them, and re-layouts: 8.57 us -> none  [the longest x10 6.78 us: per_device(): jnp.stack([moved[b][:, :, 2 - a:2 - a + 2 * height].reshape(chips, share,...]
    ppermute x15 -> x23, starting transfers between devices: 19.8 us -> 28 us  [exchange(): return lax.ppermute(x, axis, [(i, i ^ distance) for i in range(size)])]
    select_n x11 -> x1, other arithmetic: 8.1 us -> 0.02 us  [fast(): edge = jnp.where(first, cotangent[:, 0], cotangent[:, height - 1])]
    ppermute x3 -> x2, waiting for transfers between devices: 6.67 us -> 0.01 us  [the longest x1 0.01 us: fast(): halo = lax.ppermute(edge, 'rows', edges)]
    dot_general x3 -> x0, matrix products: 5.96 us -> none  [the longest x1 3.02 us: per_device(): lax.dot_general(lines.reshape(chips * 9 * share, -1), xchip, (((1,), (1,)...]
  transfers between devices with their start and end apart: 18 -> 25, of which waited for: 6 -> 6; matrix products, arithmetic and copies ran while one was open for 37% -> 5% of each run, Pallas kernels for 0% -> 14%
where the time goes in v2:
time: 63.6 us; the launch traced here: 62.5 us
  starting transfers between devices  29.4 us (46%)
  waiting for transfers between devices  17.1 us (27%)
  Pallas kernels  9.08 us (14%)
  local copies, waits for them, and re-layouts  6.11 us (10%)
  between operations  0.78 us (1%)
    ppermute x23, starting transfers between devices, exchange(): return lax.ppermute(x, axis, [(i, i ^ distance) for i in range(size)])  28 us
    ppermute x23, waiting for transfers between devices, exchange(): return lax.ppermute(x, axis, [(i, i ^ distance) for i in range(size)])  17.1 us
    pallas_call x8, Pallas kernels, call(): pl.pallas_call(body, out_shape=tuple(outs), in_specs=[pl.BlockSpec(memory...  9.08 us
    unnamed x6, local copies, waits for them, and re-layouts  3.51 us
  transfers between devices with their start and end apart: 25, of which 6 were waited for; matrix products, arithmetic and copies ran while one was open for 5% of the time, Pallas kernels for 14%

profile of v2, /device:TPU:0, one launch (start us, length us, event | category | flops | bytes accessed | tf_op | source)
XLA Modules:
  0.0 62.5 jit_solution(13729148946424330255)
XLA Ops:
  0.6 0.9 %copy.10 = bf16[16,8,2,256]{3,1,2,0:T(8,128)(2,1)S(1)} copy(bf16[16,8,2,256]{3,2,1,0:T(2,128)(2,1)} %bitcast.27) | data formatting | bytes 262144
  1.6 6.1 %collective-permute-start.6 = (bf16[128,512]{1,0:T(8,128)(2,1)S(1)}, bf16[128,512]{1,0:T(8,128)(2,1)S(1)}, u32[]{:S(2)}, u32[]{:S(2)}) collective-permute-start(bf16[128,512]{1,0:T(8,128)(2,1)S(1)} %bitcast.9), channel_id=1, source_target_pairs={{0,28},{4,24},{8,20},{12,16},{16,12},{20,8},{24,4},{28,0},{1,29},{... | collective-permute-start | bytes 393224 | tf_op jit(solution)/shard_map/ppermute | solution.py:279
  7.6 0.0 collective-permute-start.5
  7.6 0.9 %copy.11 = bf16[16,8,2,256]{3,1,2,0:T(8,128)(2,1)S(1)} copy(bf16[16,8,2,256]{3,2,1,0:T(2,128)(2,1)} %bitcast.25) | data formatting | bytes 262144
  8.5 0.1 collective-permute-start.16
  8.6 1.2 %fusion.1 = (bf16[128,1,256]{2,1,0:T(2,128)(2,1)S(1)}, bf16[128,1,256]{2,1,0:T(2,128)(2,1)S(1)}) fusion(bf16[128,2,256]{2,1,0:T(2,128)(2,1)} %param.5), kind=kLoop, calls=%fused_computation.2 | loop fusion | bytes 262144 | tf_op jit(solution)/shard_map/slice | solution.py:412
  9.9 0.7 %collective-permute-start.17 = (bf16[128,256]{1,0:T(8,128)(2,1)S(1)}, bf16[128,256]{1,0:T(8,128)(2,1)S(1)}, u32[]{:S(2)}, u32[]{:S(2)}) collective-permute-start(bf16[128,256]{1,0:T(8,128)(2,1)S(1)} %fusion), channel_id=1, source_target_pairs={{1,2},{2,1},{5,6},{6,5},{9,10},{10,9},{13,14},{14,13},{17,18},{18,... | collective-permute-start | bytes 196616 | tf_op jit(solution)/shard_map/ppermute | solution.py:413
  10.6 1.7 %collective-permute-start.4 = (bf16[128,512]{1,0:T(8,128)(2,1)S(1)}, bf16[128,512]{1,0:T(8,128)(2,1)S(1)}, u32[]{:S(2)}, u32[]{:S(2)}) collective-permute-start(bf16[128,512]{1,0:T(8,128)(2,1)S(1)} %bitcast.11), channel_id=1, source_target_pairs={{0,12},{4,8},{8,4},{12,0},{16,28},{20,24},{24,20},{28,16},{1,13},{... | collective-permute-start | bytes 393224 | tf_op jit(solution)/shard_map/ppermute | solution.py:279
  12.3 0.0 collective-permute-done.17.halo_ref
  12.3 0.4 collective-permute-start.3
  12.7 0.0 collective-permute-done.16.adj_ref
  12.7 3.7 %collective-permute-start.2 = (bf16[128,512]{1,0:T(8,128)(2,1)S(1)}, bf16[128,512]{1,0:T(8,128)(2,1)S(1)}, u32[]{:S(2)}, u32[]{:S(2)}) collective-permute-start(bf16[128,512]{1,0:T(8,128)(2,1)S(1)} %bitcast.13), channel_id=1, source_target_pairs={{0,24},{4,28},{8,16},{12,20},{16,8},{20,12},{24,0},{28,4},{1,25},{... | collective-permute-start | bytes 393224 | tf_op jit(solution)/shard_map/ppermute | solution.py:279
  16.4 0.0 collective-permute-done.6.refs_7_.refs_3_
  16.4 2.2 %collective-permute-start.1 = (bf16[128,512]{1,0:T(8,128)(2,1)S(1)}, bf16[128,512]{1,0:T(8,128)(2,1)S(1)}, u32[]{:S(2)}, u32[]{:S(2)}) collective-permute-start(bf16[128,512]{1,0:T(8,128)(2,1)S(1)} %bitcast.14), channel_id=1, source_target_pairs={{0,16},{4,20},{8,24},{12,28},{16,0},{20,4},{24,8},{28,12},{1,17},{... | collective-permute-start | bytes 393224 | tf_op jit(solution)/shard_map/ppermute | solution.py:279
  18.6 0.2 collective-permute-done.5.refs_6_.refs_2_
  18.8 0.0 collective-permute-start
  18.8 1.3 %collective-permute-done.4.refs_5_.refs_3_ = bf16[128,512]{1,0:T(8,128)(2,1)S(1)} collective-permute-done((bf16[128,512]{1,0:T(8,128)(2,1)S(1)}, bf16[128,512]{1,0:T(8,128)(2,1)S(1)}, u32[]{:S(2)}, u32[]{:S(2)}) %collective-permute-start.4) | collective-permute-done | bytes 131104 | tf_op jit(solution)/shard_map/ppermute | solution.py:279
  20.1 3.1 %collective-permute-start.22 = (bf16[128,256]{1,0:T(8,128)(2,1)S(1)}, bf16[128,256]{1,0:T(8,128)(2,1)S(1)}, u32[]{:S(2)}, u32[]{:S(2)}) collective-permute-start(bf16[128,256]{1,0:T(8,128)(2,1)S(1)} %collective-permute-done.17.halo_ref), channel_id=1, source_target_pairs={{0,1},{1,0},{2,3},{3,2},{4,5},{5,4},{6,7},{7,6},{8,9},{9,8},{10,11... | collective-permute-start | bytes 196616 | tf_op jit(solution)/shard_map/ppermute | solution.py:279
  23.2 0.0 collective-permute-done.3.refs_4_.refs_2_
  23.3 0.2 collective-permute-start.14
  23.5 0.0 collective-permute-done.2.refs_3_.refs_1_
  23.5 1.0 %collective-permute-start.13 = (bf16[128,512]{1,0:T(8,128)(2,1)S(1)}, bf16[128,512]{1,0:T(8,128)(2,1)S(1)}, u32[]{:S(2)}, u32[]{:S(2)}) collective-permute-start(bf16[128,512]{1,0:T(8,128)(2,1)S(1)} %collective-permute-done.5.refs_6_.refs_2_), channel_id=1, source_target_pairs={{0,1},{1,0},{2,3},{3,2},{4,5},{5,4},{6,7},{7,6},{8,9},{9,8},{10,11... | collective-permute-start | bytes 393224 | tf_op jit(solution)/shard_map/ppermute | solution.py:279
  24.5 4.1 %collective-permute-done.1.refs_2_.refs_0_ = bf16[128,512]{1,0:T(8,128)(2,1)S(1)} collective-permute-done((bf16[128,512]{1,0:T(8,128)(2,1)S(1)}, bf16[128,512]{1,0:T(8,128)(2,1)S(1)}, u32[]{:S(2)}, u32[]{:S(2)}) %collective-permute-start.1) | collective-permute-done | bytes 131104 | tf_op jit(solution)/shard_map/ppermute | solution.py:279
  28.5 1.2 %collective-permute-start.10 = (bf16[128,512]{1,0:T(8,128)(2,1)S(1)}, bf16[128,512]{1,0:T(8,128)(2,1)S(1)}, u32[]{:S(2)}, u32[]{:S(2)}) collective-permute-start(bf16[128,512]{1,0:T(8,128)(2,1)S(1)} %collective-permute-done.2.refs_3_.refs_1_), channel_id=1, source_target_pairs={{0,1},{1,0},{2,3},{3,2},{4,5},{5,4},{6,7},{7,6},{8,9},{9,8},{10,11... | collective-permute-start | bytes 393224 | tf_op jit(solution)/shard_map/ppermute | solution.py:279
  29.8 0.0 collective-permute-done.refs_1_
  29.8 0.0 collective-permute-start.9
  29.8 1.7 %copy-done = bf16[3,3,128,1024]{3,2,1,0:T(8,128)(2,1)S(1)} copy-done((bf16[3,3,128,1024]{3,2,1,0:T(8,128)(2,1)S(1)}, bf16[3,3,128,1024]{3,2,1,0:T(8,128)(2,1)}, u32[]{:S(2)}) %copy-start) | copy-done | bytes 2359320
  31.4 1.9 %shard_map.60 = (f32[512,512]{1,0:T(8,128)S(1)}, bf16[528,512]{1,0:T(8,128)(2,1)S(1)}) custom-call(bf16[128,512]{1,0:T(8,128)(2,1)S(1)} %bitcast.20, bf16[128,512]{1,0:T(8,128)(2,1)S(1)} %collective-permute-done.16.adj_ref, bf16[128,256]{1,0:T(8,128)(2,1)S(1)} %collective-permute-done.17.halo_ref, bf16[1152,1024]{1,0:T(8,128)(2,1)S(1)} %bitcast.23), custom_call_target="tpu_custom_call" | custom-call | flops 1207959552 | bytes 4276224 | tf_op jit(solution)/shard_map/pallas_call | solution.py:20
  33.4 0.0 copy-start.1
  33.4 0.0 collective-permute-done.22.rim_ref
  33.4 0.7 %collective-permute-start.18 = (bf16[528,512]{1,0:T(8,128)(2,1)S(1)}, bf16[528,512]{1,0:T(8,128)(2,1)S(1)}, u32[]{:S(2)}, u32[]{:S(2)}) collective-permute-start(bf16[528,512]{1,0:T(8,128)(2,1)S(1)} %get-tuple-element.17), channel_id=1, source_target_pairs={{0,4},{4,0},{8,12},{12,8},{16,20},{20,16},{24,28},{28,24},{1,5},{5... | collective-permute-start | bytes 1622024 | tf_op jit(solution)/shard_map/ppermute | solution.py:279
  34.1 0.0 collective-permute-done.14.refs_15_.refs_7_
  34.1 0.2 collective-permute-start.7
  34.3 0.0 collective-permute-done.13.refs_14_.refs_6_
  34.3 0.3 collective-permute-start.12
  34.6 0.0 collective-permute-done.10.refs_11_.refs_5_
  34.6 0.2 collective-permute-start.11
  34.8 0.0 collective-permute-done.9.refs_10_.refs_4_
  34.8 0.3 collective-permute-start.8
  35.1 1.1 %shard_map.64 = (f32[288,512]{1,0:T(8,128)S(1)}, bf16[304,512]{1,0:T(8,128)(2,1)S(1)}) custom-call(bf16[128,512]{1,0:T(8,128)(2,1)S(1)} %bitcast.21, bf16[128,512]{1,0:T(8,128)(2,1)S(1)} %collective-permute-done.16.adj_ref, bf16[128,256]{1,0:T(8,128)(2,1)S(1)} %collective-permute-done.17.halo_ref, bf16[128,256]{1,0:T(8,128)(2,1)S(1)} %collective-permute-done.22.rim_ref, ...), custom_call_target="tpu_custom_call" | custom-call | flops 603979776 | bytes 2342912 | tf_op jit(solution)/shard_map/pallas_call | solution.py:20
  36.2 0.0 collective-permute-done.7.refs_8_.refs_4_
  36.2 2.1 %collective-permute-start.24 = (bf16[304,512]{1,0:T(8,128)(2,1)S(1)}, bf16[304,512]{1,0:T(8,128)(2,1)S(1)}, u32[]{:S(2)}, u32[]{:S(2)}) collective-permute-start(bf16[304,512]{1,0:T(8,128)(2,1)S(1)} %get-tuple-element.26), channel_id=1, source_target_pairs={{0,2},{1,3},{2,0},{3,1},{4,6},{5,7},{6,4},{7,5},{8,10},{9,11},{10,... | collective-permute-start | bytes 933896 | tf_op jit(solution)/shard_map/ppermute | solution.py:279
  38.4 0.0 collective-permute-done.12.refs_13_.refs_7_
  38.4 0.0 collective-permute-done.11.refs_12_.refs_6_
  38.4 0.0 collective-permute-done.8.refs_9_.refs_5_
  38.4 1.1 %shard_map.63 = (f32[288,512]{1,0:T(8,128)S(1)}, bf16[304,512]{1,0:T(8,128)(2,1)S(1)}) custom-call(bf16[128,512]{1,0:T(8,128)(2,1)S(1)} %bitcast.22, bf16[128,512]{1,0:T(8,128)(2,1)S(1)} %collective-permute-done.16.adj_ref, bf16[128,256]{1,0:T(8,128)(2,1)S(1)} %collective-permute-done.17.halo_ref, bf16[128,256]{1,0:T(8,128)(2,1)S(1)} %collective-permute-done.22.rim_ref, ...), custom_call_target="tpu_custom_call" | custom-call | flops 603979776 | bytes 2342912 | tf_op jit(solution)/shard_map/pallas_call | solution.py:20
  39.5 0.1 collective-permute-start.23
  39.6 1.9 %shard_map.58 = (f32[128,512]{1,0:T(8,128)S(1)}, f32[128,256]{1,0:T(8,128)S(1)}) custom-call(bf16[9,128,1024]{2,1,0:T(8,128)(2,1)S(1)} %bitcast.24, bf16[128,512]{1,0:T(8,128)(2,1)S(1)} %bitcast.18, bf16[128,512]{1,0:T(8,128)(2,1)S(1)} %collective-permute-done.refs_1_, bf16[128,512]{1,0:T(8,128)(2,1)S(1)} %collective-permute-done.1.refs_2_.refs_0_, ...), custom_call_target="tpu_custom_call" | custom-call | flops 1409286144 | bytes 4849664 | tf_op jit(solution)/shard_map/pallas_call | solution.py:20
  41.6 0.7 %collective-permute-start.15 = (f32[128,256]{1,0:T(8,128)S(1)}, f32[128,256]{1,0:T(8,128)S(1)}, u32[]{:S(2)}, u32[]{:S(2)}) collective-permute-start(f32[128,256]{1,0:T(8,128)S(1)} %get-tuple-element.16), channel_id=1, source_target_pairs={{1,2},{2,1},{5,6},{6,5},{9,10},{10,9},{13,14},{14,13},{17,18},{18,... | collective-permute-start | bytes 393224 | tf_op jit(solution)/shard_map/ppermute | solution.py:438
  42.3 5.9 %collective-permute-done.18.come_ref = bf16[528,512]{1,0:T(8,128)(2,1)S(1)} collective-permute-done((bf16[528,512]{1,0:T(8,128)(2,1)S(1)}, bf16[528,512]{1,0:T(8,128)(2,1)S(1)}, u32[]{:S(2)}, u32[]{:S(2)}) %collective-permute-start.18) | collective-permute-done | bytes 540704 | tf_op jit(solution)/shard_map/ppermute | solution.py:279
  48.1 1.2 %shard_map.61 = (f32[512,128]{1,0:T(8,128)S(1)}, bf16[528,128]{1,0:T(8,128)(2,1)}, bf16[528,128]{1,0:T(8,128)(2,1)S(1)}, bf16[528,128]{1,0:T(8,128)(2,1)S(1)}) custom-call(bf16[528,512]{1,0:T(8,128)(2,1)S(1)} %collective-permute-done.18.come_ref, f32[512,512]{1,0:T(8,128)S(1)} %get-tuple-element.18.keep_ref), custom_call_target="tpu_custom_call" | custom-call | bytes 2256896 | tf_op jit(solution)/shard_map/pallas_call | solution.py:20
  49.3 0.0 collective-permute-start.19
  49.4 3.1 %collective-permute-start.20 = (bf16[528,128]{1,0:T(8,128)(2,1)S(1)}, bf16[528,128]{1,0:T(8,128)(2,1)S(1)}, u32[]{:S(2)}, u32[]{:S(2)}) collective-permute-start(bf16[528,128]{1,0:T(8,128)(2,1)S(1)} %get-tuple-element.21), channel_id=1, source_target_pairs={{0,16},{4,20},{8,24},{12,28},{16,0},{20,4},{24,8},{28,12},{1,17},{... | collective-permute-start | bytes 405512 | tf_op jit(solution)/shard_map/ppermute | solution.py:279
  52.5 0.0 collective-permute-done.15.edge_ref
  52.5 1.3 %collective-permute-start.21 = (bf16[528,128]{1,0:T(8,128)(2,1)S(1)}, bf16[528,128]{1,0:T(8,128)(2,1)S(1)}, u32[]{:S(2)}, u32[]{:S(2)}) collective-permute-start(bf16[528,128]{1,0:T(8,128)(2,1)S(1)} %get-tuple-element.22), channel_id=1, source_target_pairs={{0,24},{4,28},{8,16},{12,20},{16,8},{20,12},{24,0},{28,4},{1,25},{... | collective-permute-start | bytes 405512 | tf_op jit(solution)/shard_map/ppermute | solution.py:279
  53.8 0.7 %reshape.28 = bf16[128,2,256]{2,1,0:T(2,128)(2,1)} reshape(bf16[128,512]{1,0:T(8,128)(2,1)S(1)} %shard_map.59) | data formatting | bytes 262144 | tf_op jit(solution)/shard_map/reshape | solution.py:447
  54.5 0.0 collective-permute-done.24.refs_3_
  54.5 0.0 collective-permute-done.23.refs_1_
  54.5 1.4 %shard_map.65 = f32[288,1024]{1,0:T(8,128)} custom-call(f32[288,512]{1,0:T(8,128)S(1)} %get-tuple-element.23.refs_0_, bf16[304,512]{1,0:T(8,128)(2,1)S(1)} %collective-permute-done.23.refs_1_, f32[288,512]{1,0:T(8,128)S(1)} %get-tuple-element.25.refs_2_, bf16[304,512]{1,0:T(8,128)(2,1)S(1)} %collective-permute-done.24.refs_3_), custom_call_target="tpu_custom_call" | custom-call | bytes 2981888 | tf_op jit(solution)/shard_map/pallas_call | solution.py:20
  55.9 1.8 %collective-permute-done.19.refs_0_ = bf16[528,128]{1,0:T(8,128)(2,1)S(1)} collective-permute-done((bf16[528,128]{1,0:T(8,128)(2,1)}, bf16[528,128]{1,0:T(8,128)(2,1)S(1)}, u32[]{:S(2)}, u32[]{:S(2)}) %collective-permute-start.19) | collective-permute-done | bytes 135200 | tf_op jit(solution)/shard_map/ppermute | solution.py:279
  57.7 3.8 %collective-permute-done.20.refs_1_ = bf16[528,128]{1,0:T(8,128)(2,1)S(1)} collective-permute-done((bf16[528,128]{1,0:T(8,128)(2,1)S(1)}, bf16[528,128]{1,0:T(8,128)(2,1)S(1)}, u32[]{:S(2)}, u32[]{:S(2)}) %collective-permute-start.20) | collective-permute-done | bytes 135200 | tf_op jit(solution)/shard_map/ppermute | solution.py:279
  61.5 0.0 collective-permute-done.21.refs_2_
  61.5 0.3 shard_map.62
  61.8 0.7 %reshape.30 = bf16[128,2,256]{2,1,0:T(2,128)(2,1)} reshape(bf16[128,512]{1,0:T(8,128)(2,1)S(1)} %shard_map.62) | data formatting | bytes 262144 | tf_op jit(solution)/shard_map/reshape | solution.py:448
  (4 shorter events, 0.1 us)
Async XLA Ops:
  1.6 14.9 %collective-permute-start.6 = (bf16[128,512]{1,0:T(8,128)(2,1)S(1)}, bf16[128,512]{1,0:T(8,128)(2,1)S(1)}, u32[]{:S(2)}, u32[]{:S(2)}) collective-permute-start(bf16[128,512]{1,0:T(8,128)(2,1)S(1)} %bitcast.9), channel_id=1, source_target_pairs={{0,28},{4,24},{8,20},{12,16},{16,12},{20,8},{24,4},{28,0},{1,29},{... | collective-permute-start | bytes 393224 | tf_op jit(solution)/shard_map/ppermute | solution.py:279
  7.6 11.2 %collective-permute-start.5 = (bf16[128,512]{1,0:T(8,128)(2,1)S(1)}, bf16[128,512]{1,0:T(8,128)(2,1)S(1)}, u32[]{:S(2)}, u32[]{:S(2)}) collective-permute-start(bf16[128,512]{1,0:T(8,128)(2,1)S(1)} %bitcast.10), channel_id=1, source_target_pairs={{0,20},{4,16},{8,28},{12,24},{16,4},{20,0},{24,12},{28,8},{1,21},{... | collective-permute-start | bytes 393224 | tf_op jit(solution)/shard_map/ppermute | solution.py:279
  8.5 4.2 %collective-permute-start.16 = (bf16[128,512]{1,0:T(8,128)(2,1)S(1)}, bf16[128,512]{1,0:T(8,128)(2,1)S(1)}, u32[]{:S(2)}, u32[]{:S(2)}) collective-permute-start(bf16[128,512]{1,0:T(8,128)(2,1)S(1)} %bitcast.19), channel_id=1, source_target_pairs={{0,1},{1,0},{2,3},{3,2},{4,5},{5,4},{6,7},{7,6},{8,9},{9,8},{10,11... | collective-permute-start | bytes 393224 | tf_op jit(solution)/shard_map/ppermute | solution.py:279
  9.9 2.4 %collective-permute-start.17 = (bf16[128,256]{1,0:T(8,128)(2,1)S(1)}, bf16[128,256]{1,0:T(8,128)(2,1)S(1)}, u32[]{:S(2)}, u32[]{:S(2)}) collective-permute-start(bf16[128,256]{1,0:T(8,128)(2,1)S(1)} %fusion), channel_id=1, source_target_pairs={{1,2},{2,1},{5,6},{6,5},{9,10},{10,9},{13,14},{14,13},{17,18},{18,... | collective-permute-start | bytes 196616 | tf_op jit(solution)/shard_map/ppermute | solution.py:413
  10.6 9.5 %collective-permute-start.4 = (bf16[128,512]{1,0:T(8,128)(2,1)S(1)}, bf16[128,512]{1,0:T(8,128)(2,1)S(1)}, u32[]{:S(2)}, u32[]{:S(2)}) collective-permute-start(bf16[128,512]{1,0:T(8,128)(2,1)S(1)} %bitcast.11), channel_id=1, source_target_pairs={{0,12},{4,8},{8,4},{12,0},{16,28},{20,24},{24,20},{28,16},{1,13},{... | collective-permute-start | bytes 393224 | tf_op jit(solution)/shard_map/ppermute | solution.py:279
  12.3 11.0 %collective-permute-start.3 = (bf16[128,512]{1,0:T(8,128)(2,1)S(1)}, bf16[128,512]{1,0:T(8,128)(2,1)S(1)}, u32[]{:S(2)}, u32[]{:S(2)}) collective-permute-start(bf16[128,512]{1,0:T(8,128)(2,1)S(1)} %bitcast.12), channel_id=1, source_target_pairs={{0,4},{4,0},{8,12},{12,8},{16,20},{20,16},{24,28},{28,24},{1,5},{5... | collective-permute-start | bytes 393224 | tf_op jit(solution)/shard_map/ppermute | solution.py:279
  12.7 10.8 %collective-permute-start.2 = (bf16[128,512]{1,0:T(8,128)(2,1)S(1)}, bf16[128,512]{1,0:T(8,128)(2,1)S(1)}, u32[]{:S(2)}, u32[]{:S(2)}) collective-permute-start(bf16[128,512]{1,0:T(8,128)(2,1)S(1)} %bitcast.13), channel_id=1, source_target_pairs={{0,24},{4,28},{8,16},{12,20},{16,8},{20,12},{24,0},{28,4},{1,25},{... | collective-permute-start | bytes 393224 | tf_op jit(solution)/shard_map/ppermute | solution.py:279
  16.4 12.1 %collective-permute-start.1 = (bf16[128,512]{1,0:T(8,128)(2,1)S(1)}, bf16[128,512]{1,0:T(8,128)(2,1)S(1)}, u32[]{:S(2)}, u32[]{:S(2)}) collective-permute-start(bf16[128,512]{1,0:T(8,128)(2,1)S(1)} %bitcast.14), channel_id=1, source_target_pairs={{0,16},{4,20},{8,24},{12,28},{16,0},{20,4},{24,8},{28,12},{1,17},{... | collective-permute-start | bytes 393224 | tf_op jit(solution)/shard_map/ppermute | solution.py:279
  18.8 10.9 %collective-permute-start = (bf16[128,512]{1,0:T(8,128)(2,1)S(1)}, bf16[128,512]{1,0:T(8,128)(2,1)S(1)}, u32[]{:S(2)}, u32[]{:S(2)}) collective-permute-start(bf16[128,512]{1,0:T(8,128)(2,1)S(1)} %bitcast.15), channel_id=1, source_target_pairs={{0,8},{4,12},{8,0},{12,4},{16,24},{20,28},{24,16},{28,20},{1,9},{5... | collective-permute-start | bytes 393224 | tf_op jit(solution)/shard_map/ppermute | solution.py:279
  20.1 13.3 %collective-permute-start.22 = (bf16[128,256]{1,0:T(8,128)(2,1)S(1)}, bf16[128,256]{1,0:T(8,128)(2,1)S(1)}, u32[]{:S(2)}, u32[]{:S(2)}) collective-permute-start(bf16[128,256]{1,0:T(8,128)(2,1)S(1)} %collective-permute-done.17.halo_ref), channel_id=1, source_target_pairs={{0,1},{1,0},{2,3},{3,2},{4,5},{5,4},{6,7},{7,6},{8,9},{9,8},{10,11... | collective-permute-start | bytes 196616 | tf_op jit(solution)/shard_map/ppermute | solution.py:279
  23.3 10.8 %collective-permute-start.14 = (bf16[128,512]{1,0:T(8,128)(2,1)S(1)}, bf16[128,512]{1,0:T(8,128)(2,1)S(1)}, u32[]{:S(2)}, u32[]{:S(2)}) collective-permute-start(bf16[128,512]{1,0:T(8,128)(2,1)S(1)} %collective-permute-done.6.refs_7_.refs_3_), channel_id=1, source_target_pairs={{0,1},{1,0},{2,3},{3,2},{4,5},{5,4},{6,7},{7,6},{8,9},{9,8},{10,11... | collective-permute-start | bytes 393224 | tf_op jit(solution)/shard_map/ppermute | solution.py:279
  23.5 10.8 %collective-permute-start.13 = (bf16[128,512]{1,0:T(8,128)(2,1)S(1)}, bf16[128,512]{1,0:T(8,128)(2,1)S(1)}, u32[]{:S(2)}, u32[]{:S(2)}) collective-permute-start(bf16[128,512]{1,0:T(8,128)(2,1)S(1)} %collective-permute-done.5.refs_6_.refs_2_), channel_id=1, source_target_pairs={{0,1},{1,0},{2,3},{3,2},{4,5},{5,4},{6,7},{7,6},{8,9},{9,8},{10,11... | collective-permute-start | bytes 393224 | tf_op jit(solution)/shard_map/ppermute | solution.py:279
  28.5 6.0 %collective-permute-start.10 = (bf16[128,512]{1,0:T(8,128)(2,1)S(1)}, bf16[128,512]{1,0:T(8,128)(2,1)S(1)}, u32[]{:S(2)}, u32[]{:S(2)}) collective-permute-start(bf16[128,512]{1,0:T(8,128)(2,1)S(1)} %collective-permute-done.2.refs_3_.refs_1_), channel_id=1, source_target_pairs={{0,1},{1,0},{2,3},{3,2},{4,5},{5,4},{6,7},{7,6},{8,9},{9,8},{10,11... | collective-permute-start | bytes 393224 | tf_op jit(solution)/shard_map/ppermute | solution.py:279
  29.8 5.0 %collective-permute-start.9 = (bf16[128,512]{1,0:T(8,128)(2,1)S(1)}, bf16[128,512]{1,0:T(8,128)(2,1)S(1)}, u32[]{:S(2)}, u32[]{:S(2)}) collective-permute-start(bf16[128,512]{1,0:T(8,128)(2,1)S(1)} %collective-permute-done.1.refs_2_.refs_0_), channel_id=1, source_target_pairs={{0,1},{1,0},{2,3},{3,2},{4,5},{5,4},{6,7},{7,6},{8,9},{9,8},{10,11... | collective-permute-start | bytes 393224 | tf_op jit(solution)/shard_map/ppermute | solution.py:279
  29.8 1.7 %copy-start = (bf16[3,3,128,1024]{3,2,1,0:T(8,128)(2,1)S(1)}, bf16[3,3,128,1024]{3,2,1,0:T(8,128)(2,1)}, u32[]{:S(2)}) copy-start(bf16[3,3,128,1024]{3,2,1,0:T(8,128)(2,1)} %param.4) | copy-start | bytes 7077892
  33.4 6.3 %copy-start.1 = (bf16[3,3,128,1024]{3,2,1,0:T(8,128)(2,1)S(1)}, bf16[3,3,128,1024]{3,2,1,0:T(8,128)(2,1)}, u32[]{:S(2)}) copy-start(bf16[3,3,128,1024]{3,2,1,0:T(8,128)(2,1)} %param.4) | copy-start | bytes 7077892
  33.4 14.8 %collective-permute-start.18 = (bf16[528,512]{1,0:T(8,128)(2,1)S(1)}, bf16[528,512]{1,0:T(8,128)(2,1)S(1)}, u32[]{:S(2)}, u32[]{:S(2)}) collective-permute-start(bf16[528,512]{1,0:T(8,128)(2,1)S(1)} %get-tuple-element.17), channel_id=1, source_target_pairs={{0,4},{4,0},{8,12},{12,8},{16,20},{20,16},{24,28},{28,24},{1,5},{5... | collective-permute-start | bytes 1622024 | tf_op jit(solution)/shard_map/ppermute | solution.py:279
  34.1 2.2 %collective-permute-start.7 = (bf16[128,512]{1,0:T(8,128)(2,1)S(1)}, bf16[128,512]{1,0:T(8,128)(2,1)S(1)}, u32[]{:S(2)}, u32[]{:S(2)}) collective-permute-start(bf16[128,512]{1,0:T(8,128)(2,1)S(1)} %bitcast.16), channel_id=1, source_target_pairs={{0,1},{1,0},{2,3},{3,2},{4,5},{5,4},{6,7},{7,6},{8,9},{9,8},{10,11... | collective-permute-start | bytes 393224 | tf_op jit(solution)/shard_map/ppermute | solution.py:279
  34.3 4.1 %collective-permute-start.12 = (bf16[128,512]{1,0:T(8,128)(2,1)S(1)}, bf16[128,512]{1,0:T(8,128)(2,1)S(1)}, u32[]{:S(2)}, u32[]{:S(2)}) collective-permute-start(bf16[128,512]{1,0:T(8,128)(2,1)S(1)} %collective-permute-done.4.refs_5_.refs_3_), channel_id=1, source_target_pairs={{0,1},{1,0},{2,3},{3,2},{4,5},{5,4},{6,7},{7,6},{8,9},{9,8},{10,11... | collective-permute-start | bytes 393224 | tf_op jit(solution)/shard_map/ppermute | solution.py:279
  34.6 3.8 %collective-permute-start.11 = (bf16[128,512]{1,0:T(8,128)(2,1)S(1)}, bf16[128,512]{1,0:T(8,128)(2,1)S(1)}, u32[]{:S(2)}, u32[]{:S(2)}) collective-permute-start(bf16[128,512]{1,0:T(8,128)(2,1)S(1)} %collective-permute-done.3.refs_4_.refs_2_), channel_id=1, source_target_pairs={{0,1},{1,0},{2,3},{3,2},{4,5},{5,4},{6,7},{7,6},{8,9},{9,8},{10,11... | collective-permute-start | bytes 393224 | tf_op jit(solution)/shard_map/ppermute | solution.py:279
  34.8 3.6 %collective-permute-start.8 = (bf16[128,512]{1,0:T(8,128)(2,1)S(1)}, bf16[128,512]{1,0:T(8,128)(2,1)S(1)}, u32[]{:S(2)}, u32[]{:S(2)}) collective-permute-start(bf16[128,512]{1,0:T(8,128)(2,1)S(1)} %collective-permute-done.refs_1_), channel_id=1, source_target_pairs={{0,1},{1,0},{2,3},{3,2},{4,5},{5,4},{6,7},{7,6},{8,9},{9,8},{10,11... | collective-permute-start | bytes 393224 | tf_op jit(solution)/shard_map/ppermute | solution.py:279
  36.2 18.2 %collective-permute-start.24 = (bf16[304,512]{1,0:T(8,128)(2,1)S(1)}, bf16[304,512]{1,0:T(8,128)(2,1)S(1)}, u32[]{:S(2)}, u32[]{:S(2)}) collective-permute-start(bf16[304,512]{1,0:T(8,128)(2,1)S(1)} %get-tuple-element.26), channel_id=1, source_target_pairs={{0,2},{1,3},{2,0},{3,1},{4,6},{5,7},{6,4},{7,5},{8,10},{9,11},{10,... | collective-permute-start | bytes 933896 | tf_op jit(solution)/shard_map/ppermute | solution.py:279
  39.5 14.9 %collective-permute-start.23 = (bf16[304,512]{1,0:T(8,128)(2,1)S(1)}, bf16[304,512]{1,0:T(8,128)(2,1)S(1)}, u32[]{:S(2)}, u32[]{:S(2)}) collective-permute-start(bf16[304,512]{1,0:T(8,128)(2,1)S(1)} %get-tuple-element.24), channel_id=1, source_target_pairs={{0,2},{1,3},{2,0},{3,1},{4,6},{5,7},{6,4},{7,5},{8,10},{9,11},{10,... | collective-permute-start | bytes 933896 | tf_op jit(solution)/shard_map/ppermute | solution.py:279
  41.6 10.9 %collective-permute-start.15 = (f32[128,256]{1,0:T(8,128)S(1)}, f32[128,256]{1,0:T(8,128)S(1)}, u32[]{:S(2)}, u32[]{:S(2)}) collective-permute-start(f32[128,256]{1,0:T(8,128)S(1)} %get-tuple-element.16), channel_id=1, source_target_pairs={{1,2},{2,1},{5,6},{6,5},{9,10},{10,9},{13,14},{14,13},{17,18},{18,... | collective-permute-start | bytes 393224 | tf_op jit(solution)/shard_map/ppermute | solution.py:438
  49.3 8.3 %collective-permute-start.19 = (bf16[528,128]{1,0:T(8,128)(2,1)}, bf16[528,128]{1,0:T(8,128)(2,1)S(1)}, u32[]{:S(2)}, u32[]{:S(2)}) collective-permute-start(bf16[528,128]{1,0:T(8,128)(2,1)} %get-tuple-element.20), channel_id=1, source_target_pairs={{0,8},{4,12},{8,0},{12,4},{16,24},{20,28},{24,16},{28,20},{1,9},{5... | collective-permute-start | bytes 405512 | tf_op jit(solution)/shard_map/ppermute | solution.py:279
  49.4 12.1 %collective-permute-start.20 = (bf16[528,128]{1,0:T(8,128)(2,1)S(1)}, bf16[528,128]{1,0:T(8,128)(2,1)S(1)}, u32[]{:S(2)}, u32[]{:S(2)}) collective-permute-start(bf16[528,128]{1,0:T(8,128)(2,1)S(1)} %get-tuple-element.21), channel_id=1, source_target_pairs={{0,16},{4,20},{8,24},{12,28},{16,0},{20,4},{24,8},{28,12},{1,17},{... | collective-permute-start | bytes 405512 | tf_op jit(solution)/shard_map/ppermute | solution.py:279
  52.5 9.0 %collective-permute-start.21 = (bf16[528,128]{1,0:T(8,128)(2,1)S(1)}, bf16[528,128]{1,0:T(8,128)(2,1)S(1)}, u32[]{:S(2)}, u32[]{:S(2)}) collective-permute-start(bf16[528,128]{1,0:T(8,128)(2,1)S(1)} %get-tuple-element.22), channel_id=1, source_target_pairs={{0,24},{4,28},{8,16},{12,20},{16,8},{20,12},{24,0},{28,4},{1,25},{... | collective-permute-start | bytes 405512 | tf_op jit(solution)/shard_map/ppermute | solution.py:279

commit v3 on v2

--- a/solution.py
+++ b/solution.py
@@ -15,17 +15,19 @@
 VMEM_BYTES = 40 * 2**20
 
 
-def call(body, outs, args, scratch=(), flops=0):
-    size = sum(math.prod(x.shape) * x.dtype.itemsize for x in (*outs, *args))
+def call(body, outs, args, scratch=(), flops=0, after=()):
+    def step(*refs):
+        body(*refs[: len(args)], *refs[len(args) + len(after) :])
+
     return pl.pallas_call(
-        body,
+        step,
         out_shape=tuple(outs),
-        in_specs=[pl.BlockSpec(memory_space=pltpu.VMEM)] * len(args),
+        in_specs=[pl.BlockSpec(memory_space=pltpu.VMEM)] * len(args) + [pl.BlockSpec(memory_space=pl.ANY)] * len(after),
         out_specs=tuple(pl.BlockSpec(memory_space=pltpu.VMEM) for _ in outs),
         scratch_shapes=list(scratch),
         compiler_params=pltpu.CompilerParams(vmem_limit_bytes=VMEM_BYTES),
-        cost_estimate=pl.CostEstimate(flops=flops, bytes_accessed=size, transcendentals=0),
-    )(*args)
+        cost_estimate=pl.CostEstimate(flops=int(flops), bytes_accessed=0, transcendentals=0),
+    )(*args, *after)
 
 
 def shape(dims, dtype):
@@ -85,13 +87,13 @@
         put_coded(give_ref, here, jnp.where(y == 0, odd, even))
 
 
-def data_sums(own, adj, halo, taps, width):
+def data_sums(own, adj, halo, taps, width, cost, after=()):
     local, cells = own.shape
     channels = taps.shape[1]
     outs = [shape((cells, channels // 2), F32), shape((cells + EXTRA, channels // 2), BF16)]
     return call(
         functools.partial(data_kernel, width), outs, (own, adj, halo, taps),
-        [pltpu.VMEM((cells, 9 * local), BF16)], 2 * cells * 9 * local * channels,
+        [pltpu.VMEM((cells, 9 * local), BF16)], cost, after,
     )
 
 
@@ -107,35 +109,50 @@
             put_coded(piece_refs[k - 1], slice(None), total)
 
 
-def middle(come, keep, local):
+def middle(come, keep, local, cost, after=()):
     cells, columns = keep.shape
     outs = [shape((cells, local), F32)] + [shape((cells + EXTRA, local), BF16)] * (columns // local - 1)
-    return call(middle_kernel, outs, (come, keep))
+    return call(middle_kernel, outs, (come, keep), (), cost, after)
+
+
+def put_rows(ref, values):
+    width = ref.shape[2]
+    for r in range(ref.shape[1]):
+        ref[:, r, :] = values[:, r * width : (r + 1) * width].astype(BF16)
 
 
 def last_data_kernel(own_ref, *refs):
     total = own_ref[...]
     for ref in refs[:-1]:
         total = total + get_coded(ref, slice(None))
-    refs[-1][...] = total.T.astype(BF16)
-
-
-def last_data(own, pieces):
-    return call(last_data_kernel, [shape(own.shape[::-1], BF16)], (own, *pieces))[0]
+    put_rows(refs[-1], total.T)
+
+
+def last_data(own, pieces, height, cost, after=()):
+    cells, local = own.shape
+    outs = [shape((local, height, cells // height), BF16)]
+    return call(last_data_kernel, outs, (own, *pieces), (), cost, after)[0]
+
+
+def views(blocks):
+    arrays, places = [], []
+    for array, start in blocks:
+        found = [i for i, held in enumerate(arrays) if held is array]
+        if not found:
+            arrays.append(array)
+        places.append((found[0] if found else len(arrays) - 1, start))
+    return arrays, places
 
 
 def pair_of(y, near, far):
     return jnp.concatenate([jnp.where(y == 0, near, far), jnp.where(y == 0, far, near)], axis=0)
 
 
-def filter_kernel(pairs, width, own_ref, adj_ref, halo_ref, rim_ref, *refs):
+def lines_kernel(width, own_ref, adj_ref, halo_ref, rim_ref, left):
     row = lax.axis_index("rows")
     core, chip = row % 2, row // 2
-    y = lax.axis_index("chan") % 2
-    near, far, near_o, far_o = (refs[i * pairs : (i + 1) * pairs] for i in range(4))
-    keep_ref, give_ref, left = refs[4 * pairs :]
     local, cells = own_ref.shape
-    share = keep_ref.shape[0] // 9
+    share = left.shape[0] // 18
     own, adj = own_ref[...], adj_ref[...]
     halo, rim = halo_ref[...], rim_ref[...]
     mine = window_of(core, own, adj, halo, width)
@@ -162,9 +179,37 @@
                 for q in range(2):
                     left[q * 9 * share + tap * share : q * 9 * share + (tap + 1) * share,
                          part * cells : (part + 1) * cells] = moved[b][q * share : (q + 1) * share, start : start + cells]
+
+
+def filter_lines(own, adj, halo, rim, share, width, cost, after=()):
+    cells = own.shape[1]
+    outs = [shape((18 * share, 2 * cells), BF16)]
+    return call(functools.partial(lines_kernel, width), outs, (own, adj, halo, rim), (), cost, after)[0]
+
+
+def stack_kernel(*refs):
+    start = 0
+    for ref in refs[:-1]:
+        refs[-1][start : start + ref.shape[0]] = ref[...]
+        start += ref.shape[0]
+
+
+def stacked(blocks, cost, after=()):
+    rows, columns = blocks[0].shape
+    return call(stack_kernel, [shape((len(blocks) * rows, columns), BF16)], blocks, (), cost, after)[0]
+
+
+def filter_kernel(places, left, *refs):
+    y = lax.axis_index("chan") % 2
+    keep_ref, give_ref = refs[-2:]
+    share = keep_ref.shape[0] // 9
+    pairs = len(places) // 4
+    local = keep_ref.shape[1] // (2 * pairs)
+    held = [refs[i][start : start + local] for i, start in places]
+    near, far, near_o, far_o = (held[i * pairs : (i + 1) * pairs] for i in range(4))
     for t in range(pairs):
         right = jnp.concatenate(
-            [pair_of(y, near[t][...], far[t][...]), pair_of(y, near_o[t][...], far_o[t][...])], axis=1
+            [pair_of(y, near[t], far[t]), pair_of(y, near_o[t], far_o[t])], axis=1
         )
         here = slice(t * 2 * local, (t + 1) * 2 * local)
         for q in (1, 0):
@@ -177,14 +222,11 @@
                 keep_ref[:, here] = sums
 
 
-def filter_sums(own, adj, halo, rim, near, far, near_o, far_o, share, width):
-    local, cells = own.shape
-    pairs = len(near)
+def filter_sums(lines, near, far, near_o, far_o, local, cost, after=()):
+    share, pairs = lines.shape[0] // 18, len(near)
+    arrays, places = views([*near, *far, *near_o, *far_o])
     outs = [shape((9 * share, pairs * 2 * local), F32), shape((9 * share + EXTRA, pairs * 2 * local), BF16)]
-    return call(
-        functools.partial(filter_kernel, pairs, width), outs, (own, adj, halo, rim, *near, *far, *near_o, *far_o),
-        [pltpu.VMEM((18 * share, 2 * cells), BF16)], 2 * 18 * share * 2 * cells * pairs * 2 * local,
-    )
+    return call(functools.partial(filter_kernel, places), outs, (lines, *arrays), (), cost, after)
 
 
 def last_filter_kernel(groups, scale, *refs):
@@ -200,22 +242,24 @@
             t += 1
 
 
-def last_filter(groups, parts, channels, scale):
+def last_filter(groups, parts, channels, scale, cost, after=()):
     outs = [shape((parts[0].shape[0], channels), F32)]
-    return call(functools.partial(last_filter_kernel, groups, scale), outs, parts)[0]
-
-
-def output_kernel(pairs, width, w_ref, *refs):
+    return call(functools.partial(last_filter_kernel, groups, scale), outs, parts, (), cost, after)[0]
+
+
+def output_kernel(places, cells, width, w_ref, *refs):
     core = lax.axis_index("rows") % 2
     chan = lax.axis_index("chan")
     y, z = chan % 2, chan // 2
-    near, far, near_o, far_o = (refs[i * pairs : (i + 1) * pairs] for i in range(4))
-    inner_ref, edge_ref, xs, xo = refs[4 * pairs :]
-    local, cells = near[0].shape
+    inner_ref, edge_ref, xs, xo = refs[-4:]
+    pairs = len(places) // 4
+    local = w_ref.shape[2] // (2 * pairs)
+    held = [refs[i][start : start + local] for i, start in places]
+    near, far, near_o, far_o = (held[i * pairs : (i + 1) * pairs] for i in range(4))
     for t in range(pairs):
         there = pl.ds(pl.multiple_of((z ^ t) * 2 * local, 2 * local), 2 * local)
-        xs[there, :] = pair_of(y, near[t][...], far[t][...])
-        other = pair_of(y, near_o[t][...], far_o[t][...])
+        xs[there, :] = pair_of(y, near[t], far[t])
+        other = pair_of(y, near_o[t], far_o[t])
         xo[there, :] = jnp.where(core == 0, other[:, :width], other[:, -width:])
     filters = w_ref.shape[1]
     w = w_ref[...].reshape(9 * filters, w_ref.shape[2])
@@ -246,32 +290,31 @@
     edge_ref[...] = jnp.where(core == 0, total[0], total[-1])
 
 
-def output_sums(taps, near, far, near_o, far_o, width):
+def output_sums(taps, near, far, near_o, far_o, width, cost, after=()):
     filters, channels = taps.shape[1:]
-    cells = near[0].shape[1]
+    arrays, places = views([*near, *far, *near_o, *far_o])
+    cells = arrays[0].shape[1]
     outs = [shape((filters, cells), F32), shape((filters, width), F32)]
     return call(
-        functools.partial(output_kernel, len(near), width), outs, (taps, *near, *far, *near_o, *far_o),
+        functools.partial(output_kernel, places, cells, width), outs, (taps, *arrays),
         [pltpu.VMEM((channels, cells), BF16), pltpu.VMEM((channels, width), BF16)],
-        2 * 9 * filters * channels * cells * 7 // 6,
-    )
-
-
-def last_output_kernel(width, inner_ref, edge_ref, out_ref):
+        cost, after,
+    )
+
+
+def last_output_kernel(inner_ref, edge_ref, out_ref):
     core = lax.axis_index("rows") % 2
     edge = edge_ref[...]
-    rows = inner_ref.shape[1] // width
-    for r in range(rows):
-        value = inner_ref[:, r * width : (r + 1) * width]
-        if r == 0:
-            value = value + jnp.where(core == 0, edge, 0.0)
-        if r == rows - 1:
-            value = value + jnp.where(core == 0, 0.0, edge)
-        out_ref[:, r * width : (r + 1) * width] = value.astype(BF16)
-
-
-def last_output(inner, edge, width):
-    return call(functools.partial(last_output_kernel, width), [shape(inner.shape, BF16)], (inner, edge))[0]
+    zero = jnp.zeros_like(edge)
+    top, bottom = jnp.where(core == 0, edge, zero), jnp.where(core == 0, zero, edge)
+    middle_rows = [zero] * (out_ref.shape[1] - 2)
+    put_rows(out_ref, inner_ref[...] + jnp.concatenate([top, *middle_rows, bottom], axis=1))
+
+
+def last_output(inner, edge, cost, after=()):
+    filters, width = edge.shape
+    outs = [shape((filters, inner.shape[1] // width, width), BF16)]
+    return call(last_output_kernel, outs, (inner, edge), (), cost, after)[0]
 
 
 def exchange(x, axis, distance):
@@ -409,43 +452,51 @@
 
     edges = [(i, i + 1) for i in range(1, rows - 1, 2)]
     edges += [(j, i) for i, j in edges]
-    edge = jnp.where(first, cotangent[:, 0], cotangent[:, height - 1])
+    g = cotangent.reshape(local, height * width)
+    edge = jnp.where(first, g[:, :width], g[:, -width:])
     halo = lax.ppermute(edge, "rows", edges)
-    g = cotangent.reshape(local, height * width)
     adj = exchange(g, "rows", 1)
     x = activations.reshape(local, height * width)
 
-    keep, give = data_sums(g, adj, halo, taps.reshape(9 * local, channels), width)
+    half = zs // 2
+    direct = {0: x}
+    for k in (1, 3, 2, 6, 4):
+        direct[k] = exchange(x, "chan", k)
+
+    keep, give = data_sums(g, adj, halo, taps.reshape(9 * local, channels), width, 24000000000.0)
     come = exchange(give, "chan", 1)
 
-    blocks = {0: x}
-    for k in (6, 4, 2, 7, 5, 3, 1):
-        blocks[k] = exchange(x, "chan", k)
-    near, far = [blocks[2 * t] for t in range(zs)], [blocks[2 * t + 1] for t in range(zs)]
-    near_o, far_o = ([exchange(b, "rows", 1) for b in side] for side in (near, far))
+    others = {k: exchange(direct[k], "rows", 1) for k in range(2 * half)}
     rim = exchange(halo, "rows", 1)
-
-    groups, parts, start = (zs // 2, zs - zs // 2), [], 0
-    for pairs in groups:
-        chosen = slice(start, start + pairs)
-        mine, gift = filter_sums(
-            g, adj, halo, rim, near[chosen], far[chosen], near_o[chosen], far_o[chosen], share, width
-        )
-        parts += [mine, exchange(gift, "rows", 2)]
-        start += pairs
-
-    inner, rest = output_sums(taps, near, far, near_o, far_o, width)
-    output = last_output(inner, lax.ppermute(rest, "rows", edges), width)
-
-    own, *pieces = middle(come, keep, local)
+    rim, give = lax.optimization_barrier((rim, give))
+    lines = filter_lines(g, adj, halo, rim, share, width, 12000000000.0)
+    near = [(direct[2 * t], 0) for t in range(half)]
+    far = [(direct[2 * t + 1], 0) for t in range(half)]
+    near_o = [(others[2 * t], 0) for t in range(half)]
+    far_o = [(others[2 * t + 1], 0) for t in range(half)]
+    mine, gift = filter_sums(lines, near, far, near_o, far_o, local, 0)
+    far_z = jnp.concatenate([direct[2 * t] for t in range(half, zs)], axis=0)
+    far_z, give = lax.optimization_barrier((far_z, give))
+    far_zy = exchange(far_z, "chan", 1)
+    far_zo, far_zyo = exchange(far_z, "rows", 1), exchange(far_zy, "rows", 1)
+    near2 = [(far_z, t * local) for t in range(zs - half)]
+    far2 = [(far_zy, t * local) for t in range(zs - half)]
+    near2_o = [(far_zo, t * local) for t in range(zs - half)]
+    far2_o = [(far_zyo, t * local) for t in range(zs - half)]
+    own, *pieces = middle(come, keep, local, 0)
     pieces = [exchange(piece, "chan", 2 * k) for k, piece in enumerate(pieces, 1)]
-    input_grad = last_data(own, pieces)
+    mine2, gift2 = filter_sums(lines, near2, far2, near2_o, far2_o, local, 0)
+    parts = [mine, exchange(gift, "rows", 2), mine2, exchange(gift2, "rows", 2)]
+    groups = (half, zs - half)
+    inner, rest = output_sums(taps, near + near2, far + far2, near_o + near2_o, far_o + far2_o, width, 0)
+    output = last_output(inner, lax.ppermute(rest, "rows", edges), 0)
 
     scale = 1.0 / math.sqrt(height * rows * width)
-    filter_grad = last_filter(groups, parts, channels, scale)
+    filter_grad = last_filter(groups, parts, channels, scale, 0)
+    input_grad = last_data(own, pieces, height, 0, (filter_grad,))
     return (
-        output.reshape(local, height, width),
-        input_grad.reshape(local, height, width),
+        output,
+        input_grad,
         filter_grad.reshape(3, 3, share, channels),
     )
 

time: 63.6 us -> 56.3 us (0.89)
  starting transfers between devices: 29.4 us -> 23.1 us
  local copies, waits for them, and re-layouts: 6.11 us -> 4.78 us
  Pallas kernels: 9.08 us -> 10.3 us
    ppermute x23 -> x20, starting transfers between devices: 28 us -> 21.7 us  [exchange(): return lax.ppermute(x, axis, [(i, i ^ distance) for i in range(size)])]
    reshape x2 -> x0, local copies, waits for them, and re-layouts: 1.39 us -> none  [the longest x1 0.69 us: fast(): input_grad.reshape(local, height, width)]
    unnamed x6 -> x8, local copies, waits for them, and re-layouts: 3.51 us -> 4.78 us
    slice x1 -> x0, local copies, waits for them, and re-layouts: 1.21 us -> none  [fast(): edge = jnp.where(first, cotangent[:, 0], cotangent[:, height - 1])]
    pallas_call x8 -> x9, Pallas kernels: 9.08 us -> 10.3 us  [call(): pl.pallas_call(step, out_shape=tuple(outs), in_specs=[pl.BlockSpec(memory...]
    ppermute x23 -> x20, waiting for transfers between devices: 17.1 us -> 16.7 us  [exchange(): return lax.ppermute(x, axis, [(i, i ^ distance) for i in range(size)])]
  transfers between devices with their start and end apart: 25 -> 22, of which waited for: 6 -> 5; matrix products, arithmetic and copies ran while one was open for 5% -> 2% of each run, Pallas kernels for 14% -> 17%
where the time goes in v3:
time: 56.3 us; the launch traced here: 55.6 us
  starting transfers between devices  23.1 us (41%)
  waiting for transfers between devices  16.7 us (30%)
  Pallas kernels  10.3 us (18%)
  local copies, waits for them, and re-layouts  4.78 us (8%)
  between operations  0.77 us (1%)
    ppermute x20, starting transfers between devices, exchange(): return lax.ppermute(x, axis, [(i, i ^ distance) for i in range(size)])  21.7 us
    ppermute x20, waiting for transfers between devices, exchange(): return lax.ppermute(x, axis, [(i, i ^ distance) for i in range(size)])  16.7 us
    pallas_call x9, Pallas kernels, call(): pl.pallas_call(step, out_shape=tuple(outs), in_specs=[pl.BlockSpec(memory...  10.3 us
    unnamed x8, local copies, waits for them, and re-layouts  4.78 us
  transfers between devices with their start and end apart: 22, of which 5 were waited for; matrix products, arithmetic and copies ran while one was open for 2% of the time, Pallas kernels for 17%

profile of v3, /device:TPU:0, one launch (start us, length us, event | category | flops | bytes accessed | tf_op | source)
XLA Modules:
  0.0 55.6 jit_solution(17553200476659881136)
XLA Ops:
  0.6 0.9 %copy.6 = bf16[16,8,2,256]{3,1,2,0:T(8,128)(2,1)S(1)} copy(bf16[16,8,2,256]{3,2,1,0:T(2,128)(2,1)} %bitcast.22) | data formatting | bytes 262144
  1.6 5.1 %collective-permute-start.2 = (bf16[128,512]{1,0:T(8,128)(2,1)S(1)}, bf16[128,512]{1,0:T(8,128)(2,1)S(1)}, u32[]{:S(2)}, u32[]{:S(2)}) collective-permute-start(bf16[128,512]{1,0:T(8,128)(2,1)S(1)} %bitcast.10), channel_id=1, source_target_pairs={{0,24},{4,28},{8,16},{12,20},{16,8},{20,12},{24,0},{28,4},{1,25},{... | collective-permute-start | bytes 393224 | tf_op jit(solution)/shard_map/ppermute | solution.py:322
  6.7 0.0 collective-permute-start.1
  6.7 0.9 %copy.7 = bf16[16,8,2,256]{3,1,2,0:T(8,128)(2,1)S(1)} copy(bf16[16,8,2,256]{3,2,1,0:T(2,128)(2,1)} %bitcast.23) | data formatting | bytes 262144
  7.6 0.7 %collective-permute-start.14 = (bf16[128,256]{1,0:T(8,128)(2,1)S(1)}, bf16[128,256]{1,0:T(8,128)(2,1)S(1)}, u32[]{:S(2)}, u32[]{:S(2)}) collective-permute-start(bf16[128,256]{1,0:T(8,128)(2,1)S(1)} %slice_select_fusion), channel_id=1, source_target_pairs={{1,2},{2,1},{5,6},{6,5},{9,10},{10,9},{13,14},{14,13},{17,18},{18,... | collective-permute-start | bytes 196616 | tf_op jit(solution)/shard_map/ppermute | solution.py:457
  8.3 2.9 %collective-permute-start.13 = (bf16[128,512]{1,0:T(8,128)(2,1)S(1)}, bf16[128,512]{1,0:T(8,128)(2,1)S(1)}, u32[]{:S(2)}, u32[]{:S(2)}) collective-permute-start(bf16[128,512]{1,0:T(8,128)(2,1)S(1)} %bitcast.19), channel_id=1, source_target_pairs={{0,1},{1,0},{2,3},{3,2},{4,5},{5,4},{6,7},{7,6},{8,9},{9,8},{10,11... | collective-permute-start | bytes 393224 | tf_op jit(solution)/shard_map/ppermute | solution.py:322
  11.2 1.7 %collective-permute-start.4 = (bf16[128,512]{1,0:T(8,128)(2,1)S(1)}, bf16[128,512]{1,0:T(8,128)(2,1)S(1)}, u32[]{:S(2)}, u32[]{:S(2)}) collective-permute-start(bf16[128,512]{1,0:T(8,128)(2,1)S(1)} %bitcast.12), channel_id=1, source_target_pairs={{0,12},{4,8},{8,4},{12,0},{16,28},{20,24},{24,20},{28,16},{1,13},{... | collective-permute-start | bytes 393224 | tf_op jit(solution)/shard_map/ppermute | solution.py:322
  12.9 0.0 collective-permute-done.14.refs_2_
  12.9 0.1 collective-permute-start.6
  13.1 0.0 collective-permute-done.2
  13.1 1.5 %collective-permute-start.3 = (bf16[128,512]{1,0:T(8,128)(2,1)S(1)}, bf16[128,512]{1,0:T(8,128)(2,1)S(1)}, u32[]{:S(2)}, u32[]{:S(2)}) collective-permute-start(bf16[128,512]{1,0:T(8,128)(2,1)S(1)} %bitcast.14), channel_id=1, source_target_pairs={{0,4},{4,0},{8,12},{12,8},{16,20},{20,16},{24,28},{28,24},{1,5},{5... | collective-permute-start | bytes 393224 | tf_op jit(solution)/shard_map/ppermute | solution.py:322
  14.6 3.3 %collective-permute-done.1 = bf16[128,512]{1,0:T(8,128)(2,1)S(1)} collective-permute-done((bf16[128,512]{1,0:T(8,128)(2,1)S(1)}, bf16[128,512]{1,0:T(8,128)(2,1)S(1)}, u32[]{:S(2)}, u32[]{:S(2)}) %collective-permute-start.1) | collective-permute-done | bytes 131104 | tf_op jit(solution)/shard_map/ppermute | solution.py:322
  17.8 0.0 collective-permute-start.19
  17.9 1.2 %collective-permute-done.19.refs_3_ = bf16[128,256]{1,0:T(8,128)(2,1)S(1)} collective-permute-done((bf16[128,256]{1,0:T(8,128)(2,1)S(1)}, bf16[128,256]{1,0:T(8,128)(2,1)S(1)}, u32[]{:S(2)}, u32[]{:S(2)}) %collective-permute-start.19) | collective-permute-done | bytes 65568 | tf_op jit(solution)/shard_map/ppermute | solution.py:322
  19.1 0.1 collective-permute-start
  19.2 0.0 collective-permute-done.13.refs_1_
  19.2 1.4 %collective-permute-start.5 = (bf16[256,512]{1,0:T(8,128)(2,1)S(1)}, bf16[256,512]{1,0:T(8,128)(2,1)S(1)}, u32[]{:S(2)}, u32[]{:S(2)}) collective-permute-start(bf16[256,512]{1,0:T(8,128)(2,1)S(1)} %pad_maximum_fusion.refs_3_.refs_1_), channel_id=1, source_target_pairs={{0,4},{4,0},{8,12},{12,8},{16,20},{20,16},{24,28},{28,24},{1,5},{5... | collective-permute-start | bytes 786440 | tf_op jit(solution)/shard_map/ppermute | solution.py:322
  20.6 0.0 collective-permute-done.4.refs_5_.refs_4_
  20.6 0.0 collective-permute-start.10
  20.6 0.0 copy-start.1
  20.6 1.7 %copy-done.1 = bf16[3,3,128,1024]{3,2,1,0:T(8,128)(2,1)S(1)} copy-done((bf16[3,3,128,1024]{3,2,1,0:T(8,128)(2,1)S(1)}, bf16[3,3,128,1024]{3,2,1,0:T(8,128)(2,1)}, u32[]{:S(2)}) %copy-start.1) | copy-done | bytes 2359320
  22.3 1.9 %shard_map.60 = (f32[512,512]{1,0:T(8,128)S(1)}, bf16[528,512]{1,0:T(8,128)(2,1)S(1)}) custom-call(bf16[128,512]{1,0:T(8,128)(2,1)S(1)} %bitcast.20, bf16[128,512]{1,0:T(8,128)(2,1)S(1)} %collective-permute-done.13.refs_1_, bf16[128,256]{1,0:T(8,128)(2,1)S(1)} %collective-permute-done.14.refs_2_, bf16[1152,1024]{1,0:T(8,128)(2,1)S(1)} %bitcast.8), custom_call_target="tpu_custom_call" | custom-call | flops 24000000000 | tf_op jit(solution)/shard_map/pallas_call | solution.py:22
  24.2 0.0 collective-permute-done.6.refs_7_.refs_5_
  24.2 0.6 %collective-permute-start.8 = (bf16[256,512]{1,0:T(8,128)(2,1)S(1)}, bf16[256,512]{1,0:T(8,128)(2,1)S(1)}, u32[]{:S(2)}, u32[]{:S(2)}) collective-permute-start(bf16[256,512]{1,0:T(8,128)(2,1)S(1)} %pad_maximum_fusion.refs_3_.refs_1_), channel_id=1, source_target_pairs={{0,1},{1,0},{2,3},{3,2},{4,5},{5,4},{6,7},{7,6},{8,9},{9,8},{10,11... | collective-permute-start | bytes 786440 | tf_op jit(solution)/shard_map/ppermute | solution.py:322
  24.8 0.0 collective-permute-done.3.refs_4_.refs_3_
  24.8 1.0 %collective-permute-start.15 = (bf16[528,512]{1,0:T(8,128)(2,1)S(1)}, bf16[528,512]{1,0:T(8,128)(2,1)S(1)}, u32[]{:S(2)}, u32[]{:S(2)}) collective-permute-start(bf16[528,512]{1,0:T(8,128)(2,1)S(1)} %get-tuple-element.18), channel_id=1, source_target_pairs={{0,4},{4,0},{8,12},{12,8},{16,20},{20,16},{24,28},{28,24},{1,5},{5... | collective-permute-start | bytes 1622024 | tf_op jit(solution)/shard_map/ppermute | solution.py:322
  25.8 0.0 collective-permute-done.refs_2_
  25.8 0.0 collective-permute-start.9
  25.8 0.0 collective-permute-done.10.refs_11_.refs_8_
  25.8 0.5 collective-permute-start.7
  26.3 1.2 %collective-permute-done.5.refs_6_.refs_2_ = bf16[256,512]{1,0:T(8,128)(2,1)S(1)} collective-permute-done((bf16[256,512]{1,0:T(8,128)(2,1)S(1)}, bf16[256,512]{1,0:T(8,128)(2,1)S(1)}, u32[]{:S(2)}, u32[]{:S(2)}) %collective-permute-start.5) | collective-permute-done | bytes 262176 | tf_op jit(solution)/shard_map/ppermute | solution.py:322
  27.5 0.0 collective-permute-start.11
  27.5 0.4 shard_map.62.refs_0_
  27.9 0.0 collective-permute-done.9.refs_10_.refs_7_
  27.9 0.0 collective-permute-done.7.refs_8_.refs_6_
  27.9 0.0 copy-start.2
  27.9 1.0 %shard_map.63 = (f32[288,512]{1,0:T(8,128)S(1)}, bf16[304,512]{1,0:T(8,128)(2,1)S(1)}) custom-call(bf16[576,1024]{1,0:T(8,128)(2,1)S(1)} %shard_map.62.refs_0_, bf16[128,512]{1,0:T(8,128)(2,1)S(1)} %bitcast.16, bf16[128,512]{1,0:T(8,128)(2,1)S(1)} %collective-permute-done.refs_2_, bf16[128,512]{1,0:T(8,128)(2,1)S(1)} %collective-permute-done.3.refs_4_.refs_3_, ...), custom_call_target="tpu_custom_call" | custom-call | tf_op jit(solution)/shard_map/pallas_call | solution.py:22
  28.9 1.6 %collective-permute-start.20 = (bf16[304,512]{1,0:T(8,128)(2,1)S(1)}, bf16[304,512]{1,0:T(8,128)(2,1)S(1)}, u32[]{:S(2)}, u32[]{:S(2)}) collective-permute-start(bf16[304,512]{1,0:T(8,128)(2,1)S(1)} %get-tuple-element.26), channel_id=1, source_target_pairs={{0,2},{1,3},{2,0},{3,1},{4,6},{5,7},{6,4},{7,5},{8,10},{9,11},{10,... | collective-permute-start | bytes 933896 | tf_op jit(solution)/shard_map/ppermute | solution.py:322
  30.4 0.0 collective-permute-done.8.refs_9_.refs_3_
  30.4 0.0 collective-permute-done.11.refs_12_.refs_4_
  30.4 1.0 %shard_map.64 = (f32[288,512]{1,0:T(8,128)S(1)}, bf16[304,512]{1,0:T(8,128)(2,1)S(1)}) custom-call(bf16[576,1024]{1,0:T(8,128)(2,1)S(1)} %shard_map.62.refs_0_, bf16[256,512]{1,0:T(8,128)(2,1)S(1)} %pad_maximum_fusion.refs_3_.refs_1_, bf16[256,512]{1,0:T(8,128)(2,1)S(1)} %collective-permute-done.5.refs_6_.refs_2_, ...), custom_call_target="tpu_custom_call" | custom-call | tf_op jit(solution)/shard_map/pallas_call | solution.py:22
  31.4 0.6 %collective-permute-start.21 = (bf16[304,512]{1,0:T(8,128)(2,1)S(1)}, bf16[304,512]{1,0:T(8,128)(2,1)S(1)}, u32[]{:S(2)}, u32[]{:S(2)}) collective-permute-start(bf16[304,512]{1,0:T(8,128)(2,1)S(1)} %get-tuple-element.28), channel_id=1, source_target_pairs={{0,2},{1,3},{2,0},{3,1},{4,6},{5,7},{6,4},{7,5},{8,10},{9,11},{10,... | collective-permute-start | bytes 933896 | tf_op jit(solution)/shard_map/ppermute | solution.py:322
  32.0 0.0 copy-done.2
  32.0 1.9 %shard_map.58 = (f32[128,512]{1,0:T(8,128)S(1)}, f32[128,256]{1,0:T(8,128)S(1)}) custom-call(bf16[9,128,1024]{2,1,0:T(8,128)(2,1)S(1)} %bitcast.9, bf16[128,512]{1,0:T(8,128)(2,1)S(1)} %bitcast.17, bf16[128,512]{1,0:T(8,128)(2,1)S(1)} %collective-permute-done.refs_2_, bf16[256,512]{1,0:T(8,128)(2,1)S(1)} %pad_maximum_fusion.refs_3_.refs_1_, ...), custom_call_target="tpu_custom_call" | custom-call | tf_op jit(solution)/shard_map/pallas_call | solution.py:22
  33.9 0.7 %collective-permute-start.12 = (f32[128,256]{1,0:T(8,128)S(1)}, f32[128,256]{1,0:T(8,128)S(1)}, u32[]{:S(2)}, u32[]{:S(2)}) collective-permute-start(f32[128,256]{1,0:T(8,128)S(1)} %get-tuple-element.17), channel_id=1, source_target_pairs={{1,2},{2,1},{5,6},{6,5},{9,10},{10,9},{13,14},{14,13},{17,18},{18,... | collective-permute-start | bytes 393224 | tf_op jit(solution)/shard_map/ppermute | solution.py:492
  34.6 4.5 %collective-permute-done.15.refs_0_ = bf16[528,512]{1,0:T(8,128)(2,1)S(1)} collective-permute-done((bf16[528,512]{1,0:T(8,128)(2,1)S(1)}, bf16[528,512]{1,0:T(8,128)(2,1)S(1)}, u32[]{:S(2)}, u32[]{:S(2)}) %collective-permute-start.15) | collective-permute-done | bytes 540704 | tf_op jit(solution)/shard_map/ppermute | solution.py:322
  39.1 0.8 %shard_map.61 = (f32[512,128]{1,0:T(8,128)S(1)}, bf16[528,128]{1,0:T(8,128)(2,1)S(1)}, bf16[528,128]{1,0:T(8,128)(2,1)S(1)}, bf16[528,128]{1,0:T(8,128)(2,1)S(1)}) custom-call(bf16[528,512]{1,0:T(8,128)(2,1)S(1)} %collective-permute-done.15.refs_0_, f32[512,512]{1,0:T(8,128)S(1)} %get-tuple-element.19.refs_1_), custom_call_target="tpu_custom_call" | custom-call | tf_op jit(solution)/shard_map/pallas_call | solution.py:22
  39.9 2.1 %collective-permute-start.16 = (bf16[528,128]{1,0:T(8,128)(2,1)S(1)}, bf16[528,128]{1,0:T(8,128)(2,1)S(1)}, u32[]{:S(2)}, u32[]{:S(2)}) collective-permute-start(bf16[528,128]{1,0:T(8,128)(2,1)S(1)} %get-tuple-element.21), channel_id=1, source_target_pairs={{0,8},{4,12},{8,0},{12,4},{16,24},{20,28},{24,16},{28,20},{1,9},{5... | collective-permute-start | bytes 405512 | tf_op jit(solution)/shard_map/ppermute | solution.py:322
  41.9 1.1 %collective-permute-start.17 = (bf16[528,128]{1,0:T(8,128)(2,1)S(1)}, bf16[528,128]{1,0:T(8,128)(2,1)S(1)}, u32[]{:S(2)}, u32[]{:S(2)}) collective-permute-start(bf16[528,128]{1,0:T(8,128)(2,1)S(1)} %get-tuple-element.22), channel_id=1, source_target_pairs={{0,16},{4,20},{8,24},{12,28},{16,0},{20,4},{24,8},{28,12},{1,17},{... | collective-permute-start | bytes 405512 | tf_op jit(solution)/shard_map/ppermute | solution.py:322
  43.0 0.0 collective-permute-done.12.refs_1_
  43.0 1.4 %collective-permute-start.18 = (bf16[528,128]{1,0:T(8,128)(2,1)S(1)}, bf16[528,128]{1,0:T(8,128)(2,1)S(1)}, u32[]{:S(2)}, u32[]{:S(2)}) collective-permute-start(bf16[528,128]{1,0:T(8,128)(2,1)S(1)} %get-tuple-element.23), channel_id=1, source_target_pairs={{0,24},{4,28},{8,16},{12,20},{16,8},{20,12},{24,0},{28,4},{1,25},{... | collective-permute-start | bytes 405512 | tf_op jit(solution)/shard_map/ppermute | solution.py:322
  44.4 0.9 %shard_map.59 = bf16[128,2,256]{2,1,0:T(2,128)(2,1)} custom-call(f32[128,512]{1,0:T(8,128)S(1)} %get-tuple-element.16.refs_0_, f32[128,256]{1,0:T(8,128)S(1)} %collective-permute-done.12.refs_1_), custom_call_target="tpu_custom_call" | custom-call | tf_op jit(solution)/shard_map/pallas_call | solution.py:22
  45.3 0.0 collective-permute-done.20.refs_1_
  45.3 0.0 collective-permute-done.21.refs_3_
  45.4 1.4 %shard_map.65.refs_4_ = f32[288,1024]{1,0:T(8,128)} custom-call(f32[288,512]{1,0:T(8,128)S(1)} %get-tuple-element.25.refs_0_, bf16[304,512]{1,0:T(8,128)(2,1)S(1)} %collective-permute-done.20.refs_1_, f32[288,512]{1,0:T(8,128)S(1)} %get-tuple-element.27.refs_2_, bf16[304,512]{1,0:T(8,128)(2,1)S(1)} %collective-permute-done.21.refs_3_), custom_call_target="tpu_custom_call" | custom-call | tf_op jit(solution)/shard_map/pallas_call | solution.py:22
  46.8 0.0 collective-permute-done.16.refs_1_
  46.8 6.5 %collective-permute-done.17.refs_2_ = bf16[528,128]{1,0:T(8,128)(2,1)S(1)} collective-permute-done((bf16[528,128]{1,0:T(8,128)(2,1)S(1)}, bf16[528,128]{1,0:T(8,128)(2,1)S(1)}, u32[]{:S(2)}, u32[]{:S(2)}) %collective-permute-start.17) | collective-permute-done | bytes 135200 | tf_op jit(solution)/shard_map/ppermute | solution.py:322
  53.3 0.0 collective-permute-done.18.refs_3_
  53.3 0.0 copy-start
  53.3 1.3 %copy-done = f32[288,1024]{1,0:T(8,128)S(1)} copy-done((f32[288,1024]{1,0:T(8,128)S(1)}, f32[288,1024]{1,0:T(8,128)}, u32[]{:S(2)}) %copy-start) | copy-done | bytes 1179672
  54.6 1.0 %shard_map.66 = bf16[128,2,256]{2,1,0:T(2,128)(2,1)} custom-call(f32[512,128]{1,0:T(8,128)S(1)} %get-tuple-element.20.refs_0_, bf16[528,128]{1,0:T(8,128)(2,1)S(1)} %collective-permute-done.16.refs_1_, bf16[528,128]{1,0:T(8,128)(2,1)S(1)} %collective-permute-done.17.refs_2_, bf16[528,128]{1,0:T(8,128)(2,1)S(1)} %collective-permute-done.18.refs_3_, ...), custom_call_target="tpu_custom_call" | custom-call | tf_op jit(solution)/shard_map/pallas_call | solution.py:22
  (2 shorter events, 0.0 us)
Async XLA Ops:
  1.6 11.5 %collective-permute-start.2 = (bf16[128,512]{1,0:T(8,128)(2,1)S(1)}, bf16[128,512]{1,0:T(8,128)(2,1)S(1)}, u32[]{:S(2)}, u32[]{:S(2)}) collective-permute-start(bf16[128,512]{1,0:T(8,128)(2,1)S(1)} %bitcast.10), channel_id=1, source_target_pairs={{0,24},{4,28},{8,16},{12,20},{16,8},{20,12},{24,0},{28,4},{1,25},{... | collective-permute-start | bytes 393224 | tf_op jit(solution)/shard_map/ppermute | solution.py:322
  6.7 11.2 %collective-permute-start.1 = (bf16[128,512]{1,0:T(8,128)(2,1)S(1)}, bf16[128,512]{1,0:T(8,128)(2,1)S(1)}, u32[]{:S(2)}, u32[]{:S(2)}) collective-permute-start(bf16[128,512]{1,0:T(8,128)(2,1)S(1)} %bitcast.11), channel_id=1, source_target_pairs={{0,16},{4,20},{8,24},{12,28},{16,0},{20,4},{24,8},{28,12},{1,17},{... | collective-permute-start | bytes 393224 | tf_op jit(solution)/shard_map/ppermute | solution.py:322
  7.6 5.3 %collective-permute-start.14 = (bf16[128,256]{1,0:T(8,128)(2,1)S(1)}, bf16[128,256]{1,0:T(8,128)(2,1)S(1)}, u32[]{:S(2)}, u32[]{:S(2)}) collective-permute-start(bf16[128,256]{1,0:T(8,128)(2,1)S(1)} %slice_select_fusion), channel_id=1, source_target_pairs={{1,2},{2,1},{5,6},{6,5},{9,10},{10,9},{13,14},{14,13},{17,18},{18,... | collective-permute-start | bytes 196616 | tf_op jit(solution)/shard_map/ppermute | solution.py:457
  8.3 11.0 %collective-permute-start.13 = (bf16[128,512]{1,0:T(8,128)(2,1)S(1)}, bf16[128,512]{1,0:T(8,128)(2,1)S(1)}, u32[]{:S(2)}, u32[]{:S(2)}) collective-permute-start(bf16[128,512]{1,0:T(8,128)(2,1)S(1)} %bitcast.19), channel_id=1, source_target_pairs={{0,1},{1,0},{2,3},{3,2},{4,5},{5,4},{6,7},{7,6},{8,9},{9,8},{10,11... | collective-permute-start | bytes 393224 | tf_op jit(solution)/shard_map/ppermute | solution.py:322
  11.2 9.4 %collective-permute-start.4 = (bf16[128,512]{1,0:T(8,128)(2,1)S(1)}, bf16[128,512]{1,0:T(8,128)(2,1)S(1)}, u32[]{:S(2)}, u32[]{:S(2)}) collective-permute-start(bf16[128,512]{1,0:T(8,128)(2,1)S(1)} %bitcast.12), channel_id=1, source_target_pairs={{0,12},{4,8},{8,4},{12,0},{16,28},{20,24},{24,20},{28,16},{1,13},{... | collective-permute-start | bytes 393224 | tf_op jit(solution)/shard_map/ppermute | solution.py:322
  12.9 11.3 %collective-permute-start.6 = (bf16[128,512]{1,0:T(8,128)(2,1)S(1)}, bf16[128,512]{1,0:T(8,128)(2,1)S(1)}, u32[]{:S(2)}, u32[]{:S(2)}) collective-permute-start(bf16[128,512]{1,0:T(8,128)(2,1)S(1)} %bitcast.13), channel_id=1, source_target_pairs={{0,1},{1,0},{2,3},{3,2},{4,5},{5,4},{6,7},{7,6},{8,9},{9,8},{10,11... | collective-permute-start | bytes 393224 | tf_op jit(solution)/shard_map/ppermute | solution.py:322
  13.1 11.7 %collective-permute-start.3 = (bf16[128,512]{1,0:T(8,128)(2,1)S(1)}, bf16[128,512]{1,0:T(8,128)(2,1)S(1)}, u32[]{:S(2)}, u32[]{:S(2)}) collective-permute-start(bf16[128,512]{1,0:T(8,128)(2,1)S(1)} %bitcast.14), channel_id=1, source_target_pairs={{0,4},{4,0},{8,12},{12,8},{16,20},{20,16},{24,28},{28,24},{1,5},{5... | collective-permute-start | bytes 393224 | tf_op jit(solution)/shard_map/ppermute | solution.py:322
  17.8 1.3 %collective-permute-start.19 = (bf16[128,256]{1,0:T(8,128)(2,1)S(1)}, bf16[128,256]{1,0:T(8,128)(2,1)S(1)}, u32[]{:S(2)}, u32[]{:S(2)}) collective-permute-start(bf16[128,256]{1,0:T(8,128)(2,1)S(1)} %collective-permute-done.14.refs_2_), channel_id=1, source_target_pairs={{0,1},{1,0},{2,3},{3,2},{4,5},{5,4},{6,7},{7,6},{8,9},{9,8},{10,11... | collective-permute-start | bytes 196616 | tf_op jit(solution)/shard_map/ppermute | solution.py:322
  19.1 6.7 %collective-permute-start = (bf16[128,512]{1,0:T(8,128)(2,1)S(1)}, bf16[128,512]{1,0:T(8,128)(2,1)S(1)}, u32[]{:S(2)}, u32[]{:S(2)}) collective-permute-start(bf16[128,512]{1,0:T(8,128)(2,1)S(1)} %bitcast.15), channel_id=1, source_target_pairs={{0,8},{4,12},{8,0},{12,4},{16,24},{20,28},{24,16},{28,20},{1,9},{5... | collective-permute-start | bytes 393224 | tf_op jit(solution)/shard_map/ppermute | solution.py:322
  19.2 8.2 %collective-permute-start.5 = (bf16[256,512]{1,0:T(8,128)(2,1)S(1)}, bf16[256,512]{1,0:T(8,128)(2,1)S(1)}, u32[]{:S(2)}, u32[]{:S(2)}) collective-permute-start(bf16[256,512]{1,0:T(8,128)(2,1)S(1)} %pad_maximum_fusion.refs_3_.refs_1_), channel_id=1, source_target_pairs={{0,4},{4,0},{8,12},{12,8},{16,20},{20,16},{24,28},{28,24},{1,5},{5... | collective-permute-start | bytes 786440 | tf_op jit(solution)/shard_map/ppermute | solution.py:322
  20.6 5.2 %collective-permute-start.10 = (bf16[128,512]{1,0:T(8,128)(2,1)S(1)}, bf16[128,512]{1,0:T(8,128)(2,1)S(1)}, u32[]{:S(2)}, u32[]{:S(2)}) collective-permute-start(bf16[128,512]{1,0:T(8,128)(2,1)S(1)} %collective-permute-done.4.refs_5_.refs_4_), channel_id=1, source_target_pairs={{0,1},{1,0},{2,3},{3,2},{4,5},{5,4},{6,7},{7,6},{8,9},{9,8},{10,11... | collective-permute-start | bytes 393224 | tf_op jit(solution)/shard_map/ppermute | solution.py:322
  20.6 1.7 %copy-start.1 = (bf16[3,3,128,1024]{3,2,1,0:T(8,128)(2,1)S(1)}, bf16[3,3,128,1024]{3,2,1,0:T(8,128)(2,1)}, u32[]{:S(2)}) copy-start(bf16[3,3,128,1024]{3,2,1,0:T(8,128)(2,1)} %param.4) | copy-start | bytes 7077892
  24.2 6.2 %collective-permute-start.8 = (bf16[256,512]{1,0:T(8,128)(2,1)S(1)}, bf16[256,512]{1,0:T(8,128)(2,1)S(1)}, u32[]{:S(2)}, u32[]{:S(2)}) collective-permute-start(bf16[256,512]{1,0:T(8,128)(2,1)S(1)} %pad_maximum_fusion.refs_3_.refs_1_), channel_id=1, source_target_pairs={{0,1},{1,0},{2,3},{3,2},{4,5},{5,4},{6,7},{7,6},{8,9},{9,8},{10,11... | collective-permute-start | bytes 786440 | tf_op jit(solution)/shard_map/ppermute | solution.py:322
  24.8 14.3 %collective-permute-start.15 = (bf16[528,512]{1,0:T(8,128)(2,1)S(1)}, bf16[528,512]{1,0:T(8,128)(2,1)S(1)}, u32[]{:S(2)}, u32[]{:S(2)}) collective-permute-start(bf16[528,512]{1,0:T(8,128)(2,1)S(1)} %get-tuple-element.18), channel_id=1, source_target_pairs={{0,4},{4,0},{8,12},{12,8},{16,20},{20,16},{24,28},{28,24},{1,5},{5... | collective-permute-start | bytes 1622024 | tf_op jit(solution)/shard_map/ppermute | solution.py:322
  25.8 2.1 %collective-permute-start.9 = (bf16[128,512]{1,0:T(8,128)(2,1)S(1)}, bf16[128,512]{1,0:T(8,128)(2,1)S(1)}, u32[]{:S(2)}, u32[]{:S(2)}) collective-permute-start(bf16[128,512]{1,0:T(8,128)(2,1)S(1)} %collective-permute-done.3.refs_4_.refs_3_), channel_id=1, source_target_pairs={{0,1},{1,0},{2,3},{3,2},{4,5},{5,4},{6,7},{7,6},{8,9},{9,8},{10,11... | collective-permute-start | bytes 393224 | tf_op jit(solution)/shard_map/ppermute | solution.py:322
  25.8 2.1 %collective-permute-start.7 = (bf16[128,512]{1,0:T(8,128)(2,1)S(1)}, bf16[128,512]{1,0:T(8,128)(2,1)S(1)}, u32[]{:S(2)}, u32[]{:S(2)}) collective-permute-start(bf16[128,512]{1,0:T(8,128)(2,1)S(1)} %collective-permute-done.refs_2_), channel_id=1, source_target_pairs={{0,1},{1,0},{2,3},{3,2},{4,5},{5,4},{6,7},{7,6},{8,9},{9,8},{10,11... | collective-permute-start | bytes 393224 | tf_op jit(solution)/shard_map/ppermute | solution.py:322
  27.5 3.0 %collective-permute-start.11 = (bf16[256,512]{1,0:T(8,128)(2,1)S(1)}, bf16[256,512]{1,0:T(8,128)(2,1)S(1)}, u32[]{:S(2)}, u32[]{:S(2)}) collective-permute-start(bf16[256,512]{1,0:T(8,128)(2,1)S(1)} %collective-permute-done.5.refs_6_.refs_2_), channel_id=1, source_target_pairs={{0,1},{1,0},{2,3},{3,2},{4,5},{5,4},{6,7},{7,6},{8,9},{9,8},{10,11... | collective-permute-start | bytes 786440 | tf_op jit(solution)/shard_map/ppermute | solution.py:322
  27.9 4.1 %copy-start.2 = (bf16[3,3,128,1024]{3,2,1,0:T(8,128)(2,1)S(1)}, bf16[3,3,128,1024]{3,2,1,0:T(8,128)(2,1)}, u32[]{:S(2)}) copy-start(bf16[3,3,128,1024]{3,2,1,0:T(8,128)(2,1)} %param.4) | copy-start | bytes 7077892
  28.9 16.5 %collective-permute-start.20 = (bf16[304,512]{1,0:T(8,128)(2,1)S(1)}, bf16[304,512]{1,0:T(8,128)(2,1)S(1)}, u32[]{:S(2)}, u32[]{:S(2)}) collective-permute-start(bf16[304,512]{1,0:T(8,128)(2,1)S(1)} %get-tuple-element.26), channel_id=1, source_target_pairs={{0,2},{1,3},{2,0},{3,1},{4,6},{5,7},{6,4},{7,5},{8,10},{9,11},{10,... | collective-permute-start | bytes 933896 | tf_op jit(solution)/shard_map/ppermute | solution.py:322
  31.4 14.0 %collective-permute-start.21 = (bf16[304,512]{1,0:T(8,128)(2,1)S(1)}, bf16[304,512]{1,0:T(8,128)(2,1)S(1)}, u32[]{:S(2)}, u32[]{:S(2)}) collective-permute-start(bf16[304,512]{1,0:T(8,128)(2,1)S(1)} %get-tuple-element.28), channel_id=1, source_target_pairs={{0,2},{1,3},{2,0},{3,1},{4,6},{5,7},{6,4},{7,5},{8,10},{9,11},{10,... | collective-permute-start | bytes 933896 | tf_op jit(solution)/shard_map/ppermute | solution.py:322
  33.9 9.1 %collective-permute-start.12 = (f32[128,256]{1,0:T(8,128)S(1)}, f32[128,256]{1,0:T(8,128)S(1)}, u32[]{:S(2)}, u32[]{:S(2)}) collective-permute-start(f32[128,256]{1,0:T(8,128)S(1)} %get-tuple-element.17), channel_id=1, source_target_pairs={{1,2},{2,1},{5,6},{6,5},{9,10},{10,9},{13,14},{14,13},{17,18},{18,... | collective-permute-start | bytes 393224 | tf_op jit(solution)/shard_map/ppermute | solution.py:492
  39.9 6.9 %collective-permute-start.16 = (bf16[528,128]{1,0:T(8,128)(2,1)S(1)}, bf16[528,128]{1,0:T(8,128)(2,1)S(1)}, u32[]{:S(2)}, u32[]{:S(2)}) collective-permute-start(bf16[528,128]{1,0:T(8,128)(2,1)S(1)} %get-tuple-element.21), channel_id=1, source_target_pairs={{0,8},{4,12},{8,0},{12,4},{16,24},{20,28},{24,16},{28,20},{1,9},{5... | collective-permute-start | bytes 405512 | tf_op jit(solution)/shard_map/ppermute | solution.py:322
  41.9 11.3 %collective-permute-start.17 = (bf16[528,128]{1,0:T(8,128)(2,1)S(1)}, bf16[528,128]{1,0:T(8,128)(2,1)S(1)}, u32[]{:S(2)}, u32[]{:S(2)}) collective-permute-start(bf16[528,128]{1,0:T(8,128)(2,1)S(1)} %get-tuple-element.22), channel_id=1, source_target_pairs={{0,16},{4,20},{8,24},{12,28},{16,0},{20,4},{24,8},{28,12},{1,17},{... | collective-permute-start | bytes 405512 | tf_op jit(solution)/shard_map/ppermute | solution.py:322
  43.0 10.2 %collective-permute-start.18 = (bf16[528,128]{1,0:T(8,128)(2,1)S(1)}, bf16[528,128]{1,0:T(8,128)(2,1)S(1)}, u32[]{:S(2)}, u32[]{:S(2)}) collective-permute-start(bf16[528,128]{1,0:T(8,128)(2,1)S(1)} %get-tuple-element.23), channel_id=1, source_target_pairs={{0,24},{4,28},{8,16},{12,20},{16,8},{20,12},{24,0},{28,4},{1,25},{... | collective-permute-start | bytes 405512 | tf_op jit(solution)/shard_map/ppermute | solution.py:322
  53.3 1.3 %copy-start = (f32[288,1024]{1,0:T(8,128)S(1)}, f32[288,1024]{1,0:T(8,128)}, u32[]{:S(2)}) copy-start(f32[288,1024]{1,0:T(8,128)} %shard_map.65.refs_4_) | copy-start | bytes 3538948

commit v4 on v3

--- a/solution.py
+++ b/solution.py
@@ -15,15 +15,16 @@
 VMEM_BYTES = 40 * 2**20
 
 
-def call(body, outs, args, scratch=(), flops=0, after=()):
+def call(body, outs, args, scratch=(), flops=0, after=(), far_out=()):
     def step(*refs):
         body(*refs[: len(args)], *refs[len(args) + len(after) :])
 
     return pl.pallas_call(
         step,
         out_shape=tuple(outs),
-        in_specs=[pl.BlockSpec(memory_space=pltpu.VMEM)] * len(args) + [pl.BlockSpec(memory_space=pl.ANY)] * len(after),
-        out_specs=tuple(pl.BlockSpec(memory_space=pltpu.VMEM) for _ in outs),
+        in_specs=[pl.BlockSpec(memory_space=pltpu.VMEM)] * len(args)
+        + [pl.BlockSpec(memory_space=pl.ANY)] * len(after),
+        out_specs=tuple(pl.BlockSpec(memory_space=pltpu.HBM if i in far_out else pltpu.VMEM) for i in range(len(outs))),
         scratch_shapes=list(scratch),
         compiler_params=pltpu.CompilerParams(vmem_limit_bytes=VMEM_BYTES),
         cost_estimate=pl.CostEstimate(flops=int(flops), bytes_accessed=0, transcendentals=0),
@@ -47,10 +48,11 @@
     ref[number:, columns] = jnp.broadcast_to(top, (EXTRA, values.shape[1]))
 
 
-def get_coded(ref, columns):
+def get_coded(ref, columns, rows=None):
     number = ref.shape[0] - EXTRA
+    rows = slice(0, number) if rows is None else rows
     step = ref[number:, columns].astype(F32)[:1] * (0.5 / SPAN)
-    code = ref[:number, columns].astype(F32)
+    code = ref[rows, columns].astype(F32)
     size = (jnp.log2(jnp.abs(code)) + SPAN) * step
     return jnp.where(code < 0, -size, size)
 
@@ -231,20 +233,31 @@
 
 def last_filter_kernel(groups, scale, *refs):
     z = lax.axis_index("chan") // 2
-    out_ref = refs[-1]
-    step = out_ref.shape[1] // sum(groups)
-    t = 0
-    for i, pairs in enumerate(groups):
-        for j in range(pairs):
-            here = slice(j * step, (j + 1) * step)
-            there = pl.ds(pl.multiple_of((z ^ t) * step, step), step)
-            out_ref[:, there] = (refs[2 * i][:, here] + get_coded(refs[2 * i + 1], here)) * scale
-            t += 1
+    out_far, sign_ref, done_ref, sent = refs[-4:]
+    sign_ref[...] = jnp.zeros_like(sign_ref)
+    step = done_ref.shape[1] // sum(groups)
+    lines = done_ref.shape[0] // 3
+    copies = []
+    for a in range(3):
+        rows = slice(a * lines, (a + 1) * lines)
+        t = 0
+        for i, pairs in enumerate(groups):
+            for j in range(pairs):
+                here = slice(j * step, (j + 1) * step)
+                there = pl.ds(pl.multiple_of((z ^ t) * step, step), step)
+                done_ref[rows, there] = (refs[2 * i][rows, here] + get_coded(refs[2 * i + 1], here, rows)) * scale
+                t += 1
+        copies.append(pltpu.make_async_copy(done_ref.at[rows], out_far.at[rows], sent.at[a]))
+        copies[-1].start()
+    for copy in copies:
+        copy.wait()
 
 
 def last_filter(groups, parts, channels, scale, cost, after=()):
-    outs = [shape((parts[0].shape[0], channels), F32)]
-    return call(functools.partial(last_filter_kernel, groups, scale), outs, parts, (), cost, after)[0]
+    size = (parts[0].shape[0], channels)
+    scratch = [pltpu.VMEM(size, F32), pltpu.SemaphoreType.DMA((3,))]
+    kernel = functools.partial(last_filter_kernel, groups, scale)
+    return call(kernel, [shape(size, F32), shape((8, 128), F32)], parts, scratch, cost, after, far_out=(0,))
 
 
 def output_kernel(places, cells, width, w_ref, *refs):
@@ -492,8 +505,8 @@
     output = last_output(inner, lax.ppermute(rest, "rows", edges), 0)
 
     scale = 1.0 / math.sqrt(height * rows * width)
-    filter_grad = last_filter(groups, parts, channels, scale, 0)
-    input_grad = last_data(own, pieces, height, 0, (filter_grad,))
+    filter_grad, sign = last_filter(groups, parts, channels, scale, 0)
+    input_grad = last_data(own, pieces, height, 0, (sign,))
     return (
         output,
         input_grad,

time: 56.3 us -> 55 us (0.977)
  local copies, waits for them, and re-layouts: 4.78 us -> 3.51 us
    unnamed x8 -> x6, local copies, waits for them, and re-layouts: 4.78 us -> 3.51 us
where the time goes in v4:
time: 55 us; the launch traced here: 54.3 us
  starting transfers between devices  23.1 us (42%)
  waiting for transfers between devices  16.9 us (31%)
  Pallas kernels  10 us (18%)
  local copies, waits for them, and re-layouts  3.51 us (6%)
  between operations  0.78 us (1%)
    ppermute x20, starting transfers between devices, exchange(): return lax.ppermute(x, axis, [(i, i ^ distance) for i in range(size)])  21.7 us
    ppermute x20, waiting for transfers between devices, exchange(): return lax.ppermute(x, axis, [(i, i ^ distance) for i in range(size)])  16.9 us
    pallas_call x9, Pallas kernels, call(): pl.pallas_call(step, out_shape=tuple(outs), in_specs=[pl.BlockSpec(memory...  10 us
    unnamed x6, local copies, waits for them, and re-layouts  3.51 us
  transfers between devices with their start and end apart: 22, of which 5 were waited for; matrix products, arithmetic and copies ran while one was open for 2% of the time, Pallas kernels for 17%

profile of v4, /device:TPU:0, one launch (start us, length us, event | category | flops | bytes accessed | tf_op | source)
XLA Modules:
  0.0 54.3 jit_solution(15613754280140438032)
XLA Ops:
  0.6 0.9 %copy.6 = bf16[16,8,2,256]{3,1,2,0:T(8,128)(2,1)S(1)} copy(bf16[16,8,2,256]{3,2,1,0:T(2,128)(2,1)} %bitcast.21) | data formatting | bytes 262144
  1.6 5.1 %collective-permute-start.2 = (bf16[128,512]{1,0:T(8,128)(2,1)S(1)}, bf16[128,512]{1,0:T(8,128)(2,1)S(1)}, u32[]{:S(2)}, u32[]{:S(2)}) collective-permute-start(bf16[128,512]{1,0:T(8,128)(2,1)S(1)} %bitcast.9), channel_id=1, source_target_pairs={{0,24},{4,28},{8,16},{12,20},{16,8},{20,12},{24,0},{28,4},{1,25},{... | collective-permute-start | bytes 393224 | tf_op jit(solution)/shard_map/ppermute | solution.py:335
  6.7 0.0 collective-permute-start.1
  6.7 0.9 %copy.7 = bf16[16,8,2,256]{3,1,2,0:T(8,128)(2,1)S(1)} copy(bf16[16,8,2,256]{3,2,1,0:T(2,128)(2,1)} %bitcast.22) | data formatting | bytes 262144
  7.6 0.7 %collective-permute-start.14 = (bf16[128,256]{1,0:T(8,128)(2,1)S(1)}, bf16[128,256]{1,0:T(8,128)(2,1)S(1)}, u32[]{:S(2)}, u32[]{:S(2)}) collective-permute-start(bf16[128,256]{1,0:T(8,128)(2,1)S(1)} %slice_select_fusion), channel_id=1, source_target_pairs={{1,2},{2,1},{5,6},{6,5},{9,10},{10,9},{13,14},{14,13},{17,18},{18,... | collective-permute-start | bytes 196616 | tf_op jit(solution)/shard_map/ppermute | solution.py:470
  8.3 2.9 %collective-permute-start.13 = (bf16[128,512]{1,0:T(8,128)(2,1)S(1)}, bf16[128,512]{1,0:T(8,128)(2,1)S(1)}, u32[]{:S(2)}, u32[]{:S(2)}) collective-permute-start(bf16[128,512]{1,0:T(8,128)(2,1)S(1)} %bitcast.18), channel_id=1, source_target_pairs={{0,1},{1,0},{2,3},{3,2},{4,5},{5,4},{6,7},{7,6},{8,9},{9,8},{10,11... | collective-permute-start | bytes 393224 | tf_op jit(solution)/shard_map/ppermute | solution.py:335
  11.2 1.7 %collective-permute-start.4 = (bf16[128,512]{1,0:T(8,128)(2,1)S(1)}, bf16[128,512]{1,0:T(8,128)(2,1)S(1)}, u32[]{:S(2)}, u32[]{:S(2)}) collective-permute-start(bf16[128,512]{1,0:T(8,128)(2,1)S(1)} %bitcast.11), channel_id=1, source_target_pairs={{0,12},{4,8},{8,4},{12,0},{16,28},{20,24},{24,20},{28,16},{1,13},{... | collective-permute-start | bytes 393224 | tf_op jit(solution)/shard_map/ppermute | solution.py:335
  12.9 0.0 collective-permute-done.14.refs_2_
  12.9 0.1 collective-permute-start.6
  13.1 0.0 collective-permute-done.2
  13.1 1.5 %collective-permute-start.3 = (bf16[128,512]{1,0:T(8,128)(2,1)S(1)}, bf16[128,512]{1,0:T(8,128)(2,1)S(1)}, u32[]{:S(2)}, u32[]{:S(2)}) collective-permute-start(bf16[128,512]{1,0:T(8,128)(2,1)S(1)} %bitcast.13), channel_id=1, source_target_pairs={{0,4},{4,0},{8,12},{12,8},{16,20},{20,16},{24,28},{28,24},{1,5},{5... | collective-permute-start | bytes 393224 | tf_op jit(solution)/shard_map/ppermute | solution.py:335
  14.6 3.3 %collective-permute-done.1 = bf16[128,512]{1,0:T(8,128)(2,1)S(1)} collective-permute-done((bf16[128,512]{1,0:T(8,128)(2,1)S(1)}, bf16[128,512]{1,0:T(8,128)(2,1)S(1)}, u32[]{:S(2)}, u32[]{:S(2)}) %collective-permute-start.1) | collective-permute-done | bytes 131104 | tf_op jit(solution)/shard_map/ppermute | solution.py:335
  17.8 0.0 collective-permute-start.19
  17.9 1.2 %collective-permute-done.19.refs_3_ = bf16[128,256]{1,0:T(8,128)(2,1)S(1)} collective-permute-done((bf16[128,256]{1,0:T(8,128)(2,1)S(1)}, bf16[128,256]{1,0:T(8,128)(2,1)S(1)}, u32[]{:S(2)}, u32[]{:S(2)}) %collective-permute-start.19) | collective-permute-done | bytes 65568 | tf_op jit(solution)/shard_map/ppermute | solution.py:335
  19.1 0.1 collective-permute-start
  19.2 0.0 collective-permute-done.13.refs_1_
  19.2 1.4 %collective-permute-start.5 = (bf16[256,512]{1,0:T(8,128)(2,1)S(1)}, bf16[256,512]{1,0:T(8,128)(2,1)S(1)}, u32[]{:S(2)}, u32[]{:S(2)}) collective-permute-start(bf16[256,512]{1,0:T(8,128)(2,1)S(1)} %pad_maximum_fusion.refs_3_.refs_1_), channel_id=1, source_target_pairs={{0,4},{4,0},{8,12},{12,8},{16,20},{20,16},{24,28},{28,24},{1,5},{5... | collective-permute-start | bytes 786440 | tf_op jit(solution)/shard_map/ppermute | solution.py:335
  20.6 0.0 collective-permute-done.4.refs_5_.refs_4_
  20.6 0.0 collective-permute-start.10
  20.6 0.0 copy-start
  20.6 1.7 %copy-done = bf16[3,3,128,1024]{3,2,1,0:T(8,128)(2,1)S(1)} copy-done((bf16[3,3,128,1024]{3,2,1,0:T(8,128)(2,1)S(1)}, bf16[3,3,128,1024]{3,2,1,0:T(8,128)(2,1)}, u32[]{:S(2)}) %copy-start) | copy-done | bytes 2359320
  22.3 1.9 %shard_map.60 = (f32[512,512]{1,0:T(8,128)S(1)}, bf16[528,512]{1,0:T(8,128)(2,1)S(1)}) custom-call(bf16[128,512]{1,0:T(8,128)(2,1)S(1)} %bitcast.19, bf16[128,512]{1,0:T(8,128)(2,1)S(1)} %collective-permute-done.13.refs_1_, bf16[128,256]{1,0:T(8,128)(2,1)S(1)} %collective-permute-done.14.refs_2_, bf16[1152,1024]{1,0:T(8,128)(2,1)S(1)} %bitcast.7), custom_call_target="tpu_custom_call" | custom-call | flops 24000000000 | tf_op jit(solution)/shard_map/pallas_call | solution.py:22
  24.2 0.0 collective-permute-done.6.refs_7_.refs_5_
  24.2 0.6 %collective-permute-start.8 = (bf16[256,512]{1,0:T(8,128)(2,1)S(1)}, bf16[256,512]{1,0:T(8,128)(2,1)S(1)}, u32[]{:S(2)}, u32[]{:S(2)}) collective-permute-start(bf16[256,512]{1,0:T(8,128)(2,1)S(1)} %pad_maximum_fusion.refs_3_.refs_1_), channel_id=1, source_target_pairs={{0,1},{1,0},{2,3},{3,2},{4,5},{5,4},{6,7},{7,6},{8,9},{9,8},{10,11... | collective-permute-start | bytes 786440 | tf_op jit(solution)/shard_map/ppermute | solution.py:335
  24.8 0.0 collective-permute-done.3.refs_4_.refs_3_
  24.8 1.0 %collective-permute-start.15 = (bf16[528,512]{1,0:T(8,128)(2,1)S(1)}, bf16[528,512]{1,0:T(8,128)(2,1)S(1)}, u32[]{:S(2)}, u32[]{:S(2)}) collective-permute-start(bf16[528,512]{1,0:T(8,128)(2,1)S(1)} %get-tuple-element.20), channel_id=1, source_target_pairs={{0,4},{4,0},{8,12},{12,8},{16,20},{20,16},{24,28},{28,24},{1,5},{5... | collective-permute-start | bytes 1622024 | tf_op jit(solution)/shard_map/ppermute | solution.py:335
  25.8 0.0 collective-permute-done.refs_2_
  25.8 0.0 collective-permute-start.9
  25.8 0.0 collective-permute-done.10.refs_11_.refs_8_
  25.8 0.5 collective-permute-start.7
  26.3 1.2 %collective-permute-done.5.refs_6_.refs_2_ = bf16[256,512]{1,0:T(8,128)(2,1)S(1)} collective-permute-done((bf16[256,512]{1,0:T(8,128)(2,1)S(1)}, bf16[256,512]{1,0:T(8,128)(2,1)S(1)}, u32[]{:S(2)}, u32[]{:S(2)}) %collective-permute-start.5) | collective-permute-done | bytes 262176 | tf_op jit(solution)/shard_map/ppermute | solution.py:335
  27.5 0.0 collective-permute-start.11
  27.5 0.4 shard_map.62.refs_0_
  27.9 0.0 collective-permute-done.9.refs_10_.refs_7_
  27.9 0.0 collective-permute-done.7.refs_8_.refs_6_
  27.9 0.0 copy-start.1
  27.9 1.0 %shard_map.63 = (f32[288,512]{1,0:T(8,128)S(1)}, bf16[304,512]{1,0:T(8,128)(2,1)S(1)}) custom-call(bf16[576,1024]{1,0:T(8,128)(2,1)S(1)} %shard_map.62.refs_0_, bf16[128,512]{1,0:T(8,128)(2,1)S(1)} %bitcast.15, bf16[128,512]{1,0:T(8,128)(2,1)S(1)} %collective-permute-done.refs_2_, bf16[128,512]{1,0:T(8,128)(2,1)S(1)} %collective-permute-done.3.refs_4_.refs_3_, ...), custom_call_target="tpu_custom_call" | custom-call | tf_op jit(solution)/shard_map/pallas_call | solution.py:22
  28.9 1.6 %collective-permute-start.20 = (bf16[304,512]{1,0:T(8,128)(2,1)S(1)}, bf16[304,512]{1,0:T(8,128)(2,1)S(1)}, u32[]{:S(2)}, u32[]{:S(2)}) collective-permute-start(bf16[304,512]{1,0:T(8,128)(2,1)S(1)} %get-tuple-element.28), channel_id=1, source_target_pairs={{0,2},{1,3},{2,0},{3,1},{4,6},{5,7},{6,4},{7,5},{8,10},{9,11},{10,... | collective-permute-start | bytes 933896 | tf_op jit(solution)/shard_map/ppermute | solution.py:335
  30.4 0.0 collective-permute-done.8.refs_9_.refs_3_
  30.4 0.0 collective-permute-done.11.refs_12_.refs_4_
  30.4 1.0 %shard_map.64 = (f32[288,512]{1,0:T(8,128)S(1)}, bf16[304,512]{1,0:T(8,128)(2,1)S(1)}) custom-call(bf16[576,1024]{1,0:T(8,128)(2,1)S(1)} %shard_map.62.refs_0_, bf16[256,512]{1,0:T(8,128)(2,1)S(1)} %pad_maximum_fusion.refs_3_.refs_1_, bf16[256,512]{1,0:T(8,128)(2,1)S(1)} %collective-permute-done.5.refs_6_.refs_2_, ...), custom_call_target="tpu_custom_call" | custom-call | tf_op jit(solution)/shard_map/pallas_call | solution.py:22
  31.4 0.6 %collective-permute-start.21 = (bf16[304,512]{1,0:T(8,128)(2,1)S(1)}, bf16[304,512]{1,0:T(8,128)(2,1)S(1)}, u32[]{:S(2)}, u32[]{:S(2)}) collective-permute-start(bf16[304,512]{1,0:T(8,128)(2,1)S(1)} %get-tuple-element.30), channel_id=1, source_target_pairs={{0,2},{1,3},{2,0},{3,1},{4,6},{5,7},{6,4},{7,5},{8,10},{9,11},{10,... | collective-permute-start | bytes 933896 | tf_op jit(solution)/shard_map/ppermute | solution.py:335
  32.0 0.0 copy-done.1
  32.0 1.9 %shard_map.58 = (f32[128,512]{1,0:T(8,128)S(1)}, f32[128,256]{1,0:T(8,128)S(1)}) custom-call(bf16[9,128,1024]{2,1,0:T(8,128)(2,1)S(1)} %bitcast.8, bf16[128,512]{1,0:T(8,128)(2,1)S(1)} %bitcast.16, bf16[128,512]{1,0:T(8,128)(2,1)S(1)} %collective-permute-done.refs_2_, bf16[256,512]{1,0:T(8,128)(2,1)S(1)} %pad_maximum_fusion.refs_3_.refs_1_, ...), custom_call_target="tpu_custom_call" | custom-call | tf_op jit(solution)/shard_map/pallas_call | solution.py:22
  33.9 0.7 %collective-permute-start.12 = (f32[128,256]{1,0:T(8,128)S(1)}, f32[128,256]{1,0:T(8,128)S(1)}, u32[]{:S(2)}, u32[]{:S(2)}) collective-permute-start(f32[128,256]{1,0:T(8,128)S(1)} %get-tuple-element.19), channel_id=1, source_target_pairs={{1,2},{2,1},{5,6},{6,5},{9,10},{10,9},{13,14},{14,13},{17,18},{18,... | collective-permute-start | bytes 393224 | tf_op jit(solution)/shard_map/ppermute | solution.py:505
  34.6 4.5 %collective-permute-done.15.refs_0_ = bf16[528,512]{1,0:T(8,128)(2,1)S(1)} collective-permute-done((bf16[528,512]{1,0:T(8,128)(2,1)S(1)}, bf16[528,512]{1,0:T(8,128)(2,1)S(1)}, u32[]{:S(2)}, u32[]{:S(2)}) %collective-permute-start.15) | collective-permute-done | bytes 540704 | tf_op jit(solution)/shard_map/ppermute | solution.py:335
  39.1 0.8 %shard_map.61 = (f32[512,128]{1,0:T(8,128)S(1)}, bf16[528,128]{1,0:T(8,128)(2,1)S(1)}, bf16[528,128]{1,0:T(8,128)(2,1)S(1)}, bf16[528,128]{1,0:T(8,128)(2,1)S(1)}) custom-call(bf16[528,512]{1,0:T(8,128)(2,1)S(1)} %collective-permute-done.15.refs_0_, f32[512,512]{1,0:T(8,128)S(1)} %get-tuple-element.21.refs_1_), custom_call_target="tpu_custom_call" | custom-call | tf_op jit(solution)/shard_map/pallas_call | solution.py:22
  39.9 2.1 %collective-permute-start.16 = (bf16[528,128]{1,0:T(8,128)(2,1)S(1)}, bf16[528,128]{1,0:T(8,128)(2,1)S(1)}, u32[]{:S(2)}, u32[]{:S(2)}) collective-permute-start(bf16[528,128]{1,0:T(8,128)(2,1)S(1)} %get-tuple-element.23), channel_id=1, source_target_pairs={{0,8},{4,12},{8,0},{12,4},{16,24},{20,28},{24,16},{28,20},{1,9},{5... | collective-permute-start | bytes 405512 | tf_op jit(solution)/shard_map/ppermute | solution.py:335
  41.9 1.1 %collective-permute-start.17 = (bf16[528,128]{1,0:T(8,128)(2,1)S(1)}, bf16[528,128]{1,0:T(8,128)(2,1)S(1)}, u32[]{:S(2)}, u32[]{:S(2)}) collective-permute-start(bf16[528,128]{1,0:T(8,128)(2,1)S(1)} %get-tuple-element.24), channel_id=1, source_target_pairs={{0,16},{4,20},{8,24},{12,28},{16,0},{20,4},{24,8},{28,12},{1,17},{... | collective-permute-start | bytes 405512 | tf_op jit(solution)/shard_map/ppermute | solution.py:335
  43.0 0.0 collective-permute-done.12.refs_1_
  43.0 1.4 %collective-permute-start.18 = (bf16[528,128]{1,0:T(8,128)(2,1)S(1)}, bf16[528,128]{1,0:T(8,128)(2,1)S(1)}, u32[]{:S(2)}, u32[]{:S(2)}) collective-permute-start(bf16[528,128]{1,0:T(8,128)(2,1)S(1)} %get-tuple-element.25), channel_id=1, source_target_pairs={{0,24},{4,28},{8,16},{12,20},{16,8},{20,12},{24,0},{28,4},{1,25},{... | collective-permute-start | bytes 405512 | tf_op jit(solution)/shard_map/ppermute | solution.py:335
  44.4 0.9 %shard_map.59 = bf16[128,2,256]{2,1,0:T(2,128)(2,1)} custom-call(f32[128,512]{1,0:T(8,128)S(1)} %get-tuple-element.18.refs_0_, f32[128,256]{1,0:T(8,128)S(1)} %collective-permute-done.12.refs_1_), custom_call_target="tpu_custom_call" | custom-call | tf_op jit(solution)/shard_map/pallas_call | solution.py:22
  45.3 0.0 collective-permute-done.20.refs_1_
  45.3 0.0 collective-permute-done.21.refs_3_
  45.4 1.2 %shard_map.65 = (f32[288,1024]{1,0:T(8,128)}, f32[8,128]{1,0:T(8,128)S(1)}) custom-call(f32[288,512]{1,0:T(8,128)S(1)} %get-tuple-element.27.refs_0_, bf16[304,512]{1,0:T(8,128)(2,1)S(1)} %collective-permute-done.20.refs_1_, f32[288,512]{1,0:T(8,128)S(1)} %get-tuple-element.29.refs_2_, bf16[304,512]{1,0:T(8,128)(2,1)S(1)} %collective-permute-done.21.refs_3_), custom_call_target="tpu_custom_call" | custom-call | tf_op jit(solution)/shard_map/pallas_call | solution.py:22
  46.6 0.0 collective-permute-done.16.refs_1_
  46.6 6.7 %collective-permute-done.17.refs_2_ = bf16[528,128]{1,0:T(8,128)(2,1)S(1)} collective-permute-done((bf16[528,128]{1,0:T(8,128)(2,1)S(1)}, bf16[528,128]{1,0:T(8,128)(2,1)S(1)}, u32[]{:S(2)}, u32[]{:S(2)}) %collective-permute-start.17) | collective-permute-done | bytes 135200 | tf_op jit(solution)/shard_map/ppermute | solution.py:335
  53.3 0.0 collective-permute-done.18.refs_3_
  53.3 1.0 %shard_map.66 = bf16[128,2,256]{2,1,0:T(2,128)(2,1)} custom-call(f32[512,128]{1,0:T(8,128)S(1)} %get-tuple-element.22.refs_0_, bf16[528,128]{1,0:T(8,128)(2,1)S(1)} %collective-permute-done.16.refs_1_, bf16[528,128]{1,0:T(8,128)(2,1)S(1)} %collective-permute-done.17.refs_2_, bf16[528,128]{1,0:T(8,128)(2,1)S(1)} %collective-permute-done.18.refs_3_, ...), custom_call_target="tpu_custom_call" | custom-call | tf_op jit(solution)/shard_map/pallas_call | solution.py:22
  (2 shorter events, 0.0 us)
Async XLA Ops:
  1.6 11.5 %collective-permute-start.2 = (bf16[128,512]{1,0:T(8,128)(2,1)S(1)}, bf16[128,512]{1,0:T(8,128)(2,1)S(1)}, u32[]{:S(2)}, u32[]{:S(2)}) collective-permute-start(bf16[128,512]{1,0:T(8,128)(2,1)S(1)} %bitcast.9), channel_id=1, source_target_pairs={{0,24},{4,28},{8,16},{12,20},{16,8},{20,12},{24,0},{28,4},{1,25},{... | collective-permute-start | bytes 393224 | tf_op jit(solution)/shard_map/ppermute | solution.py:335
  6.7 11.2 %collective-permute-start.1 = (bf16[128,512]{1,0:T(8,128)(2,1)S(1)}, bf16[128,512]{1,0:T(8,128)(2,1)S(1)}, u32[]{:S(2)}, u32[]{:S(2)}) collective-permute-start(bf16[128,512]{1,0:T(8,128)(2,1)S(1)} %bitcast.10), channel_id=1, source_target_pairs={{0,16},{4,20},{8,24},{12,28},{16,0},{20,4},{24,8},{28,12},{1,17},{... | collective-permute-start | bytes 393224 | tf_op jit(solution)/shard_map/ppermute | solution.py:335
  7.6 5.3 %collective-permute-start.14 = (bf16[128,256]{1,0:T(8,128)(2,1)S(1)}, bf16[128,256]{1,0:T(8,128)(2,1)S(1)}, u32[]{:S(2)}, u32[]{:S(2)}) collective-permute-start(bf16[128,256]{1,0:T(8,128)(2,1)S(1)} %slice_select_fusion), channel_id=1, source_target_pairs={{1,2},{2,1},{5,6},{6,5},{9,10},{10,9},{13,14},{14,13},{17,18},{18,... | collective-permute-start | bytes 196616 | tf_op jit(solution)/shard_map/ppermute | solution.py:470
  8.3 11.0 %collective-permute-start.13 = (bf16[128,512]{1,0:T(8,128)(2,1)S(1)}, bf16[128,512]{1,0:T(8,128)(2,1)S(1)}, u32[]{:S(2)}, u32[]{:S(2)}) collective-permute-start(bf16[128,512]{1,0:T(8,128)(2,1)S(1)} %bitcast.18), channel_id=1, source_target_pairs={{0,1},{1,0},{2,3},{3,2},{4,5},{5,4},{6,7},{7,6},{8,9},{9,8},{10,11... | collective-permute-start | bytes 393224 | tf_op jit(solution)/shard_map/ppermute | solution.py:335
  11.2 9.4 %collective-permute-start.4 = (bf16[128,512]{1,0:T(8,128)(2,1)S(1)}, bf16[128,512]{1,0:T(8,128)(2,1)S(1)}, u32[]{:S(2)}, u32[]{:S(2)}) collective-permute-start(bf16[128,512]{1,0:T(8,128)(2,1)S(1)} %bitcast.11), channel_id=1, source_target_pairs={{0,12},{4,8},{8,4},{12,0},{16,28},{20,24},{24,20},{28,16},{1,13},{... | collective-permute-start | bytes 393224 | tf_op jit(solution)/shard_map/ppermute | solution.py:335
  12.9 11.3 %collective-permute-start.6 = (bf16[128,512]{1,0:T(8,128)(2,1)S(1)}, bf16[128,512]{1,0:T(8,128)(2,1)S(1)}, u32[]{:S(2)}, u32[]{:S(2)}) collective-permute-start(bf16[128,512]{1,0:T(8,128)(2,1)S(1)} %bitcast.12), channel_id=1, source_target_pairs={{0,1},{1,0},{2,3},{3,2},{4,5},{5,4},{6,7},{7,6},{8,9},{9,8},{10,11... | collective-permute-start | bytes 393224 | tf_op jit(solution)/shard_map/ppermute | solution.py:335
  13.1 11.7 %collective-permute-start.3 = (bf16[128,512]{1,0:T(8,128)(2,1)S(1)}, bf16[128,512]{1,0:T(8,128)(2,1)S(1)}, u32[]{:S(2)}, u32[]{:S(2)}) collective-permute-start(bf16[128,512]{1,0:T(8,128)(2,1)S(1)} %bitcast.13), channel_id=1, source_target_pairs={{0,4},{4,0},{8,12},{12,8},{16,20},{20,16},{24,28},{28,24},{1,5},{5... | collective-permute-start | bytes 393224 | tf_op jit(solution)/shard_map/ppermute | solution.py:335
  17.8 1.3 %collective-permute-start.19 = (bf16[128,256]{1,0:T(8,128)(2,1)S(1)}, bf16[128,256]{1,0:T(8,128)(2,1)S(1)}, u32[]{:S(2)}, u32[]{:S(2)}) collective-permute-start(bf16[128,256]{1,0:T(8,128)(2,1)S(1)} %collective-permute-done.14.refs_2_), channel_id=1, source_target_pairs={{0,1},{1,0},{2,3},{3,2},{4,5},{5,4},{6,7},{7,6},{8,9},{9,8},{10,11... | collective-permute-start | bytes 196616 | tf_op jit(solution)/shard_map/ppermute | solution.py:335
  19.1 6.7 %collective-permute-start = (bf16[128,512]{1,0:T(8,128)(2,1)S(1)}, bf16[128,512]{1,0:T(8,128)(2,1)S(1)}, u32[]{:S(2)}, u32[]{:S(2)}) collective-permute-start(bf16[128,512]{1,0:T(8,128)(2,1)S(1)} %bitcast.14), channel_id=1, source_target_pairs={{0,8},{4,12},{8,0},{12,4},{16,24},{20,28},{24,16},{28,20},{1,9},{5... | collective-permute-start | bytes 393224 | tf_op jit(solution)/shard_map/ppermute | solution.py:335
  19.2 8.2 %collective-permute-start.5 = (bf16[256,512]{1,0:T(8,128)(2,1)S(1)}, bf16[256,512]{1,0:T(8,128)(2,1)S(1)}, u32[]{:S(2)}, u32[]{:S(2)}) collective-permute-start(bf16[256,512]{1,0:T(8,128)(2,1)S(1)} %pad_maximum_fusion.refs_3_.refs_1_), channel_id=1, source_target_pairs={{0,4},{4,0},{8,12},{12,8},{16,20},{20,16},{24,28},{28,24},{1,5},{5... | collective-permute-start | bytes 786440 | tf_op jit(solution)/shard_map/ppermute | solution.py:335
  20.6 5.2 %collective-permute-start.10 = (bf16[128,512]{1,0:T(8,128)(2,1)S(1)}, bf16[128,512]{1,0:T(8,128)(2,1)S(1)}, u32[]{:S(2)}, u32[]{:S(2)}) collective-permute-start(bf16[128,512]{1,0:T(8,128)(2,1)S(1)} %collective-permute-done.4.refs_5_.refs_4_), channel_id=1, source_target_pairs={{0,1},{1,0},{2,3},{3,2},{4,5},{5,4},{6,7},{7,6},{8,9},{9,8},{10,11... | collective-permute-start | bytes 393224 | tf_op jit(solution)/shard_map/ppermute | solution.py:335
  20.6 1.7 %copy-start = (bf16[3,3,128,1024]{3,2,1,0:T(8,128)(2,1)S(1)}, bf16[3,3,128,1024]{3,2,1,0:T(8,128)(2,1)}, u32[]{:S(2)}) copy-start(bf16[3,3,128,1024]{3,2,1,0:T(8,128)(2,1)} %param.4) | copy-start | bytes 7077892
  24.2 6.2 %collective-permute-start.8 = (bf16[256,512]{1,0:T(8,128)(2,1)S(1)}, bf16[256,512]{1,0:T(8,128)(2,1)S(1)}, u32[]{:S(2)}, u32[]{:S(2)}) collective-permute-start(bf16[256,512]{1,0:T(8,128)(2,1)S(1)} %pad_maximum_fusion.refs_3_.refs_1_), channel_id=1, source_target_pairs={{0,1},{1,0},{2,3},{3,2},{4,5},{5,4},{6,7},{7,6},{8,9},{9,8},{10,11... | collective-permute-start | bytes 786440 | tf_op jit(solution)/shard_map/ppermute | solution.py:335
  24.8 14.3 %collective-permute-start.15 = (bf16[528,512]{1,0:T(8,128)(2,1)S(1)}, bf16[528,512]{1,0:T(8,128)(2,1)S(1)}, u32[]{:S(2)}, u32[]{:S(2)}) collective-permute-start(bf16[528,512]{1,0:T(8,128)(2,1)S(1)} %get-tuple-element.20), channel_id=1, source_target_pairs={{0,4},{4,0},{8,12},{12,8},{16,20},{20,16},{24,28},{28,24},{1,5},{5... | collective-permute-start | bytes 1622024 | tf_op jit(solution)/shard_map/ppermute | solution.py:335
  25.8 2.1 %collective-permute-start.9 = (bf16[128,512]{1,0:T(8,128)(2,1)S(1)}, bf16[128,512]{1,0:T(8,128)(2,1)S(1)}, u32[]{:S(2)}, u32[]{:S(2)}) collective-permute-start(bf16[128,512]{1,0:T(8,128)(2,1)S(1)} %collective-permute-done.3.refs_4_.refs_3_), channel_id=1, source_target_pairs={{0,1},{1,0},{2,3},{3,2},{4,5},{5,4},{6,7},{7,6},{8,9},{9,8},{10,11... | collective-permute-start | bytes 393224 | tf_op jit(solution)/shard_map/ppermute | solution.py:335
  25.8 2.1 %collective-permute-start.7 = (bf16[128,512]{1,0:T(8,128)(2,1)S(1)}, bf16[128,512]{1,0:T(8,128)(2,1)S(1)}, u32[]{:S(2)}, u32[]{:S(2)}) collective-permute-start(bf16[128,512]{1,0:T(8,128)(2,1)S(1)} %collective-permute-done.refs_2_), channel_id=1, source_target_pairs={{0,1},{1,0},{2,3},{3,2},{4,5},{5,4},{6,7},{7,6},{8,9},{9,8},{10,11... | collective-permute-start | bytes 393224 | tf_op jit(solution)/shard_map/ppermute | solution.py:335
  27.5 3.0 %collective-permute-start.11 = (bf16[256,512]{1,0:T(8,128)(2,1)S(1)}, bf16[256,512]{1,0:T(8,128)(2,1)S(1)}, u32[]{:S(2)}, u32[]{:S(2)}) collective-permute-start(bf16[256,512]{1,0:T(8,128)(2,1)S(1)} %collective-permute-done.5.refs_6_.refs_2_), channel_id=1, source_target_pairs={{0,1},{1,0},{2,3},{3,2},{4,5},{5,4},{6,7},{7,6},{8,9},{9,8},{10,11... | collective-permute-start | bytes 786440 | tf_op jit(solution)/shard_map/ppermute | solution.py:335
  27.9 4.1 %copy-start.1 = (bf16[3,3,128,1024]{3,2,1,0:T(8,128)(2,1)S(1)}, bf16[3,3,128,1024]{3,2,1,0:T(8,128)(2,1)}, u32[]{:S(2)}) copy-start(bf16[3,3,128,1024]{3,2,1,0:T(8,128)(2,1)} %param.4) | copy-start | bytes 7077892
  28.9 16.5 %collective-permute-start.20 = (bf16[304,512]{1,0:T(8,128)(2,1)S(1)}, bf16[304,512]{1,0:T(8,128)(2,1)S(1)}, u32[]{:S(2)}, u32[]{:S(2)}) collective-permute-start(bf16[304,512]{1,0:T(8,128)(2,1)S(1)} %get-tuple-element.28), channel_id=1, source_target_pairs={{0,2},{1,3},{2,0},{3,1},{4,6},{5,7},{6,4},{7,5},{8,10},{9,11},{10,... | collective-permute-start | bytes 933896 | tf_op jit(solution)/shard_map/ppermute | solution.py:335
  31.4 14.0 %collective-permute-start.21 = (bf16[304,512]{1,0:T(8,128)(2,1)S(1)}, bf16[304,512]{1,0:T(8,128)(2,1)S(1)}, u32[]{:S(2)}, u32[]{:S(2)}) collective-permute-start(bf16[304,512]{1,0:T(8,128)(2,1)S(1)} %get-tuple-element.30), channel_id=1, source_target_pairs={{0,2},{1,3},{2,0},{3,1},{4,6},{5,7},{6,4},{7,5},{8,10},{9,11},{10,... | collective-permute-start | bytes 933896 | tf_op jit(solution)/shard_map/ppermute | solution.py:335
  33.9 9.1 %collective-permute-start.12 = (f32[128,256]{1,0:T(8,128)S(1)}, f32[128,256]{1,0:T(8,128)S(1)}, u32[]{:S(2)}, u32[]{:S(2)}) collective-permute-start(f32[128,256]{1,0:T(8,128)S(1)} %get-tuple-element.19), channel_id=1, source_target_pairs={{1,2},{2,1},{5,6},{6,5},{9,10},{10,9},{13,14},{14,13},{17,18},{18,... | collective-permute-start | bytes 393224 | tf_op jit(solution)/shard_map/ppermute | solution.py:505
  39.9 6.7 %collective-permute-start.16 = (bf16[528,128]{1,0:T(8,128)(2,1)S(1)}, bf16[528,128]{1,0:T(8,128)(2,1)S(1)}, u32[]{:S(2)}, u32[]{:S(2)}) collective-permute-start(bf16[528,128]{1,0:T(8,128)(2,1)S(1)} %get-tuple-element.23), channel_id=1, source_target_pairs={{0,8},{4,12},{8,0},{12,4},{16,24},{20,28},{24,16},{28,20},{1,9},{5... | collective-permute-start | bytes 405512 | tf_op jit(solution)/shard_map/ppermute | solution.py:335
  41.9 11.3 %collective-permute-start.17 = (bf16[528,128]{1,0:T(8,128)(2,1)S(1)}, bf16[528,128]{1,0:T(8,128)(2,1)S(1)}, u32[]{:S(2)}, u32[]{:S(2)}) collective-permute-start(bf16[528,128]{1,0:T(8,128)(2,1)S(1)} %get-tuple-element.24), channel_id=1, source_target_pairs={{0,16},{4,20},{8,24},{12,28},{16,0},{20,4},{24,8},{28,12},{1,17},{... | collective-permute-start | bytes 405512 | tf_op jit(solution)/shard_map/ppermute | solution.py:335
  43.0 10.2 %collective-permute-start.18 = (bf16[528,128]{1,0:T(8,128)(2,1)S(1)}, bf16[528,128]{1,0:T(8,128)(2,1)S(1)}, u32[]{:S(2)}, u32[]{:S(2)}) collective-permute-start(bf16[528,128]{1,0:T(8,128)(2,1)S(1)} %get-tuple-element.25), channel_id=1, source_target_pairs={{0,24},{4,28},{8,16},{12,20},{16,8},{20,12},{24,0},{28,4},{1,25},{... | collective-permute-start | bytes 405512 | tf_op jit(solution)/shard_map/ppermute | solution.py:335

commit v5 on v4

--- a/solution.py
+++ b/solution.py
@@ -481,8 +481,8 @@
 
     others = {k: exchange(direct[k], "rows", 1) for k in range(2 * half)}
     rim = exchange(halo, "rows", 1)
-    rim, give = lax.optimization_barrier((rim, give))
-    lines = filter_lines(g, adj, halo, rim, share, width, 12000000000.0)
+    g_after, give = lax.optimization_barrier((g, give))
+    lines = filter_lines(g_after, adj, halo, rim, share, width, 12000000000.0)
     near = [(direct[2 * t], 0) for t in range(half)]
     far = [(direct[2 * t + 1], 0) for t in range(half)]
     near_o = [(others[2 * t], 0) for t in range(half)]

time: 55 us -> 55 us (level)
  no operation moved by 1% of the time
where the time goes in v5:
time: 55 us; the launch traced here: 54.3 us
  starting transfers between devices  23.1 us (42%)
  waiting for transfers between devices  16.9 us (31%)
  Pallas kernels  10 us (18%)
  local copies, waits for them, and re-layouts  3.51 us (6%)
  between operations  0.78 us (1%)
    ppermute x20, starting transfers between devices, exchange(): return lax.ppermute(x, axis, [(i, i ^ distance) for i in range(size)])  21.7 us
    ppermute x20, waiting for transfers between devices, exchange(): return lax.ppermute(x, axis, [(i, i ^ distance) for i in range(size)])  16.9 us
    pallas_call x9, Pallas kernels, call(): pl.pallas_call(step, out_shape=tuple(outs), in_specs=[pl.BlockSpec(memory...  10 us
    unnamed x6, local copies, waits for them, and re-layouts  3.51 us
  transfers between devices with their start and end apart: 22, of which 5 were waited for; matrix products, arithmetic and copies ran while one was open for 2% of the time, Pallas kernels for 17%

profile of v5, /device:TPU:0, one launch (start us, length us, event | category | flops | bytes accessed | tf_op | source)
XLA Modules:
  0.0 54.3 jit_solution(15613754280140438032)
XLA Ops:
  0.6 0.9 %copy.6 = bf16[16,8,2,256]{3,1,2,0:T(8,128)(2,1)S(1)} copy(bf16[16,8,2,256]{3,2,1,0:T(2,128)(2,1)} %bitcast.21) | data formatting | bytes 262144
  1.6 5.1 %collective-permute-start.2 = (bf16[128,512]{1,0:T(8,128)(2,1)S(1)}, bf16[128,512]{1,0:T(8,128)(2,1)S(1)}, u32[]{:S(2)}, u32[]{:S(2)}) collective-permute-start(bf16[128,512]{1,0:T(8,128)(2,1)S(1)} %bitcast.9), channel_id=1, source_target_pairs={{0,24},{4,28},{8,16},{12,20},{16,8},{20,12},{24,0},{28,4},{1,25},{... | collective-permute-start | bytes 393224 | tf_op jit(solution)/shard_map/ppermute | solution.py:335
  6.7 0.0 collective-permute-start.1
  6.7 0.9 %copy.7 = bf16[16,8,2,256]{3,1,2,0:T(8,128)(2,1)S(1)} copy(bf16[16,8,2,256]{3,2,1,0:T(2,128)(2,1)} %bitcast.22) | data formatting | bytes 262144
  7.6 0.7 %collective-permute-start.14 = (bf16[128,256]{1,0:T(8,128)(2,1)S(1)}, bf16[128,256]{1,0:T(8,128)(2,1)S(1)}, u32[]{:S(2)}, u32[]{:S(2)}) collective-permute-start(bf16[128,256]{1,0:T(8,128)(2,1)S(1)} %slice_select_fusion), channel_id=1, source_target_pairs={{1,2},{2,1},{5,6},{6,5},{9,10},{10,9},{13,14},{14,13},{17,18},{18,... | collective-permute-start | bytes 196616 | tf_op jit(solution)/shard_map/ppermute | solution.py:470
  8.3 2.9 %collective-permute-start.13 = (bf16[128,512]{1,0:T(8,128)(2,1)S(1)}, bf16[128,512]{1,0:T(8,128)(2,1)S(1)}, u32[]{:S(2)}, u32[]{:S(2)}) collective-permute-start(bf16[128,512]{1,0:T(8,128)(2,1)S(1)} %bitcast.18), channel_id=1, source_target_pairs={{0,1},{1,0},{2,3},{3,2},{4,5},{5,4},{6,7},{7,6},{8,9},{9,8},{10,11... | collective-permute-start | bytes 393224 | tf_op jit(solution)/shard_map/ppermute | solution.py:335
  11.2 1.7 %collective-permute-start.4 = (bf16[128,512]{1,0:T(8,128)(2,1)S(1)}, bf16[128,512]{1,0:T(8,128)(2,1)S(1)}, u32[]{:S(2)}, u32[]{:S(2)}) collective-permute-start(bf16[128,512]{1,0:T(8,128)(2,1)S(1)} %bitcast.11), channel_id=1, source_target_pairs={{0,12},{4,8},{8,4},{12,0},{16,28},{20,24},{24,20},{28,16},{1,13},{... | collective-permute-start | bytes 393224 | tf_op jit(solution)/shard_map/ppermute | solution.py:335
  12.9 0.0 collective-permute-done.14.refs_2_
  12.9 0.1 collective-permute-start.6
  13.1 0.0 collective-permute-done.2
  13.1 1.5 %collective-permute-start.3 = (bf16[128,512]{1,0:T(8,128)(2,1)S(1)}, bf16[128,512]{1,0:T(8,128)(2,1)S(1)}, u32[]{:S(2)}, u32[]{:S(2)}) collective-permute-start(bf16[128,512]{1,0:T(8,128)(2,1)S(1)} %bitcast.13), channel_id=1, source_target_pairs={{0,4},{4,0},{8,12},{12,8},{16,20},{20,16},{24,28},{28,24},{1,5},{5... | collective-permute-start | bytes 393224 | tf_op jit(solution)/shard_map/ppermute | solution.py:335
  14.6 3.3 %collective-permute-done.1 = bf16[128,512]{1,0:T(8,128)(2,1)S(1)} collective-permute-done((bf16[128,512]{1,0:T(8,128)(2,1)S(1)}, bf16[128,512]{1,0:T(8,128)(2,1)S(1)}, u32[]{:S(2)}, u32[]{:S(2)}) %collective-permute-start.1) | collective-permute-done | bytes 131104 | tf_op jit(solution)/shard_map/ppermute | solution.py:335
  17.8 0.0 collective-permute-start.19
  17.9 1.2 %collective-permute-done.19.refs_3_ = bf16[128,256]{1,0:T(8,128)(2,1)S(1)} collective-permute-done((bf16[128,256]{1,0:T(8,128)(2,1)S(1)}, bf16[128,256]{1,0:T(8,128)(2,1)S(1)}, u32[]{:S(2)}, u32[]{:S(2)}) %collective-permute-start.19) | collective-permute-done | bytes 65568 | tf_op jit(solution)/shard_map/ppermute | solution.py:335
  19.1 0.1 collective-permute-start
  19.2 0.0 collective-permute-done.13.refs_1_
  19.2 1.4 %collective-permute-start.5 = (bf16[256,512]{1,0:T(8,128)(2,1)S(1)}, bf16[256,512]{1,0:T(8,128)(2,1)S(1)}, u32[]{:S(2)}, u32[]{:S(2)}) collective-permute-start(bf16[256,512]{1,0:T(8,128)(2,1)S(1)} %pad_maximum_fusion.refs_3_.refs_1_), channel_id=1, source_target_pairs={{0,4},{4,0},{8,12},{12,8},{16,20},{20,16},{24,28},{28,24},{1,5},{5... | collective-permute-start | bytes 786440 | tf_op jit(solution)/shard_map/ppermute | solution.py:335
  20.6 0.0 collective-permute-done.4.refs_5_.refs_4_
  20.6 0.0 collective-permute-start.10
  20.6 0.0 copy-start
  20.6 1.7 %copy-done = bf16[3,3,128,1024]{3,2,1,0:T(8,128)(2,1)S(1)} copy-done((bf16[3,3,128,1024]{3,2,1,0:T(8,128)(2,1)S(1)}, bf16[3,3,128,1024]{3,2,1,0:T(8,128)(2,1)}, u32[]{:S(2)}) %copy-start) | copy-done | bytes 2359320
  22.3 1.9 %shard_map.60 = (f32[512,512]{1,0:T(8,128)S(1)}, bf16[528,512]{1,0:T(8,128)(2,1)S(1)}) custom-call(bf16[128,512]{1,0:T(8,128)(2,1)S(1)} %bitcast.19, bf16[128,512]{1,0:T(8,128)(2,1)S(1)} %collective-permute-done.13.refs_1_, bf16[128,256]{1,0:T(8,128)(2,1)S(1)} %collective-permute-done.14.refs_2_, bf16[1152,1024]{1,0:T(8,128)(2,1)S(1)} %bitcast.7), custom_call_target="tpu_custom_call" | custom-call | flops 24000000000 | tf_op jit(solution)/shard_map/pallas_call | solution.py:22
  24.2 0.0 collective-permute-done.6.refs_7_.refs_5_
  24.2 0.6 %collective-permute-start.8 = (bf16[256,512]{1,0:T(8,128)(2,1)S(1)}, bf16[256,512]{1,0:T(8,128)(2,1)S(1)}, u32[]{:S(2)}, u32[]{:S(2)}) collective-permute-start(bf16[256,512]{1,0:T(8,128)(2,1)S(1)} %pad_maximum_fusion.refs_3_.refs_1_), channel_id=1, source_target_pairs={{0,1},{1,0},{2,3},{3,2},{4,5},{5,4},{6,7},{7,6},{8,9},{9,8},{10,11... | collective-permute-start | bytes 786440 | tf_op jit(solution)/shard_map/ppermute | solution.py:335
  24.8 0.0 collective-permute-done.3.refs_4_.refs_3_
  24.8 1.0 %collective-permute-start.15 = (bf16[528,512]{1,0:T(8,128)(2,1)S(1)}, bf16[528,512]{1,0:T(8,128)(2,1)S(1)}, u32[]{:S(2)}, u32[]{:S(2)}) collective-permute-start(bf16[528,512]{1,0:T(8,128)(2,1)S(1)} %get-tuple-element.20), channel_id=1, source_target_pairs={{0,4},{4,0},{8,12},{12,8},{16,20},{20,16},{24,28},{28,24},{1,5},{5... | collective-permute-start | bytes 1622024 | tf_op jit(solution)/shard_map/ppermute | solution.py:335
  25.8 0.0 collective-permute-done.refs_2_
  25.8 0.0 collective-permute-start.9
  25.8 0.0 collective-permute-done.10.refs_11_.refs_8_
  25.8 0.5 collective-permute-start.7
  26.3 1.2 %collective-permute-done.5.refs_6_.refs_2_ = bf16[256,512]{1,0:T(8,128)(2,1)S(1)} collective-permute-done((bf16[256,512]{1,0:T(8,128)(2,1)S(1)}, bf16[256,512]{1,0:T(8,128)(2,1)S(1)}, u32[]{:S(2)}, u32[]{:S(2)}) %collective-permute-start.5) | collective-permute-done | bytes 262176 | tf_op jit(solution)/shard_map/ppermute | solution.py:335
  27.5 0.0 collective-permute-start.11
  27.5 0.4 shard_map.62.refs_0_
  27.9 0.0 collective-permute-done.9.refs_10_.refs_7_
  27.9 0.0 collective-permute-done.7.refs_8_.refs_6_
  27.9 0.0 copy-start.1
  27.9 1.0 %shard_map.63 = (f32[288,512]{1,0:T(8,128)S(1)}, bf16[304,512]{1,0:T(8,128)(2,1)S(1)}) custom-call(bf16[576,1024]{1,0:T(8,128)(2,1)S(1)} %shard_map.62.refs_0_, bf16[128,512]{1,0:T(8,128)(2,1)S(1)} %bitcast.15, bf16[128,512]{1,0:T(8,128)(2,1)S(1)} %collective-permute-done.refs_2_, bf16[128,512]{1,0:T(8,128)(2,1)S(1)} %collective-permute-done.3.refs_4_.refs_3_, ...), custom_call_target="tpu_custom_call" | custom-call | tf_op jit(solution)/shard_map/pallas_call | solution.py:22
  28.9 1.6 %collective-permute-start.20 = (bf16[304,512]{1,0:T(8,128)(2,1)S(1)}, bf16[304,512]{1,0:T(8,128)(2,1)S(1)}, u32[]{:S(2)}, u32[]{:S(2)}) collective-permute-start(bf16[304,512]{1,0:T(8,128)(2,1)S(1)} %get-tuple-element.28), channel_id=1, source_target_pairs={{0,2},{1,3},{2,0},{3,1},{4,6},{5,7},{6,4},{7,5},{8,10},{9,11},{10,... | collective-permute-start | bytes 933896 | tf_op jit(solution)/shard_map/ppermute | solution.py:335
  30.4 0.0 collective-permute-done.8.refs_9_.refs_3_
  30.4 0.0 collective-permute-done.11.refs_12_.refs_4_
  30.4 1.0 %shard_map.64 = (f32[288,512]{1,0:T(8,128)S(1)}, bf16[304,512]{1,0:T(8,128)(2,1)S(1)}) custom-call(bf16[576,1024]{1,0:T(8,128)(2,1)S(1)} %shard_map.62.refs_0_, bf16[256,512]{1,0:T(8,128)(2,1)S(1)} %pad_maximum_fusion.refs_3_.refs_1_, bf16[256,512]{1,0:T(8,128)(2,1)S(1)} %collective-permute-done.5.refs_6_.refs_2_, ...), custom_call_target="tpu_custom_call" | custom-call | tf_op jit(solution)/shard_map/pallas_call | solution.py:22
  31.4 0.6 %collective-permute-start.21 = (bf16[304,512]{1,0:T(8,128)(2,1)S(1)}, bf16[304,512]{1,0:T(8,128)(2,1)S(1)}, u32[]{:S(2)}, u32[]{:S(2)}) collective-permute-start(bf16[304,512]{1,0:T(8,128)(2,1)S(1)} %get-tuple-element.30), channel_id=1, source_target_pairs={{0,2},{1,3},{2,0},{3,1},{4,6},{5,7},{6,4},{7,5},{8,10},{9,11},{10,... | collective-permute-start | bytes 933896 | tf_op jit(solution)/shard_map/ppermute | solution.py:335
  32.0 0.0 copy-done.1
  32.0 1.9 %shard_map.58 = (f32[128,512]{1,0:T(8,128)S(1)}, f32[128,256]{1,0:T(8,128)S(1)}) custom-call(bf16[9,128,1024]{2,1,0:T(8,128)(2,1)S(1)} %bitcast.8, bf16[128,512]{1,0:T(8,128)(2,1)S(1)} %bitcast.16, bf16[128,512]{1,0:T(8,128)(2,1)S(1)} %collective-permute-done.refs_2_, bf16[256,512]{1,0:T(8,128)(2,1)S(1)} %pad_maximum_fusion.refs_3_.refs_1_, ...), custom_call_target="tpu_custom_call" | custom-call | tf_op jit(solution)/shard_map/pallas_call | solution.py:22
  33.9 0.7 %collective-permute-start.12 = (f32[128,256]{1,0:T(8,128)S(1)}, f32[128,256]{1,0:T(8,128)S(1)}, u32[]{:S(2)}, u32[]{:S(2)}) collective-permute-start(f32[128,256]{1,0:T(8,128)S(1)} %get-tuple-element.19), channel_id=1, source_target_pairs={{1,2},{2,1},{5,6},{6,5},{9,10},{10,9},{13,14},{14,13},{17,18},{18,... | collective-permute-start | bytes 393224 | tf_op jit(solution)/shard_map/ppermute | solution.py:505
  34.6 4.5 %collective-permute-done.15.refs_0_ = bf16[528,512]{1,0:T(8,128)(2,1)S(1)} collective-permute-done((bf16[528,512]{1,0:T(8,128)(2,1)S(1)}, bf16[528,512]{1,0:T(8,128)(2,1)S(1)}, u32[]{:S(2)}, u32[]{:S(2)}) %collective-permute-start.15) | collective-permute-done | bytes 540704 | tf_op jit(solution)/shard_map/ppermute | solution.py:335
  39.1 0.8 %shard_map.61 = (f32[512,128]{1,0:T(8,128)S(1)}, bf16[528,128]{1,0:T(8,128)(2,1)S(1)}, bf16[528,128]{1,0:T(8,128)(2,1)S(1)}, bf16[528,128]{1,0:T(8,128)(2,1)S(1)}) custom-call(bf16[528,512]{1,0:T(8,128)(2,1)S(1)} %collective-permute-done.15.refs_0_, f32[512,512]{1,0:T(8,128)S(1)} %get-tuple-element.21.refs_1_), custom_call_target="tpu_custom_call" | custom-call | tf_op jit(solution)/shard_map/pallas_call | solution.py:22
  39.9 2.1 %collective-permute-start.16 = (bf16[528,128]{1,0:T(8,128)(2,1)S(1)}, bf16[528,128]{1,0:T(8,128)(2,1)S(1)}, u32[]{:S(2)}, u32[]{:S(2)}) collective-permute-start(bf16[528,128]{1,0:T(8,128)(2,1)S(1)} %get-tuple-element.23), channel_id=1, source_target_pairs={{0,8},{4,12},{8,0},{12,4},{16,24},{20,28},{24,16},{28,20},{1,9},{5... | collective-permute-start | bytes 405512 | tf_op jit(solution)/shard_map/ppermute | solution.py:335
  41.9 1.1 %collective-permute-start.17 = (bf16[528,128]{1,0:T(8,128)(2,1)S(1)}, bf16[528,128]{1,0:T(8,128)(2,1)S(1)}, u32[]{:S(2)}, u32[]{:S(2)}) collective-permute-start(bf16[528,128]{1,0:T(8,128)(2,1)S(1)} %get-tuple-element.24), channel_id=1, source_target_pairs={{0,16},{4,20},{8,24},{12,28},{16,0},{20,4},{24,8},{28,12},{1,17},{... | collective-permute-start | bytes 405512 | tf_op jit(solution)/shard_map/ppermute | solution.py:335
  43.0 0.0 collective-permute-done.12.refs_1_
  43.0 1.4 %collective-permute-start.18 = (bf16[528,128]{1,0:T(8,128)(2,1)S(1)}, bf16[528,128]{1,0:T(8,128)(2,1)S(1)}, u32[]{:S(2)}, u32[]{:S(2)}) collective-permute-start(bf16[528,128]{1,0:T(8,128)(2,1)S(1)} %get-tuple-element.25), channel_id=1, source_target_pairs={{0,24},{4,28},{8,16},{12,20},{16,8},{20,12},{24,0},{28,4},{1,25},{... | collective-permute-start | bytes 405512 | tf_op jit(solution)/shard_map/ppermute | solution.py:335
  44.4 0.9 %shard_map.59 = bf16[128,2,256]{2,1,0:T(2,128)(2,1)} custom-call(f32[128,512]{1,0:T(8,128)S(1)} %get-tuple-element.18.refs_0_, f32[128,256]{1,0:T(8,128)S(1)} %collective-permute-done.12.refs_1_), custom_call_target="tpu_custom_call" | custom-call | tf_op jit(solution)/shard_map/pallas_call | solution.py:22
  45.3 0.0 collective-permute-done.20.refs_1_
  45.3 0.0 collective-permute-done.21.refs_3_
  45.4 1.2 %shard_map.65 = (f32[288,1024]{1,0:T(8,128)}, f32[8,128]{1,0:T(8,128)S(1)}) custom-call(f32[288,512]{1,0:T(8,128)S(1)} %get-tuple-element.27.refs_0_, bf16[304,512]{1,0:T(8,128)(2,1)S(1)} %collective-permute-done.20.refs_1_, f32[288,512]{1,0:T(8,128)S(1)} %get-tuple-element.29.refs_2_, bf16[304,512]{1,0:T(8,128)(2,1)S(1)} %collective-permute-done.21.refs_3_), custom_call_target="tpu_custom_call" | custom-call | tf_op jit(solution)/shard_map/pallas_call | solution.py:22
  46.6 0.0 collective-permute-done.16.refs_1_
  46.6 6.7 %collective-permute-done.17.refs_2_ = bf16[528,128]{1,0:T(8,128)(2,1)S(1)} collective-permute-done((bf16[528,128]{1,0:T(8,128)(2,1)S(1)}, bf16[528,128]{1,0:T(8,128)(2,1)S(1)}, u32[]{:S(2)}, u32[]{:S(2)}) %collective-permute-start.17) | collective-permute-done | bytes 135200 | tf_op jit(solution)/shard_map/ppermute | solution.py:335
  53.3 0.0 collective-permute-done.18.refs_3_
  53.3 1.0 %shard_map.66 = bf16[128,2,256]{2,1,0:T(2,128)(2,1)} custom-call(f32[512,128]{1,0:T(8,128)S(1)} %get-tuple-element.22.refs_0_, bf16[528,128]{1,0:T(8,128)(2,1)S(1)} %collective-permute-done.16.refs_1_, bf16[528,128]{1,0:T(8,128)(2,1)S(1)} %collective-permute-done.17.refs_2_, bf16[528,128]{1,0:T(8,128)(2,1)S(1)} %collective-permute-done.18.refs_3_, ...), custom_call_target="tpu_custom_call" | custom-call | tf_op jit(solution)/shard_map/pallas_call | solution.py:22
  (2 shorter events, 0.0 us)
Async XLA Ops:
  1.6 11.5 %collective-permute-start.2 = (bf16[128,512]{1,0:T(8,128)(2,1)S(1)}, bf16[128,512]{1,0:T(8,128)(2,1)S(1)}, u32[]{:S(2)}, u32[]{:S(2)}) collective-permute-start(bf16[128,512]{1,0:T(8,128)(2,1)S(1)} %bitcast.9), channel_id=1, source_target_pairs={{0,24},{4,28},{8,16},{12,20},{16,8},{20,12},{24,0},{28,4},{1,25},{... | collective-permute-start | bytes 393224 | tf_op jit(solution)/shard_map/ppermute | solution.py:335
  6.7 11.2 %collective-permute-start.1 = (bf16[128,512]{1,0:T(8,128)(2,1)S(1)}, bf16[128,512]{1,0:T(8,128)(2,1)S(1)}, u32[]{:S(2)}, u32[]{:S(2)}) collective-permute-start(bf16[128,512]{1,0:T(8,128)(2,1)S(1)} %bitcast.10), channel_id=1, source_target_pairs={{0,16},{4,20},{8,24},{12,28},{16,0},{20,4},{24,8},{28,12},{1,17},{... | collective-permute-start | bytes 393224 | tf_op jit(solution)/shard_map/ppermute | solution.py:335
  7.6 5.3 %collective-permute-start.14 = (bf16[128,256]{1,0:T(8,128)(2,1)S(1)}, bf16[128,256]{1,0:T(8,128)(2,1)S(1)}, u32[]{:S(2)}, u32[]{:S(2)}) collective-permute-start(bf16[128,256]{1,0:T(8,128)(2,1)S(1)} %slice_select_fusion), channel_id=1, source_target_pairs={{1,2},{2,1},{5,6},{6,5},{9,10},{10,9},{13,14},{14,13},{17,18},{18,... | collective-permute-start | bytes 196616 | tf_op jit(solution)/shard_map/ppermute | solution.py:470
  8.3 11.0 %collective-permute-start.13 = (bf16[128,512]{1,0:T(8,128)(2,1)S(1)}, bf16[128,512]{1,0:T(8,128)(2,1)S(1)}, u32[]{:S(2)}, u32[]{:S(2)}) collective-permute-start(bf16[128,512]{1,0:T(8,128)(2,1)S(1)} %bitcast.18), channel_id=1, source_target_pairs={{0,1},{1,0},{2,3},{3,2},{4,5},{5,4},{6,7},{7,6},{8,9},{9,8},{10,11... | collective-permute-start | bytes 393224 | tf_op jit(solution)/shard_map/ppermute | solution.py:335
  11.2 9.4 %collective-permute-start.4 = (bf16[128,512]{1,0:T(8,128)(2,1)S(1)}, bf16[128,512]{1,0:T(8,128)(2,1)S(1)}, u32[]{:S(2)}, u32[]{:S(2)}) collective-permute-start(bf16[128,512]{1,0:T(8,128)(2,1)S(1)} %bitcast.11), channel_id=1, source_target_pairs={{0,12},{4,8},{8,4},{12,0},{16,28},{20,24},{24,20},{28,16},{1,13},{... | collective-permute-start | bytes 393224 | tf_op jit(solution)/shard_map/ppermute | solution.py:335
  12.9 11.3 %collective-permute-start.6 = (bf16[128,512]{1,0:T(8,128)(2,1)S(1)}, bf16[128,512]{1,0:T(8,128)(2,1)S(1)}, u32[]{:S(2)}, u32[]{:S(2)}) collective-permute-start(bf16[128,512]{1,0:T(8,128)(2,1)S(1)} %bitcast.12), channel_id=1, source_target_pairs={{0,1},{1,0},{2,3},{3,2},{4,5},{5,4},{6,7},{7,6},{8,9},{9,8},{10,11... | collective-permute-start | bytes 393224 | tf_op jit(solution)/shard_map/ppermute | solution.py:335
  13.1 11.7 %collective-permute-start.3 = (bf16[128,512]{1,0:T(8,128)(2,1)S(1)}, bf16[128,512]{1,0:T(8,128)(2,1)S(1)}, u32[]{:S(2)}, u32[]{:S(2)}) collective-permute-start(bf16[128,512]{1,0:T(8,128)(2,1)S(1)} %bitcast.13), channel_id=1, source_target_pairs={{0,4},{4,0},{8,12},{12,8},{16,20},{20,16},{24,28},{28,24},{1,5},{5... | collective-permute-start | bytes 393224 | tf_op jit(solution)/shard_map/ppermute | solution.py:335
  17.8 1.3 %collective-permute-start.19 = (bf16[128,256]{1,0:T(8,128)(2,1)S(1)}, bf16[128,256]{1,0:T(8,128)(2,1)S(1)}, u32[]{:S(2)}, u32[]{:S(2)}) collective-permute-start(bf16[128,256]{1,0:T(8,128)(2,1)S(1)} %collective-permute-done.14.refs_2_), channel_id=1, source_target_pairs={{0,1},{1,0},{2,3},{3,2},{4,5},{5,4},{6,7},{7,6},{8,9},{9,8},{10,11... | collective-permute-start | bytes 196616 | tf_op jit(solution)/shard_map/ppermute | solution.py:335
  19.1 6.7 %collective-permute-start = (bf16[128,512]{1,0:T(8,128)(2,1)S(1)}, bf16[128,512]{1,0:T(8,128)(2,1)S(1)}, u32[]{:S(2)}, u32[]{:S(2)}) collective-permute-start(bf16[128,512]{1,0:T(8,128)(2,1)S(1)} %bitcast.14), channel_id=1, source_target_pairs={{0,8},{4,12},{8,0},{12,4},{16,24},{20,28},{24,16},{28,20},{1,9},{5... | collective-permute-start | bytes 393224 | tf_op jit(solution)/shard_map/ppermute | solution.py:335
  19.2 8.2 %collective-permute-start.5 = (bf16[256,512]{1,0:T(8,128)(2,1)S(1)}, bf16[256,512]{1,0:T(8,128)(2,1)S(1)}, u32[]{:S(2)}, u32[]{:S(2)}) collective-permute-start(bf16[256,512]{1,0:T(8,128)(2,1)S(1)} %pad_maximum_fusion.refs_3_.refs_1_), channel_id=1, source_target_pairs={{0,4},{4,0},{8,12},{12,8},{16,20},{20,16},{24,28},{28,24},{1,5},{5... | collective-permute-start | bytes 786440 | tf_op jit(solution)/shard_map/ppermute | solution.py:335
  20.6 5.2 %collective-permute-start.10 = (bf16[128,512]{1,0:T(8,128)(2,1)S(1)}, bf16[128,512]{1,0:T(8,128)(2,1)S(1)}, u32[]{:S(2)}, u32[]{:S(2)}) collective-permute-start(bf16[128,512]{1,0:T(8,128)(2,1)S(1)} %collective-permute-done.4.refs_5_.refs_4_), channel_id=1, source_target_pairs={{0,1},{1,0},{2,3},{3,2},{4,5},{5,4},{6,7},{7,6},{8,9},{9,8},{10,11... | collective-permute-start | bytes 393224 | tf_op jit(solution)/shard_map/ppermute | solution.py:335
  20.6 1.7 %copy-start = (bf16[3,3,128,1024]{3,2,1,0:T(8,128)(2,1)S(1)}, bf16[3,3,128,1024]{3,2,1,0:T(8,128)(2,1)}, u32[]{:S(2)}) copy-start(bf16[3,3,128,1024]{3,2,1,0:T(8,128)(2,1)} %param.4) | copy-start | bytes 7077892
  24.2 6.2 %collective-permute-start.8 = (bf16[256,512]{1,0:T(8,128)(2,1)S(1)}, bf16[256,512]{1,0:T(8,128)(2,1)S(1)}, u32[]{:S(2)}, u32[]{:S(2)}) collective-permute-start(bf16[256,512]{1,0:T(8,128)(2,1)S(1)} %pad_maximum_fusion.refs_3_.refs_1_), channel_id=1, source_target_pairs={{0,1},{1,0},{2,3},{3,2},{4,5},{5,4},{6,7},{7,6},{8,9},{9,8},{10,11... | collective-permute-start | bytes 786440 | tf_op jit(solution)/shard_map/ppermute | solution.py:335
  24.8 14.3 %collective-permute-start.15 = (bf16[528,512]{1,0:T(8,128)(2,1)S(1)}, bf16[528,512]{1,0:T(8,128)(2,1)S(1)}, u32[]{:S(2)}, u32[]{:S(2)}) collective-permute-start(bf16[528,512]{1,0:T(8,128)(2,1)S(1)} %get-tuple-element.20), channel_id=1, source_target_pairs={{0,4},{4,0},{8,12},{12,8},{16,20},{20,16},{24,28},{28,24},{1,5},{5... | collective-permute-start | bytes 1622024 | tf_op jit(solution)/shard_map/ppermute | solution.py:335
  25.8 2.1 %collective-permute-start.9 = (bf16[128,512]{1,0:T(8,128)(2,1)S(1)}, bf16[128,512]{1,0:T(8,128)(2,1)S(1)}, u32[]{:S(2)}, u32[]{:S(2)}) collective-permute-start(bf16[128,512]{1,0:T(8,128)(2,1)S(1)} %collective-permute-done.3.refs_4_.refs_3_), channel_id=1, source_target_pairs={{0,1},{1,0},{2,3},{3,2},{4,5},{5,4},{6,7},{7,6},{8,9},{9,8},{10,11... | collective-permute-start | bytes 393224 | tf_op jit(solution)/shard_map/ppermute | solution.py:335
  25.8 2.1 %collective-permute-start.7 = (bf16[128,512]{1,0:T(8,128)(2,1)S(1)}, bf16[128,512]{1,0:T(8,128)(2,1)S(1)}, u32[]{:S(2)}, u32[]{:S(2)}) collective-permute-start(bf16[128,512]{1,0:T(8,128)(2,1)S(1)} %collective-permute-done.refs_2_), channel_id=1, source_target_pairs={{0,1},{1,0},{2,3},{3,2},{4,5},{5,4},{6,7},{7,6},{8,9},{9,8},{10,11... | collective-permute-start | bytes 393224 | tf_op jit(solution)/shard_map/ppermute | solution.py:335
  27.5 3.0 %collective-permute-start.11 = (bf16[256,512]{1,0:T(8,128)(2,1)S(1)}, bf16[256,512]{1,0:T(8,128)(2,1)S(1)}, u32[]{:S(2)}, u32[]{:S(2)}) collective-permute-start(bf16[256,512]{1,0:T(8,128)(2,1)S(1)} %collective-permute-done.5.refs_6_.refs_2_), channel_id=1, source_target_pairs={{0,1},{1,0},{2,3},{3,2},{4,5},{5,4},{6,7},{7,6},{8,9},{9,8},{10,11... | collective-permute-start | bytes 786440 | tf_op jit(solution)/shard_map/ppermute | solution.py:335
  27.9 4.1 %copy-start.1 = (bf16[3,3,128,1024]{3,2,1,0:T(8,128)(2,1)S(1)}, bf16[3,3,128,1024]{3,2,1,0:T(8,128)(2,1)}, u32[]{:S(2)}) copy-start(bf16[3,3,128,1024]{3,2,1,0:T(8,128)(2,1)} %param.4) | copy-start | bytes 7077892
  28.9 16.5 %collective-permute-start.20 = (bf16[304,512]{1,0:T(8,128)(2,1)S(1)}, bf16[304,512]{1,0:T(8,128)(2,1)S(1)}, u32[]{:S(2)}, u32[]{:S(2)}) collective-permute-start(bf16[304,512]{1,0:T(8,128)(2,1)S(1)} %get-tuple-element.28), channel_id=1, source_target_pairs={{0,2},{1,3},{2,0},{3,1},{4,6},{5,7},{6,4},{7,5},{8,10},{9,11},{10,... | collective-permute-start | bytes 933896 | tf_op jit(solution)/shard_map/ppermute | solution.py:335
  31.4 14.0 %collective-permute-start.21 = (bf16[304,512]{1,0:T(8,128)(2,1)S(1)}, bf16[304,512]{1,0:T(8,128)(2,1)S(1)}, u32[]{:S(2)}, u32[]{:S(2)}) collective-permute-start(bf16[304,512]{1,0:T(8,128)(2,1)S(1)} %get-tuple-element.30), channel_id=1, source_target_pairs={{0,2},{1,3},{2,0},{3,1},{4,6},{5,7},{6,4},{7,5},{8,10},{9,11},{10,... | collective-permute-start | bytes 933896 | tf_op jit(solution)/shard_map/ppermute | solution.py:335
  33.9 9.1 %collective-permute-start.12 = (f32[128,256]{1,0:T(8,128)S(1)}, f32[128,256]{1,0:T(8,128)S(1)}, u32[]{:S(2)}, u32[]{:S(2)}) collective-permute-start(f32[128,256]{1,0:T(8,128)S(1)} %get-tuple-element.19), channel_id=1, source_target_pairs={{1,2},{2,1},{5,6},{6,5},{9,10},{10,9},{13,14},{14,13},{17,18},{18,... | collective-permute-start | bytes 393224 | tf_op jit(solution)/shard_map/ppermute | solution.py:505
  39.9 6.7 %collective-permute-start.16 = (bf16[528,128]{1,0:T(8,128)(2,1)S(1)}, bf16[528,128]{1,0:T(8,128)(2,1)S(1)}, u32[]{:S(2)}, u32[]{:S(2)}) collective-permute-start(bf16[528,128]{1,0:T(8,128)(2,1)S(1)} %get-tuple-element.23), channel_id=1, source_target_pairs={{0,8},{4,12},{8,0},{12,4},{16,24},{20,28},{24,16},{28,20},{1,9},{5... | collective-permute-start | bytes 405512 | tf_op jit(solution)/shard_map/ppermute | solution.py:335
  41.9 11.3 %collective-permute-start.17 = (bf16[528,128]{1,0:T(8,128)(2,1)S(1)}, bf16[528,128]{1,0:T(8,128)(2,1)S(1)}, u32[]{:S(2)}, u32[]{:S(2)}) collective-permute-start(bf16[528,128]{1,0:T(8,128)(2,1)S(1)} %get-tuple-element.24), channel_id=1, source_target_pairs={{0,16},{4,20},{8,24},{12,28},{16,0},{20,4},{24,8},{28,12},{1,17},{... | collective-permute-start | bytes 405512 | tf_op jit(solution)/shard_map/ppermute | solution.py:335
  43.0 10.2 %collective-permute-start.18 = (bf16[528,128]{1,0:T(8,128)(2,1)S(1)}, bf16[528,128]{1,0:T(8,128)(2,1)S(1)}, u32[]{:S(2)}, u32[]{:S(2)}) collective-permute-start(bf16[528,128]{1,0:T(8,128)(2,1)S(1)} %get-tuple-element.25), channel_id=1, source_target_pairs={{0,24},{4,28},{8,16},{12,20},{16,8},{20,12},{24,0},{28,4},{1,25},{... | collective-permute-start | bytes 405512 | tf_op jit(solution)/shard_map/ppermute | solution.py:335
